TPU v7x, 256 devices: a whole 4x4x8 slice. The times are simulated.
256 devices in a mesh: lat: 64 (over x, z, y_hi), lon: 4 (over y_lo, core).
Axes of the slice: x: 4, y: 4 (y_hi: 2, y_lo: 2; y = y_hi * 2 + y_lo), z: 8, core: 2. Of those that a mesh axis runs over, the one named last changes fastest.
Arguments:
- state: bfloat16 [76, 768, 1080], P(None, 'lat', 'lon'), may hold values from -6 to 6
- sea_mask: int32 [19, 768, 1080], P(None, 'lat', 'lon'), may hold values 0 or 1
- seam: int32 [1080], replicated, may hold values from 0 to 1079, as said below
- w_in: bfloat16 [3, 3, 200, 76], replicated, may hold values from -0.21875 to 0.21875
- w_down: bfloat16 [2, 2, 200, 200], replicated, may hold values from -0.21875 to 0.21875
- w_mid: bfloat16 [3, 3, 200, 200], replicated, may hold values from -0.125 to 0.125
- w_up: bfloat16 [2, 2, 200, 200], replicated, may hold values from -0.4375 to 0.4375
- w_out: bfloat16 [3, 3, 76, 200], replicated, may hold values from -0.125 to 0.125
Outputs:
- next_state: bfloat16 [76, 768, 1080], P(None, 'lat', 'lon')
Inputs may be any that keep to these rules, and one draw needn't show every extreme that they name: The fold is a mirror: seam[j] = (c - j) mod 1080 for one odd c, the same for all j, drawn from the seed; so longitudes 2 k and 2 k + 1 name 2 m + 1 and 2 m for one m, and seam[seam[j]] = j.
All inputs are finite; a program needn't handle non-finite values. No bound on the sum of `sea_mask` on one device may be relied on, other than what follows from the above.
Results may differ from a plain program's by a relative error of at most 0.004.
Values may be sent and summed in bfloat16 or wider, within the bound.
No kernel may reach another device: no remote copies, remote signals or barrier semaphores. Data moves between devices by JAX's collectives and lax.ppermute only.
A program may use at most 64 MiB of HBM per device.

v0:
```python
import jax
import jax.numpy as jnp
from jax import lax
from jax.sharding import PartitionSpec as P

VARS = 4


def extended_2(array, sides, width, wrap):
    for axis, dim in sides:
        devices, length = (lax.axis_size(axis), array.shape[dim])
        up = [(i, (i + 1) % devices) for i in range(devices if wrap else devices - 1)]
        down = [(j, i) for i, j in up]
        last = lax.slice_in_dim(array, length - width, length, axis=dim)
        initial = lax.slice_in_dim(array, 0, width, axis=dim)
        before = lax.ppermute(last, axis, up)
        after = lax.ppermute(initial, axis, down)
        array = jnp.concatenate([before, array, after], axis=dim)
    return array


def conv_taps(extended, weight, rows, cols):
    total = None
    for row_tap in range(3):
        stacked = jnp.stack(
            [
                extended[:, row_tap : row_tap + rows, col_tap : col_tap + cols]
                for col_tap in range(3)
            ],
            0,
        )
        partial_sum = jnp.einsum(
            "boc,bcrl->orl", weight[row_tap], stacked, preferred_element_type=jnp.float32
        )
        total = partial_sum if total is None else total + partial_sum
    return total


def pick_fold(top_row, seam_map, width):
    circle = top_row.shape[1]
    start = lax.axis_index("lon") * width
    columns = jnp.mod(start - 1 + jnp.arange(width + 2, dtype=jnp.int32), circle)
    return jnp.take(top_row, jnp.take(seam_map, columns), axis=1)


def fold_line(field, seam_map):
    top_row = lax.all_gather(field[:, -1:, :], "lon", axis=2, tiled=True)
    return pick_fold(top_row[:, 0, :], seam_map, field.shape[2])


def place_fold(extended, fold_ext):
    northmost = lax.axis_index("lat") == lax.axis_size("lat") - 1
    row = jnp.where(northmost, fold_ext, extended[:, -1, :])
    return extended.at[:, -1, :].set(row)


def extend_full(field, seam):
    banded = extended_2(field, (("lat", 1),), 1, False)
    widened = extended_2(banded, (("lon", 2),), 1, True)
    return place_fold(widened, fold_line(field, seam))


def body(state, sea_mask, seam, w_in, w_down, w_mid, w_up, w_out):
    rows = state.shape[1]
    cols = state.shape[2]
    half_rows = rows // 2
    half_cols = cols // 2
    hidden = w_in.shape[2]
    cover = jnp.tile(sea_mask, (VARS, 1, 1)).astype(jnp.float32)
    masked = (state.astype(jnp.float32) * cover).astype(jnp.bfloat16)
    first = jax.nn.gelu(
        conv_taps(extend_full(masked, seam), w_in, rows, cols), approximate=True
    ).astype(jnp.bfloat16)
    blocks = first.reshape(hidden, half_rows, 2, half_cols, 2)
    coarse = jax.nn.gelu(
        jnp.einsum("abxc,ciajb->xij", w_down, blocks, preferred_element_type=jnp.float32),
        approximate=True,
    ).astype(jnp.bfloat16)
    seam_half = seam[0::2] // 2
    coarse_banded = extended_2(coarse, (("lat", 1),), 1, False)
    coarse_ext = extended_2(coarse_banded, (("lon", 2),), 1, True)
    coarse_top = lax.all_gather(coarse[:, -1:, :], "lon", axis=2, tiled=True)
    coarse_ext = place_fold(coarse_ext, pick_fold(coarse_top[:, 0, :], seam_half, half_cols))
    middle = jax.nn.gelu(
        conv_taps(coarse_ext, w_mid, half_rows, half_cols), approximate=True
    ).astype(jnp.bfloat16)
    grown = jnp.einsum("abxc,cij->xiajb", w_up, middle, preferred_element_type=jnp.float32).reshape(
        hidden, rows, cols
    )
    joined = (jax.nn.gelu(grown, approximate=True) + first.astype(jnp.float32)).astype(jnp.bfloat16)
    delta = conv_taps(extend_full(joined, seam), w_out, rows, cols)
    return ((state.astype(jnp.float32) + delta) * cover).astype(jnp.bfloat16)


def solution(mesh):
    return jax.shard_map(
        body,
        mesh=mesh,
        in_specs=(P(None, "lat", "lon"), P(None, "lat", "lon"), P(), P(), P(), P(), P(), P()),
        out_specs=P(None, "lat", "lon"),
        check_vma=False,
    )
```

profile of v0, /device:TPU:7, one launch (start us, length us, event | category | flops | bytes accessed | tf_op | source)
XLA Modules:
  0.0 138.8 jit_solution(4367170752984199149)
XLA Ops:
  0.0 1.1 convert_element_type.33
  1.2 1.3 convert_element_type.34
  2.6 1.6 %fusion.55 = bf16[76,12,270]{2,0,1:T(8,128)(2,1)S(1)} fusion(f32[76,12,270]{2,0,1:T(8,128)} %convert_element_type.34, bf16[76,12,270]{2,0,1:T(8,128)(2,1)S(1)} %copy-done.5), kind=kLoop, calls=%fused_computation.77 | loop fusion | flops 738720 | bytes 1969920 | tf_op jit(solution)/shard_map/convert_element_type | solution.py:70
  4.2 10.4 %collective-permute-start.1 = (bf16[76,1,270]{2,0,1:T(8,128)(2,1)S(1)}, bf16[76,1,270]{2,0,1:T(8,128)(2,1)S(1)}, u32[]{:S(2)}, u32[]{:S(2)}) collective-permute-start(bf16[76,1,270]{2,0,1:T(8,128)(2,1)S(1)} %get-tuple-element.69), channel_id=1, source_target_pairs={{4,0},{8,4},{12,8},{16,12},{20,16},{24,20},{28,24},{32,28},{36,32}... | collective-permute-start | bytes 123128 | tf_op jit(solution)/shard_map/ppermute | solution.py:17
  14.6 1.9 %collective-permute-start = (bf16[76,1,270]{2,0,1:T(8,128)(2,1)S(1)}, bf16[76,1,270]{2,0,1:T(8,128)(2,1)S(1)}, u32[]{:S(2)}, u32[]{:S(2)}) collective-permute-start(bf16[76,1,270]{2,0,1:T(8,128)(2,1)S(1)} %get-tuple-element.68), channel_id=1, source_target_pairs={{0,4},{4,8},{8,12},{12,16},{16,20},{20,24},{24,28},{28,32},{32,36}... | collective-permute-start | bytes 123128 | tf_op jit(solution)/shard_map/ppermute | solution.py:16
  16.6 0.2 slice.240
  16.8 2.2 %gather_fusion.4 = s32[272]{0:T(512)S(1)} fusion(s32[1080]{0:T(1024)S(1)} %copy-done.2, s32[1024]{0:T(1024)S(1)} %pad_clamp_fusion.3), kind=kCustom, calls=%fused_computation.clone | custom fusion | bytes 3264 | tf_op jit(solution)/shard_map/jit(_take)/gather | solution.py:43
  19.1 1.2 gather_fusion.1
  20.5 3.5 %collective-permute-done = bf16[76,1,270]{2,0,1:T(8,128)(2,1)S(1)} collective-permute-done((bf16[76,1,270]{2,0,1:T(8,128)(2,1)S(1)}, bf16[76,1,270]{2,0,1:T(8,128)(2,1)S(1)}, u32[]{:S(2)}, u32[]{:S(2)}) %collective-permute-start) | collective-permute-done | bytes 41072 | tf_op jit(solution)/shard_map/ppermute | solution.py:16
  24.0 0.9 pad_maximum_fusion.5
  25.0 2.4 %collective-permute-start.2 = (bf16[76,14,1]{2,0,1:T(8,128)(2,1)}, bf16[76,14,1]{2,0,1:T(8,128)(2,1)S(1)}, u32[]{:S(2)}, u32[]{:S(2)}) collective-permute-start(bf16[76,14,1]{2,0,1:T(8,128)(2,1)} %get-tuple-element.66), channel_id=1, source_target_pairs={{0,1},{1,2},{2,3},{3,0},{4,5},{5,6},{6,7},{7,4},{8,9},{9,10},{10,1... | collective-permute-start | bytes 6392 | tf_op jit(solution)/shard_map/ppermute | solution.py:16
  27.4 12.7 %all_gather.9 = bf16[76,1,1080]{0,1,2:T(2,128)(2,1)S(1)} all-gather(bf16[76,1,270]{0,1,2:T(2,128)(2,1)S(1)} %copy.45), channel_id=1, replica_groups=mesh['lat'=64,'lon'=4] {'lon'}, dimensions={2}, use_global_device_ids=true | all-gather | bytes 205200 | tf_op jit(solution)/shard_map/all_gather | solution.py:47
  40.1 1.4 gather_fusion
  41.7 0.6 pad_maximum_fusion.1
  42.3 1.5 %slice_bitcast_fusion.11 = (bf16[1,76,12,270]{3,1,2,0:T(8,128)(2,1)S(1)}, bf16[1,76,12,270]{3,1,2,0:T(8,128)(2,1)S(1)}, bf16[1,76,12,270]{3,1,2,0:T(8,128)(2,1)S...) fusion(bf16[76,14,272]{2,0,1:T(8,128)(2,1)S(1)} %fusion.140), kind=kLoop, calls=%fused_computation.126 | loop fusion | bytes 8864640 | tf_op jit(solution)/shard_map/stack | solution.py:25
  43.8 0.9 fusion.41
  44.7 0.9 fusion.35
  45.6 1.9 %fusion.25 = bf16[200,12,270]{0,2,1:T(8,128)(2,1)S(1)} fusion(f32[12,270,200,1]{2,1,0,3:T(8,128)S(1)} %fusion.41, f32[12,270,200,1]{2,1,3,0:T(8,128)S(1)} %fusion.35, bf16[1,76,12,270]{3,1,2,0:T(8,128)(2,1)S(1)} %get-tuple-element.58, bf16[1,76,12,270]{3,1,2,0:T(8,128)(2,1)S(1)} %get-tuple-element.59, bf16[1,76,12,270]{3,1,2,0:T(8,128)(2,1)S(1)} %get-tuple-element.57, ...), kind=kOutput, calls=%fused_computation.32 | convolution fusion | flops 304093440 | bytes 10315392 | tf_op jit(solution)/shard_map/boc,bcrl->orl/dot_general | solution.py:32
  47.4 2.6 %reshape.227 = bf16[200,6,2,135,2]{0,4,3,2,1:T(2,128)(2,1)} reshape(bf16[200,12,270]{0,2,1:T(8,128)(2,1)S(1)} %fusion.25) | data formatting | bytes 2592000 | tf_op jit(solution)/shard_map/reshape | solution.py:74
  50.0 2.2 %fusion.92 = bf16[200,6,135]{0,2,1:T(8,128)(2,1)S(1)} fusion(bf16[200,6,2,135,2]{0,4,3,2,1:T(2,128)(2,1)} %reshape.227, bf16[2,2,200,200]{3,2,1,0:T(8,128)(2,1)} %param.20), kind=kOutput, calls=%fused_computation.114 | convolution fusion | flops 260658000 | bytes 1940000 | tf_op jit(solution)/shard_map/abxc,ciajb->xij/dot_general | solution.py:76
  52.3 3.5 %collective-permute-start.5 = (bf16[200,1,135]{0,2,1:T(8,128)(2,1)S(1)}, bf16[200,1,135]{0,2,1:T(8,128)(2,1)S(1)}, u32[]{:S(2)}, u32[]{:S(2)}) collective-permute-start(bf16[200,1,135]{0,2,1:T(8,128)(2,1)S(1)} %get-tuple-element.82), channel_id=1, source_target_pairs={{4,0},{8,4},{12,8},{16,12},{20,16},{24,20},{28,24},{32,28},{36,32}... | collective-permute-start | bytes 162008 | tf_op jit(solution)/shard_map/ppermute | solution.py:17
  55.8 3.3 %collective-permute-start.4 = (bf16[200,1,135]{0,2,1:T(8,128)(2,1)S(1)}, bf16[200,1,135]{0,2,1:T(8,128)(2,1)S(1)}, u32[]{:S(2)}, u32[]{:S(2)}) collective-permute-start(bf16[200,1,135]{0,2,1:T(8,128)(2,1)S(1)} %get-tuple-element.81), channel_id=1, source_target_pairs={{0,4},{4,8},{8,12},{12,16},{16,20},{20,24},{24,28},{28,32},{32,36}... | collective-permute-start | bytes 162008 | tf_op jit(solution)/shard_map/ppermute | solution.py:16
  59.3 6.0 %collective-permute-done.4 = bf16[200,1,135]{0,2,1:T(8,128)(2,1)S(1)} collective-permute-done((bf16[200,1,135]{0,2,1:T(8,128)(2,1)S(1)}, bf16[200,1,135]{0,2,1:T(8,128)(2,1)S(1)}, u32[]{:S(2)}, u32[]{:S(2)}) %collective-permute-start.4) | collective-permute-done | bytes 54032 | tf_op jit(solution)/shard_map/ppermute | solution.py:16
  65.3 2.0 %collective-permute-start.6 = (bf16[200,8,1]{0,2,1:T(2,128)(2,1)S(1)}, bf16[200,8,1]{0,2,1:T(2,128)(2,1)S(1)}, u32[]{:S(2)}, u32[]{:S(2)}) collective-permute-start(bf16[200,8,1]{0,2,1:T(2,128)(2,1)S(1)} %get-tuple-element.79), channel_id=1, source_target_pairs={{0,1},{1,2},{2,3},{3,0},{4,5},{5,6},{6,7},{7,4},{8,9},{9,10},{10,1... | collective-permute-start | bytes 9608 | tf_op jit(solution)/shard_map/ppermute | solution.py:16
  67.3 8.1 %all_gather.10 = bf16[200,1,540]{0,1,2:T(2,128)(2,1)S(1)} all-gather(bf16[200,1,135]{0,1,2:T(2,128)(2,1)S(1)} %copy.52), channel_id=1, replica_groups=mesh['lat'=64,'lon'=4] {'lon'}, dimensions={2}, use_global_device_ids=true | all-gather | bytes 270000 | tf_op jit(solution)/shard_map/all_gather | solution.py:82
  75.4 0.9 gather_fusion.2
  76.3 0.2 pad_maximum_fusion.2
  76.6 0.3 slice_bitcast_fusion.26
  76.9 0.8 copy-done.8
  77.8 1.4 %convolution_bitcast_fusion.1 = f32[6,135,200]{2,1,0:T(8,128)} fusion(bf16[1,200,6,135]{1,3,2,0:T(8,128)(2,1)S(1)} %get-tuple-element.71, bf16[1,200,6,135]{1,3,2,0:T(8,128)(2,1)S(1)} %get-tuple-element.72, bf16[1,200,6,135]{1,3,2,0:T(8,128)(2,1)S(1)} %get-tuple-element.73, bf16[3,3,200,200]{3,2,1,0:T(8,128)(2,1)S(1)} %copy-done.8), kind=kOutput, calls=%fused_computation.82 | convolution fusion | flops 195372000 | bytes 2208576 | tf_op jit(solution)/shard_map/boc,bcrl->orl/dot_general | solution.py:32
  79.2 1.5 %convolution_bitcast_fusion.2 = f32[6,135,200]{2,1,0:T(8,128)} fusion(bf16[1,200,6,135]{1,3,2,0:T(8,128)(2,1)S(1)} %get-tuple-element.74, bf16[1,200,6,135]{1,3,2,0:T(8,128)(2,1)S(1)} %get-tuple-element.75, bf16[1,200,6,135]{1,3,2,0:T(8,128)(2,1)S(1)} %get-tuple-element.76, bf16[3,3,200,200]{3,2,1,0:T(8,128)(2,1)S(1)} %copy-done.8), kind=kOutput, calls=%fused_computation.83 | convolution fusion | flops 195372000 | bytes 2208576 | tf_op jit(solution)/shard_map/boc,bcrl->orl/dot_general | solution.py:32
  80.7 4.7 %convolution_bitcast_fusion = f32[200,6,2,135,2]{0,3,4,2,1:T(8,128)} fusion(f32[6,135,200]{2,1,0:T(8,128)} %convolution_bitcast_fusion.1, f32[6,135,200]{2,1,0:T(8,128)} %convolution_bitcast_fusion.2, bf16[1,200,6,135]{1,3,2,0:T(8,128)(2,1)S(1)} %get-tuple-element.77, bf16[1,200,6,135]{1,3,2,0:T(8,128)(2,1)S(1)} %get-tuple-element.78, ...), kind=kOutput, calls=%fused_computation.63 | convolution fusion | flops 456353984 | bytes 5862368 | tf_op jit(solution)/shard_map/abxc,cij->xiajb/dot_general | solution.py:87
  85.3 5.4 %copy.55 = f32[200,6,2,135,2]{0,4,3,2,1:T(2,128)} copy(f32[200,6,2,135,2]{0,3,4,2,1:T(8,128)} %convolution_bitcast_fusion) | data formatting | bytes 5184000 | tf_op jit(solution)/shard_map/abxc,cij->xiajb/transpose | solution.py:87
  90.7 5.4 %reshape.228 = f32[200,12,270]{0,2,1:T(8,128)} reshape(f32[200,6,2,135,2]{0,4,3,2,1:T(2,128)} %copy.55) | data formatting | bytes 5184000 | tf_op jit(solution)/shard_map/reshape | solution.py:87
  96.2 3.7 %fusion.34 = bf16[200,12,270]{0,2,1:T(8,128)(2,1)S(1)} fusion(f32[200,12,270]{0,2,1:T(8,128)} %reshape.228, bf16[200,12,270]{0,2,1:T(8,128)(2,1)} %copy-done.3), kind=kLoop, calls=%fused_computation.41 | loop fusion | flops 7128000 | bytes 5184000 | tf_op jit(solution)/shard_map/convert_element_type | solution.py:90
  99.9 1.9 %collective-permute-start.9 = (bf16[200,1,270]{0,2,1:T(8,128)(2,1)S(1)}, bf16[200,1,270]{0,2,1:T(8,128)(2,1)S(1)}, u32[]{:S(2)}, u32[]{:S(2)}) collective-permute-start(bf16[200,1,270]{0,2,1:T(8,128)(2,1)S(1)} %get-tuple-element.56), channel_id=1, source_target_pairs={{4,0},{8,4},{12,8},{16,12},{20,16},{24,20},{28,24},{32,28},{36,32}... | collective-permute-start | bytes 324008 | tf_op jit(solution)/shard_map/ppermute | solution.py:17
  101.8 4.9 %collective-permute-start.8 = (bf16[200,1,270]{0,2,1:T(8,128)(2,1)S(1)}, bf16[200,1,270]{0,2,1:T(8,128)(2,1)S(1)}, u32[]{:S(2)}, u32[]{:S(2)}) collective-permute-start(bf16[200,1,270]{0,2,1:T(8,128)(2,1)S(1)} %get-tuple-element.55), channel_id=1, source_target_pairs={{0,4},{4,8},{8,12},{12,16},{16,20},{20,24},{24,28},{28,32},{32,36}... | collective-permute-start | bytes 324008 | tf_op jit(solution)/shard_map/ppermute | solution.py:16
  106.7 0.2 copy.56
  106.9 1.5 %collective-permute-done.9 = bf16[200,1,270]{0,2,1:T(8,128)(2,1)S(1)} collective-permute-done((bf16[200,1,270]{0,2,1:T(8,128)(2,1)S(1)}, bf16[200,1,270]{0,2,1:T(8,128)(2,1)S(1)}, u32[]{:S(2)}, u32[]{:S(2)}) %collective-permute-start.9) | collective-permute-done | bytes 108032 | tf_op jit(solution)/shard_map/ppermute | solution.py:17
  108.4 4.7 %collective-permute-done.8 = bf16[200,1,270]{0,2,1:T(8,128)(2,1)S(1)} collective-permute-done((bf16[200,1,270]{0,2,1:T(8,128)(2,1)S(1)}, bf16[200,1,270]{0,2,1:T(8,128)(2,1)S(1)}, u32[]{:S(2)}, u32[]{:S(2)}) %collective-permute-start.8) | collective-permute-done | bytes 108032 | tf_op jit(solution)/shard_map/ppermute | solution.py:16
  113.2 2.1 %collective-permute-start.10 = (bf16[200,14,1]{0,2,1:T(2,128)(2,1)S(1)}, bf16[200,14,1]{0,2,1:T(2,128)(2,1)S(1)}, u32[]{:S(2)}, u32[]{:S(2)}) collective-permute-start(bf16[200,14,1]{0,2,1:T(2,128)(2,1)S(1)} %get-tuple-element.53), channel_id=1, source_target_pairs={{0,1},{1,2},{2,3},{3,0},{4,5},{5,6},{6,7},{7,4},{8,9},{9,10},{10,1... | collective-permute-start | bytes 16808 | tf_op jit(solution)/shard_map/ppermute | solution.py:16
  115.3 11.0 %all_gather.11 = bf16[200,1,1080]{0,1,2:T(2,128)(2,1)S(1)} all-gather(bf16[200,1,270]{0,1,2:T(2,128)(2,1)S(1)} %copy.56), channel_id=1, replica_groups=mesh['lat'=64,'lon'=4] {'lon'}, dimensions={2}, use_global_device_ids=true | all-gather | bytes 540000 | tf_op jit(solution)/shard_map/all_gather | solution.py:47
  126.5 2.0 %gather_fusion.3 = bf16[272,200]{1,0:T(8,128)(2,1)S(1)} fusion(bf16[200,1080]{0,1:T(8,128)(2,1)S(1)} %bitcast.229, s32[1024]{0:T(1024)S(1)} %pad_clamp_fusion.2), kind=kCustom, calls=%fused_computation.4 | custom fusion | bytes 218688 | tf_op jit(solution)/shard_map/jit(_take)/gather | solution.py:43
  128.5 0.7 pad_maximum_fusion
  129.4 2.6 %slice_bitcast_fusion.2 = (bf16[1,200,12,270]{1,3,2,0:T(8,128)(2,1)S(1)}, bf16[1,200,12,270]{1,3,2,0:T(8,128)(2,1)S(1)}, bf16[1,200,12,270]{1,3,2,0:T(8,128)(2,1...) fusion(bf16[200,14,272]{0,2,1:T(8,128)(2,1)S(1)} %fusion.126), kind=kLoop, calls=%fused_computation.68 | loop fusion | bytes 23328000 | tf_op jit(solution)/shard_map/stack | solution.py:25
  132.0 1.9 %fusion.6 = f32[12,270,76,1]{1,2,0,3:T(8,128)S(1)} fusion(bf16[1,200,12,270]{1,3,2,0:T(8,128)(2,1)S(1)} %get-tuple-element.47, bf16[1,200,12,270]{1,3,2,0:T(8,128)(2,1)S(1)} %get-tuple-element.48, bf16[1,200,12,270]{1,3,2,0:T(8,128)(2,1)S(1)} %get-tuple-element.49, bf16[3,3,76,200]{3,2,1,0:T(8,128)(2,1)S(1)} %copy-done.10), kind=kOutput, calls=%fused_computation.11 | convolution fusion | flops 299376000 | bytes 6121344 | tf_op jit(solution)/shard_map/boc,bcrl->orl/dot_general | solution.py:32
  133.9 1.9 %fusion = f32[12,270,76,1]{1,2,0,3:T(8,128)S(1)} fusion(bf16[1,200,12,270]{1,3,2,0:T(8,128)(2,1)S(1)} %get-tuple-element.50, bf16[1,200,12,270]{1,3,2,0:T(8,128)(2,1)S(1)} %get-tuple-element.51, bf16[1,200,12,270]{1,3,2,0:T(8,128)(2,1)S(1)} %get-tuple-element.52, bf16[3,3,76,200]{3,2,1,0:T(8,128)(2,1)S(1)} %copy-done.10), kind=kOutput, calls=%fused_computation.5 | convolution fusion | flops 299376000 | bytes 6121344 | tf_op jit(solution)/shard_map/boc,bcrl->orl/dot_general | solution.py:32
  135.9 2.9 %fusion.57 = bf16[76,12,270]{2,0,1:T(8,128)(2,1)} fusion(f32[76,12,270]{2,0,1:T(8,128)S(1)} %copy-done.4, bf16[76,12,270]{2,0,1:T(8,128)(2,1)S(1)} %copy-done.5, f32[12,270,76,1]{1,2,0,3:T(8,128)S(1)} %fusion.6, f32[12,270,76,1]{1,2,0,3:T(8,128)S(1)} %fusion, bf16[1,200,12,270]{1,3,2,0:T(8,128)(2,1)S(1)} %get-tuple-element.45, ...), kind=kOutput, calls=%fused_computation.79 | convolution fusion | flops 300853440 | bytes 10789824 | tf_op jit(solution)/shard_map/boc,bcrl->orl/dot_general | solution.py:32
  (57 shorter events, 1.4 us)
Async XLA Ops:
  0.0 80.7 %copy-start = (bf16[2,2,200,200]{3,2,1,0:T(8,128)(2,1)S(1)}, bf16[2,2,200,200]{3,2,1,0:T(8,128)(2,1)}, u32[]{:S(2)}) copy-start(bf16[2,2,200,200]{3,2,1,0:T(8,128)(2,1)} %param.22) | copy-start | bytes 960004
  1.2 1.4 copy-start.5
  2.6 14.0 %copy-start.2 = (s32[1080]{0:T(1024)S(1)}, s32[1080]{0:T(1024)}, u32[]{:S(2)}) copy-start(s32[1080]{0:T(1024)} %param.18) | copy-start | bytes 12964
  4.2 16.3 %collective-permute-start.1 = (bf16[76,1,270]{2,0,1:T(8,128)(2,1)S(1)}, bf16[76,1,270]{2,0,1:T(8,128)(2,1)S(1)}, u32[]{:S(2)}, u32[]{:S(2)}) collective-permute-start(bf16[76,1,270]{2,0,1:T(8,128)(2,1)S(1)} %get-tuple-element.69), channel_id=1, source_target_pairs={{4,0},{8,4},{12,8},{16,12},{20,16},{24,20},{28,24},{32,28},{36,32}... | collective-permute-start | bytes 123128 | tf_op jit(solution)/shard_map/ppermute | solution.py:17
  14.6 9.5 %collective-permute-start = (bf16[76,1,270]{2,0,1:T(8,128)(2,1)S(1)}, bf16[76,1,270]{2,0,1:T(8,128)(2,1)S(1)}, u32[]{:S(2)}, u32[]{:S(2)}) collective-permute-start(bf16[76,1,270]{2,0,1:T(8,128)(2,1)S(1)} %get-tuple-element.68), channel_id=1, source_target_pairs={{0,4},{4,8},{8,12},{12,16},{16,20},{20,24},{24,28},{28,32},{32,36}... | collective-permute-start | bytes 123128 | tf_op jit(solution)/shard_map/ppermute | solution.py:16
  25.0 16.7 %collective-permute-start.2 = (bf16[76,14,1]{2,0,1:T(8,128)(2,1)}, bf16[76,14,1]{2,0,1:T(8,128)(2,1)S(1)}, u32[]{:S(2)}, u32[]{:S(2)}) collective-permute-start(bf16[76,14,1]{2,0,1:T(8,128)(2,1)} %get-tuple-element.66), channel_id=1, source_target_pairs={{0,1},{1,2},{2,3},{3,0},{4,5},{5,6},{6,7},{7,4},{8,9},{9,10},{10,1... | collective-permute-start | bytes 6392 | tf_op jit(solution)/shard_map/ppermute | solution.py:16
  27.4 14.3 %collective-permute-start.3 = (bf16[76,14,1]{2,0,1:T(8,128)(2,1)}, bf16[76,14,1]{2,0,1:T(8,128)(2,1)S(1)}, u32[]{:S(2)}, u32[]{:S(2)}) collective-permute-start(bf16[76,14,1]{2,0,1:T(8,128)(2,1)} %get-tuple-element.67), channel_id=1, source_target_pairs={{1,0},{2,1},{3,2},{0,3},{5,4},{6,5},{7,6},{4,7},{9,8},{10,9},{11,1... | collective-permute-start | bytes 6392 | tf_op jit(solution)/shard_map/ppermute | solution.py:17
  42.3 1.6 %copy-start.9 = (bf16[3,3,200,76]{2,3,1,0:T(8,128)(2,1)S(1)}, bf16[3,3,200,76]{2,3,1,0:T(8,128)(2,1)}, u32[]{:S(2)}) copy-start(bf16[3,3,200,76]{2,3,1,0:T(8,128)(2,1)} %param.19) | copy-start | bytes 820804
  47.4 4.8 %copy-start.3 = (bf16[200,12,270]{0,2,1:T(8,128)(2,1)}, bf16[200,12,270]{0,2,1:T(8,128)(2,1)S(1)}, u32[]{:S(2)}) copy-start(bf16[200,12,270]{0,2,1:T(8,128)(2,1)S(1)} %fusion.25) | copy-start | bytes 3888004
  52.3 7.0 %collective-permute-start.5 = (bf16[200,1,135]{0,2,1:T(8,128)(2,1)S(1)}, bf16[200,1,135]{0,2,1:T(8,128)(2,1)S(1)}, u32[]{:S(2)}, u32[]{:S(2)}) collective-permute-start(bf16[200,1,135]{0,2,1:T(8,128)(2,1)S(1)} %get-tuple-element.82), channel_id=1, source_target_pairs={{4,0},{8,4},{12,8},{16,12},{20,16},{24,20},{28,24},{32,28},{36,32}... | collective-permute-start | bytes 162008 | tf_op jit(solution)/shard_map/ppermute | solution.py:17
  55.8 9.6 %collective-permute-start.4 = (bf16[200,1,135]{0,2,1:T(8,128)(2,1)S(1)}, bf16[200,1,135]{0,2,1:T(8,128)(2,1)S(1)}, u32[]{:S(2)}, u32[]{:S(2)}) collective-permute-start(bf16[200,1,135]{0,2,1:T(8,128)(2,1)S(1)} %get-tuple-element.81), channel_id=1, source_target_pairs={{0,4},{4,8},{8,12},{12,16},{16,20},{20,24},{24,28},{28,32},{32,36}... | collective-permute-start | bytes 162008 | tf_op jit(solution)/shard_map/ppermute | solution.py:16
  65.3 10.9 %collective-permute-start.6 = (bf16[200,8,1]{0,2,1:T(2,128)(2,1)S(1)}, bf16[200,8,1]{0,2,1:T(2,128)(2,1)S(1)}, u32[]{:S(2)}, u32[]{:S(2)}) collective-permute-start(bf16[200,8,1]{0,2,1:T(2,128)(2,1)S(1)} %get-tuple-element.79), channel_id=1, source_target_pairs={{0,1},{1,2},{2,3},{3,0},{4,5},{5,6},{6,7},{7,4},{8,9},{9,10},{10,1... | collective-permute-start | bytes 9608 | tf_op jit(solution)/shard_map/ppermute | solution.py:16
  67.3 9.0 %collective-permute-start.7 = (bf16[200,8,1]{0,2,1:T(2,128)(2,1)S(1)}, bf16[200,8,1]{0,2,1:T(2,128)(2,1)S(1)}, u32[]{:S(2)}, u32[]{:S(2)}) collective-permute-start(bf16[200,8,1]{0,2,1:T(2,128)(2,1)S(1)} %get-tuple-element.80), channel_id=1, source_target_pairs={{1,0},{2,1},{3,2},{0,3},{5,4},{6,5},{7,6},{4,7},{9,8},{10,9},{11,1... | collective-permute-start | bytes 9608 | tf_op jit(solution)/shard_map/ppermute | solution.py:17
  76.6 1.2 copy-start.8
  99.9 8.5 %collective-permute-start.9 = (bf16[200,1,270]{0,2,1:T(8,128)(2,1)S(1)}, bf16[200,1,270]{0,2,1:T(8,128)(2,1)S(1)}, u32[]{:S(2)}, u32[]{:S(2)}) collective-permute-start(bf16[200,1,270]{0,2,1:T(8,128)(2,1)S(1)} %get-tuple-element.56), channel_id=1, source_target_pairs={{4,0},{8,4},{12,8},{16,12},{20,16},{24,20},{28,24},{32,28},{36,32}... | collective-permute-start | bytes 324008 | tf_op jit(solution)/shard_map/ppermute | solution.py:17
  101.8 11.3 %collective-permute-start.8 = (bf16[200,1,270]{0,2,1:T(8,128)(2,1)S(1)}, bf16[200,1,270]{0,2,1:T(8,128)(2,1)S(1)}, u32[]{:S(2)}, u32[]{:S(2)}) collective-permute-start(bf16[200,1,270]{0,2,1:T(8,128)(2,1)S(1)} %get-tuple-element.55), channel_id=1, source_target_pairs={{0,4},{4,8},{8,12},{12,16},{16,20},{20,24},{24,28},{28,32},{32,36}... | collective-permute-start | bytes 324008 | tf_op jit(solution)/shard_map/ppermute | solution.py:16
  113.2 2.2 %copy-start.6 = (bf16[200,1,270]{0,2,1:T(8,128)(2,1)}, bf16[200,1,270]{0,2,1:T(8,128)(2,1)S(1)}, u32[]{:S(2)}) copy-start(bf16[200,1,270]{0,2,1:T(8,128)(2,1)S(1)} %collective-permute-done.8) | copy-start | bytes 324004
  113.2 15.2 %collective-permute-start.10 = (bf16[200,14,1]{0,2,1:T(2,128)(2,1)S(1)}, bf16[200,14,1]{0,2,1:T(2,128)(2,1)S(1)}, u32[]{:S(2)}, u32[]{:S(2)}) collective-permute-start(bf16[200,14,1]{0,2,1:T(2,128)(2,1)S(1)} %get-tuple-element.53), channel_id=1, source_target_pairs={{0,1},{1,2},{2,3},{3,0},{4,5},{5,6},{6,7},{7,4},{8,9},{9,10},{10,1... | collective-permute-start | bytes 16808 | tf_op jit(solution)/shard_map/ppermute | solution.py:16
  115.3 13.1 %collective-permute-start.11 = (bf16[200,14,1]{0,2,1:T(2,128)(2,1)S(1)}, bf16[200,14,1]{0,2,1:T(2,128)(2,1)S(1)}, u32[]{:S(2)}, u32[]{:S(2)}) collective-permute-start(bf16[200,14,1]{0,2,1:T(2,128)(2,1)S(1)} %get-tuple-element.54), channel_id=1, source_target_pairs={{1,0},{2,1},{3,2},{0,3},{5,4},{6,5},{7,6},{4,7},{9,8},{10,9},{11,1... | collective-permute-start | bytes 16808 | tf_op jit(solution)/shard_map/ppermute | solution.py:17
  126.4 2.1 %copy-start.7 = (bf16[200,1,270]{0,2,1:T(8,128)(2,1)S(1)}, bf16[200,1,270]{0,2,1:T(8,128)(2,1)}, u32[]{:S(2)}) copy-start(bf16[200,1,270]{0,2,1:T(8,128)(2,1)} %copy-done.6) | copy-start | bytes 324004
  129.3 2.6 %copy-start.10 = (bf16[3,3,76,200]{3,2,1,0:T(8,128)(2,1)S(1)}, bf16[3,3,76,200]{3,2,1,0:T(8,128)(2,1)}, u32[]{:S(2)}) copy-start(bf16[3,3,76,200]{3,2,1,0:T(8,128)(2,1)} %param.23) | copy-start | bytes 820804
  133.9 1.9 %copy-start.4 = (f32[76,12,270]{2,0,1:T(8,128)S(1)}, f32[76,12,270]{2,0,1:T(8,128)}, u32[]{:S(2)}) copy-start(f32[76,12,270]{2,0,1:T(8,128)} %convert_element_type.34) | copy-start | bytes 2954884
  135.9 3.0 %copy-start.1 = (bf16[2,2,200,200]{3,2,1,0:T(8,128)(2,1)S(1)}, bf16[2,2,200,200]{3,2,1,0:T(8,128)(2,1)}, u32[]{:S(2)}) copy-start(bf16[2,2,200,200]{3,2,1,0:T(8,128)(2,1)} %param.22) | copy-start | bytes 960004
where the time goes:
time: 139 us
  starting transfers between devices  32.4 us (23%)
  blocking collectives  31.8 us (23%)
  local copies, waits for them, and re-layouts  28.9 us (21%)
  matrix products  20.2 us (15%)
  waiting for transfers between devices  15.9 us (11%)
  other arithmetic  9.25 us (7%)
    all_gather x2, blocking collectives, fold_line(): top_row = lax.all_gather(field[:, -1:, :], 'lon', axis=2, tiled=True)  23.7 us
    ppermute x6, starting transfers between devices, extended_2(): before = lax.ppermute(last, axis, up)  16.6 us
    ppermute x6, starting transfers between devices, extended_2(): after = lax.ppermute(initial, axis, down)  15.8 us
    ppermute x6, waiting for transfers between devices, extended_2(): before = lax.ppermute(last, axis, up)  14.3 us
    dot_general x8, matrix products, conv_taps(): jnp.einsum('boc,bcrl->orl', weight[row_tap], stacked, preferred_element_t...  13.3 us
    all_gather x1, blocking collectives, body(): coarse_top = lax.all_gather(coarse[:, -1:, :], 'lon', axis=2, tiled=True)  8.05 us
    gather x6, local copies, waits for them, and re-layouts, pick_fold(): return jnp.take(top_row, jnp.take(seam_map, columns), axis=1)  7.77 us
    reshape x1, local copies, waits for them, and re-layouts, body(): jnp.einsum('abxc,cij->xiajb', w_up, middle, preferred_element_type=jnp.fl...  5.43 us
  transfers between devices with their start and end apart: 12, of which 5 were waited for; matrix products, arithmetic and copies ran while one was open for 6% of the time, Pallas kernels for 0%

commit v1 on v0

v1 whole, which is shorter than its diff:
```python
import jax
import jax.numpy as jnp
from jax import lax
from jax.experimental import pallas as pl
from jax.experimental.pallas import tpu as pltpu
from jax.sharding import PartitionSpec as P

VARS, LEVELS, CHANNELS, HIDDEN = 4, 19, 76, 200
ROWS, COLS = 12, 270
HALO = 5
CH = 80
LANES = 384
MAIN = 256
REST = COLS - MAIN
PIX = 144
HID = 256
TROWS = 408
F32, BF16 = jnp.float32, jnp.bfloat16


def gelu(x):
    inner = x * (0.7978845608028654 + 0.035677408136300125 * (x * x))
    half = 0.5 * x
    return half + half * jnp.tanh(inner)


def prep_kernel(state_ref, mask_ref, rows_ref, lon_ref, north_ref, south_ref, wide_ref):
    for t in range(3):
        wide_ref[t, CHANNELS:] = jnp.zeros((CH - CHANNELS, 16, 128), F32)

    def level(l, carry):
        cover = mask_ref[l].astype(F32)
        for v in range(VARS):
            masked = state_ref[v * LEVELS + l].astype(F32) * cover
            masked = jnp.concatenate([masked, jnp.zeros((ROWS, LANES - COLS), F32)], axis=1)
            for t in range(3):
                wide_ref[t, v * LEVELS + l, 0:ROWS] = masked[:, t * 128 : (t + 1) * 128]
        return carry

    lax.fori_loop(0, LEVELS, level, 0)
    flat = wide_ref.reshape(3 * CH * 16, 128)
    at = lambda r: [flat[pl.ds(t * CH * 16 + r, CH, stride=16), :] for t in range(3)]
    rows = [jnp.concatenate(at(r), axis=1) for r in range(ROWS)]
    for r in range(ROWS):
        rows_ref[r] = rows[r].astype(BF16)
    zeros = lambda n: [jnp.zeros((CH, n), F32)]
    low = jnp.concatenate([row[:, :HALO] for row in rows] + zeros(128 - ROWS * HALO), axis=1)
    high = jnp.concatenate([row[:, COLS - HALO : COLS] for row in rows] + zeros(128 - ROWS * HALO), axis=1)
    lon_ref[0] = low.astype(BF16)
    lon_ref[1] = high.astype(BF16)
    for ref, first in ((north_ref, ROWS - HALO), (south_ref, 0)):
        picked = rows[first : first + HALO]
        for k in range(HALO):
            ref[k * CH : (k + 1) * CH, :] = picked[k][:, :MAIN].astype(BF16)
        tail = jnp.concatenate([row[:, MAIN:COLS] for row in picked] + zeros(128 - HALO * REST), axis=1).astype(BF16)
        ref[HALO * CH :, :] = jnp.concatenate([tail[: CH // 2], tail[CH // 2 :]], axis=1)


def prep(state, mask):
    vmem = pl.BlockSpec(memory_space=pltpu.VMEM)
    payload = jax.ShapeDtypeStruct((HALO * CH + CH // 2, MAIN), BF16)
    return pl.pallas_call(
        prep_kernel,
        out_shape=(
            jax.ShapeDtypeStruct((ROWS, CH, LANES), BF16),
            jax.ShapeDtypeStruct((2, CH, 128), BF16),
            payload,
            payload,
        ),
        in_specs=[vmem] * 2,
        out_specs=(vmem,) * 4,
        scratch_shapes=[pltpu.VMEM((3, CH, 16, 128), F32)],
        compiler_params=pltpu.CompilerParams(vmem_limit_bytes=40 * 2**20),
    )(state, mask)


def tail_of(payload_ref):
    low = payload_ref[HALO * CH :, :]
    return jnp.concatenate([low[:, :128], low[:, 128:]], axis=0).astype(F32)


def flip(block):
    n = block.shape[1]
    return jnp.concatenate([block, jnp.zeros((128 - CH, n), F32)], axis=0).T


def main_kernel(
    seam_ref, rows_ref, west_ref, east_ref, south_ref, north_ref, fold1_ref, fold2_ref, fold3_ref, own_ref,
    w_in_ref, w_down_ref, w_mid_ref, w_up_ref, w_out_ref, state_ref, mask_ref,
    out_ref,
    t_ref, edge_ref, a_ref, f_ref, c_ref, j_ref, u_ref, y_ref, d_ref,
):
    n_lat, n_lon = lax.axis_size("lat"), lax.axis_size("lon")
    lat, lon = lax.axis_index("lat"), lax.axis_index("lon")
    bottom, top = lat == 0, lat == n_lat - 1
    keep = jnp.where(bottom, 0.0, 1.0).astype(F32)

    lane = lax.broadcasted_iota(jnp.int32, (PIX, 128), 1)

    def pack(ai):
        odd_left, even, odd, even_right = (t_ref[pl.ds(3 + s, PIX, stride=2), :] for s in range(4))
        even80, odd80 = pltpu.roll(even, CH, 1), pltpu.roll(odd, CH, 1)
        for p, (left, mid, right) in enumerate(((odd_left, even80, odd), (even, odd80, even_right))):
            low = jnp.where(lane < CH, left, mid)
            high = jnp.where(lane < 2 * CH - 128, mid, pltpu.roll(right, 2 * CH - 128, 1))
            a_ref[ai, p * PIX : (p + 1) * PIX, :] = jnp.concatenate([low, high], axis=1).astype(BF16)

    edge_ref[0] = flip(west_ref[...].astype(F32))
    edge_ref[1] = flip(east_ref[...].astype(F32))
    edge_ref[2] = flip(tail_of(south_ref))
    edge_ref[3] = flip(tail_of(north_ref))

    def own_row(r, carry):
        t_ref[8 : 8 + LANES, :] = flip(rows_ref[r].astype(F32))
        t_ref[8 - HALO : 8, :] = edge_ref[0, pl.ds(r * HALO, HALO), :]
        t_ref[8 + COLS : 8 + COLS + HALO, :] = edge_ref[1, pl.ds(r * HALO, HALO), :]
        pack(r + HALO)
        return carry

    lax.fori_loop(0, ROWS, own_row, 0)

    def halo_row(ref, side, k, ai):
        t_ref[8 : 8 + MAIN, :] = flip(ref[pl.ds(pl.multiple_of(k * CH, CH), CH), :].astype(F32))
        t_ref[8 + MAIN : 8 + COLS, :] = edge_ref[side, pl.ds(k * REST, REST), :]
        t_ref[8 - HALO : 8, :] = edge_ref[side, pl.ds(HALO * REST + k * HALO, HALO), :]
        t_ref[8 + COLS : 8 + COLS + HALO, :] = edge_ref[side, pl.ds(HALO * (REST + HALO) + k * HALO, HALO), :]
        pack(ai)

    def south_row(k, carry):
        @pl.when(bottom)
        def _():
            a_ref[k] = jnp.zeros((2 * PIX, HID), BF16)

        @pl.when(jnp.logical_not(bottom))
        def _():
            halo_row(south_ref, 2, k, k)

        return carry

    lax.fori_loop(0, HALO, south_row, 0)

    @pl.when(jnp.logical_not(top))
    def _():
        def north_row(k, carry):
            halo_row(north_ref, 3, k, ROWS + HALO + k)
            return carry

        lax.fori_loop(0, HALO, north_row, 0)

    @pl.when(top)
    def _():
        circle = n_lon * COLS
        span = 288
        column = lax.broadcasted_iota(jnp.int32, (span, 128), 0) - 8 + COLS * lon
        source = lax.rem(seam_ref[0] - column + 3 * circle, circle)
        spot = lax.broadcasted_iota(jnp.int32, (span, 128), 1)

        def fold_row(k, carry):
            kk = HALO - 1 - k
            total = jnp.zeros((span, CH), F32)
            for d, ref in enumerate((own_ref, fold1_ref, fold2_ref, fold3_ref)):
                block = lax.rem(lon + n_lon - d, n_lon)
                place = source - block * COLS
                hot = [(place == spot), (place == spot + 128)]
                inside = jnp.logical_and(place >= MAIN, place < COLS)
                hot.append(jnp.logical_and(inside, place - MAIN + kk * REST == spot))
                hot = jnp.concatenate([jnp.where(h, 1.0, 0.0).astype(BF16) for h in hot], axis=1)
                main = ref[pl.ds(pl.multiple_of(kk * CH, CH), CH), :]
                values = jnp.concatenate([main, tail_of(ref).astype(BF16)], axis=1)
                total += lax.dot_general(hot, values, (((1,), (1,)), ((), ())), preferred_element_type=F32)
            t_ref[0:span, :] = jnp.concatenate([total, jnp.zeros((span, 128 - CH), F32)], axis=1)
            pack(ROWS + HALO + k)
            return carry

        lax.fori_loop(0, HALO, fold_row, 0)

    def first_group(g, carry):
        turned = jnp.logical_and(top, g == 4)
        tap = lambda t, n: jnp.where(turned, n - 1 - t, t)
        w_in = [
            jnp.concatenate(
                [w_in_ref[tap(3 * a + b, 9)] for b in range(3)] + [jnp.zeros((HID - 3 * CH, HID), BF16)], axis=0
            )
            for a in range(3)
        ]
        w_in = jnp.concatenate(w_in, axis=0)
        for q in range(4):
            fr = 4 * g + q
            taps = jnp.concatenate([a_ref[fr + a] for a in range(3)], axis=1)
            f_ref[fr] = gelu(jnp.dot(taps, w_in, preferred_element_type=F32)).astype(BF16)
        w_down = jnp.concatenate([w_down_ref[tap(t, 4)] for t in range(4)], axis=0)
        for q in range(2):
            ci = 2 * g + q
            pieces = [f_ref[2 * ci + a, b * PIX : (b + 1) * PIX, :] for a in range(2) for b in range(2)]
            coarse = gelu(jnp.dot(jnp.concatenate(pieces, axis=1), w_down, preferred_element_type=F32))
            coarse = coarse * jnp.where(ci < 2, keep, 1.0)
            planes = [pltpu.roll(coarse, 1, 0), coarse, pltpu.roll(coarse, PIX - 1, 0)]
            c_ref[ci] = jnp.concatenate(planes, axis=1).astype(BF16)
        return carry

    lax.fori_loop(0, 5, first_group, 0)

    def mid_row(mi, carry):
        turned = jnp.logical_and(top, mi == 7)
        tap = lambda t, n: jnp.where(turned, n - 1 - t, t)
        taps = jnp.concatenate([c_ref[mi + a] for a in range(3)], axis=1)
        w_mid = jnp.concatenate([w_mid_ref[tap(t, 9)] for t in range(9)], axis=0)
        middle = gelu(jnp.dot(taps, w_mid, preferred_element_type=F32)).astype(BF16)
        held = jnp.where(mi < 1, keep, 1.0)
        for a in range(2):
            halves = []
            for b in range(2):
                grown = jnp.dot(middle, w_up_ref[tap(2 * a + b, 4)], preferred_element_type=F32)
                first = f_ref[2 * mi + a + 2, b * PIX : (b + 1) * PIX, :].astype(F32)
                halves.append((gelu(grown) + first) * held)
            even, odd = halves
            planes = (pltpu.roll(odd, 1, 0), even, odd, pltpu.roll(even, PIX - 1, 0))
            for s, plane in enumerate(planes):
                j_ref[2 * mi + a, s * PIX : (s + 1) * PIX, :] = plane.astype(BF16)
        return carry

    lax.fori_loop(0, 8, mid_row, 0)

    def out_part(i, carry):
        jr = i + 1
        taps = jnp.concatenate([j_ref[jr, b * PIX : (b + 2) * PIX, :] for b in range(3)], axis=1)
        part = jnp.dot(taps, w_out_ref[...], preferred_element_type=F32)
        for t in range(2):
            for p in range(2):
                half = part[p * PIX : (p + 1) * PIX, t * 128 : (t + 1) * 128]
                u_ref[pl.ds(t * TROWS + 4 + p, PIX, stride=2), :] = half
            y_ref[i, t * 128 : (t + 1) * 128, :] = u_ref[t * TROWS + 8 : t * TROWS + 8 + LANES, :].T
        return carry

    lax.fori_loop(0, ROWS + 2, out_part, 0)
    flat = d_ref.reshape(3 * CH * 16, 128)

    def out_row(r, carry):
        parts = [y_ref[r + a, a * CH : (a + 1) * CH, :] for a in range(3)]
        total = parts[0] + parts[1] + parts[2]
        for t in range(3):
            flat[pl.ds(t * CH * 16 + r, CH, stride=16), :] = total[:, t * 128 : (t + 1) * 128]
        return carry

    lax.fori_loop(0, ROWS, out_row, 0)

    def level(l, carry):
        cover = mask_ref[l].astype(F32)
        for v in range(VARS):
            c = v * LEVELS + l
            delta = jnp.concatenate([d_ref[t, c, 0:ROWS, :] for t in range(3)], axis=1)[:, :COLS]
            total = (state_ref[c].astype(F32) + delta) * cover
            out_ref[c] = total.astype(BF16)
        return carry

    lax.fori_loop(0, LEVELS, level, 0)


def main(*operands):
    vmem = pl.BlockSpec(memory_space=pltpu.VMEM)
    smem = pl.BlockSpec(memory_space=pltpu.SMEM)
    return pl.pallas_call(
        main_kernel,
        out_shape=jax.ShapeDtypeStruct((CHANNELS, ROWS, COLS), BF16),
        in_specs=[smem] + [vmem] * (len(operands) - 1),
        out_specs=vmem,
        scratch_shapes=[
            pltpu.VMEM((TROWS, 128), F32),
            pltpu.VMEM((4, 128, 128), F32),
            pltpu.VMEM((ROWS + 2 * HALO, 2 * PIX, HID), BF16),
            pltpu.VMEM((20, 2 * PIX, HID), BF16),
            pltpu.VMEM((10, PIX, 3 * HID), BF16),
            pltpu.VMEM((16, 4 * PIX, HID), BF16),
            pltpu.VMEM((2 * TROWS, 128), F32),
            pltpu.VMEM((ROWS + 2, HID, LANES), F32),
            pltpu.VMEM((3, CH, 16, 128), F32),
        ],
        compiler_params=pltpu.CompilerParams(vmem_limit_bytes=60 * 2**20),
    )(*operands)


def weights(w_in, w_down, w_mid, w_up, w_out):
    def laid(w, rows):
        w = jnp.swapaxes(w.reshape((-1,) + w.shape[2:]), 1, 2)
        return jnp.pad(w, ((0, 0), (0, rows - w.shape[1]), (0, HID - w.shape[2])))

    out = jnp.transpose(w_out, (1, 3, 0, 2))
    out = jnp.pad(out, ((0, 0), (0, HID - HIDDEN), (0, 0), (0, CH - CHANNELS))).reshape(3 * HID, 3 * CH)
    out = jnp.pad(out, ((0, 0), (0, HID - 3 * CH)))
    return laid(w_in, CH), laid(w_down, HID), laid(w_mid, HID), laid(w_up, HID), out


def body(state, sea_mask, seam, w_in, w_down, w_mid, w_up, w_out):
    n_lat, n_lon = lax.axis_size("lat"), lax.axis_size("lon")
    ring = lambda n, d: [(i, (i + d) % n) for i in range(n)]
    rows, edges, north_going, south_going = prep(state, sea_mask)
    west = lax.ppermute(edges[1], "lon", ring(n_lon, 1))
    east = lax.ppermute(edges[0], "lon", ring(n_lon, -1))

    def with_corners(payload, first):
        begin = HALO * REST
        pieces = []
        for side, edge in enumerate((west, east)):
            at = begin + side * HALO * HALO
            cut = edge[:, first * HALO : (first + HALO) * HALO]
            pieces.append(jnp.pad(cut, ((0, 0), (at, 128 - at - HALO * HALO))))
        added = pieces[0] + pieces[1]
        added = jnp.concatenate([added[: CH // 2], added[CH // 2 :]], axis=1)
        return payload.at[HALO * CH :].add(added)

    north_going = with_corners(north_going, ROWS - HALO)
    south_going = with_corners(south_going, 0)
    south = lax.ppermute(north_going, "lat", ring(n_lat, 1))
    north = lax.ppermute(south_going, "lat", ring(n_lat, -1))
    last = (n_lat - 1) * n_lon
    folds = [
        lax.ppermute(
            north_going,
            ("lat", "lon"),
            [(i, i) for i in range(last)] + [(last + j, last + (j + d) % n_lon) for j in range(n_lon)],
        )
        for d in (1, 2, 3)
    ]
    laid = weights(w_in, w_down, w_mid, w_up, w_out)
    return main(seam, rows, west, east, south, north, *folds, north_going, *laid, state, sea_mask)


def solution(mesh):
    return jax.shard_map(
        body,
        mesh=mesh,
        in_specs=(P(None, "lat", "lon"), P(None, "lat", "lon"), P(), P(), P(), P(), P(), P()),
        out_specs=P(None, "lat", "lon"),
        check_vma=False,
    )
```

time: 139 us -> 65.2 us (0.47)
  the two profiles are of different devices: /device:TPU:7 before, /device:TPU:1 now
where the time goes in v1:
time: 65.2 us; the launch traced here: 64.9 us
  Pallas kernels  27.5 us (42%)
  starting transfers between devices  21.5 us (33%)
  local copies, waits for them, and re-layouts  12.8 us (20%)
  waiting for transfers between devices  2.82 us (4%)
    pallas_call x1, Pallas kernels, main(): pl.pallas_call(main_kernel, out_shape=jax.ShapeDtypeStruct((CHANNELS, ROW...  26.6 us
    ppermute x1, starting transfers between devices, body(): north = lax.ppermute(south_going, 'lat', ring(n_lat, -1))  13.2 us
    unnamed x34, local copies, waits for them, and re-layouts  5.17 us
    pad x4, local copies, waits for them, and re-layouts, laid(): return jnp.pad(w, ((0, 0), (0, rows - w.shape[1]), (0, HID - w.shape[2])))  3.78 us
    ppermute x3, starting transfers between devices, body(): lax.ppermute(north_going, ('lat', 'lon'), [(i, i) for i in range(last)] +...  2.7 us
    ppermute x1, starting transfers between devices, body(): west = lax.ppermute(edges[1], 'lon', ring(n_lon, 1))  2.69 us
    ppermute x1, starting transfers between devices, body(): south = lax.ppermute(north_going, 'lat', ring(n_lat, 1))  2.38 us
    pallas_call x1, local copies, waits for them, and re-layouts, main(): pl.pallas_call(main_kernel, out_shape=jax.ShapeDtypeStruct((CHANNELS, ROW...  2.19 us
  transfers between devices with their start and end apart: 7, of which 2 were waited for; matrix products, arithmetic and copies ran while one was open for 12% of the time, Pallas kernels for 0%

profile of v1, /device:TPU:1, one launch (start us, length us, event | category | flops | bytes accessed | tf_op | source)
XLA Modules:
  0.0 64.9 jit_solution(2475767257940043594)
XLA Ops:
  0.0 1.2 %copy.19.mask_ref = s32[19,12,270]{2,1,0:T(8,128)S(1)} copy(s32[19,12,270]{2,0,1:T(8,128)} %param.13) | data formatting | bytes 492480 | tf_op args[1]
  1.2 0.1 copy-done.5
  1.3 0.2 copy.18.state_ref
  1.4 0.0 copy-start
  1.4 0.0 copy-start.6
  1.4 0.0 copy-start.8
  1.5 0.9 %shard_map.82 = (bf16[12,80,384]{2,1,0:T(8,128)(2,1)S(1)}, bf16[2,80,128]{2,1,0:T(8,128)(2,1)S(1)}, bf16[440,256]{1,0:T(8,128)(2,1)S(1)}, bf16[440,256]{1,0:T(8,128)(2,1)S(1)}) custom-call(bf16[76,12,270]{2,1,0:T(8,128)(2,1)S(1)} %copy.18.state_ref, s32[19,12,270]{2,1,0:T(8,128)S(1)} %copy.19.mask_ref), custom_call_target="tpu_custom_call" | custom-call | tf_op jit(solution)/shard_map/pallas_call | solution.py:62
  2.3 0.0 copy-done.1
  2.4 0.0 copy-start.2
  2.4 0.9 %copy-done.2 = bf16[12,80,384]{2,1,0:T(8,128)(2,1)} copy-done((bf16[12,80,384]{2,1,0:T(8,128)(2,1)}, bf16[12,80,384]{2,1,0:T(8,128)(2,1)S(1)}, u32[]{:S(2)}) %copy-start.2) | copy-done | bytes 737304
  3.2 2.7 %collective-permute-start = (bf16[80,128]{1,0:T(8,128)(2,1)S(1)}, bf16[80,128]{1,0:T(8,128)(2,1)S(1)}, u32[]{:S(2)}, u32[]{:S(2)}) collective-permute-start(bf16[80,128]{1,0:T(8,128)(2,1)S(1)} %get-tuple-element.42), channel_id=1, source_target_pairs={{0,1},{1,2},{2,3},{3,0},{4,5},{5,6},{6,7},{7,4},{8,9},{9,10},{10,1... | collective-permute-start | bytes 61448 | tf_op jit(solution)/shard_map/ppermute | solution.py:297
  5.9 0.6 collective-permute-start.1
  6.5 0.7 %collective-permute-done.west_ref = bf16[80,128]{1,0:T(8,128)(2,1)S(1)} collective-permute-done((bf16[80,128]{1,0:T(8,128)(2,1)S(1)}, bf16[80,128]{1,0:T(8,128)(2,1)S(1)}, u32[]{:S(2)}, u32[]{:S(2)}) %collective-permute-start) | collective-permute-done | bytes 20512 | tf_op jit(solution)/shard_map/ppermute | solution.py:297
  7.1 0.1 fusion.4
  7.2 2.1 %collective-permute-done.1.east_ref = bf16[80,128]{1,0:T(8,128)(2,1)S(1)} collective-permute-done((bf16[80,128]{1,0:T(8,128)(2,1)S(1)}, bf16[80,128]{1,0:T(8,128)(2,1)S(1)}, u32[]{:S(2)}, u32[]{:S(2)}) %collective-permute-start.1) | collective-permute-done | bytes 20512 | tf_op jit(solution)/shard_map/ppermute | solution.py:298
  9.4 0.1 fusion.5
  9.4 0.1 fusion.2
  9.6 0.0 copy-start.3
  9.6 0.7 %collective-permute-start.6 = (bf16[440,256]{1,0:T(8,128)(2,1)S(1)}, bf16[440,256]{1,0:T(8,128)(2,1)S(1)}, u32[]{:S(2)}, u32[]{:S(2)}) collective-permute-start(bf16[440,256]{1,0:T(8,128)(2,1)S(1)} %fusion.own_ref), channel_id=1, source_target_pairs={{0,0},{1,1},{2,2},{3,3},{4,4},{5,5},{6,6},{7,7},{8,8},{9,9},{10,10... | collective-permute-start | bytes 675848 | tf_op jit(solution)/shard_map/ppermute | solution.py:317
  10.2 0.7 %collective-permute-start.5 = (bf16[440,256]{1,0:T(8,128)(2,1)S(1)}, bf16[440,256]{1,0:T(8,128)(2,1)S(1)}, u32[]{:S(2)}, u32[]{:S(2)}) collective-permute-start(bf16[440,256]{1,0:T(8,128)(2,1)S(1)} %fusion.own_ref), channel_id=1, source_target_pairs={{0,0},{1,1},{2,2},{3,3},{4,4},{5,5},{6,6},{7,7},{8,8},{9,9},{10,10... | collective-permute-start | bytes 675848 | tf_op jit(solution)/shard_map/ppermute | solution.py:317
  10.9 1.3 %collective-permute-start.4 = (bf16[440,256]{1,0:T(8,128)(2,1)S(1)}, bf16[440,256]{1,0:T(8,128)(2,1)}, u32[]{:S(2)}, u32[]{:S(2)}) collective-permute-start(bf16[440,256]{1,0:T(8,128)(2,1)S(1)} %fusion.own_ref), channel_id=1, source_target_pairs={{0,0},{1,1},{2,2},{3,3},{4,4},{5,5},{6,6},{7,7},{8,8},{9,9},{10,10... | collective-permute-start | bytes 675848 | tf_op jit(solution)/shard_map/ppermute | solution.py:317
  12.3 2.4 %collective-permute-start.2 = (bf16[440,256]{1,0:T(8,128)(2,1)S(1)}, bf16[440,256]{1,0:T(8,128)(2,1)}, u32[]{:S(2)}, u32[]{:S(2)}) collective-permute-start(bf16[440,256]{1,0:T(8,128)(2,1)S(1)} %fusion.own_ref), channel_id=1, source_target_pairs={{0,4},{4,8},{8,12},{12,16},{16,20},{20,24},{24,28},{28,32},{32,36}... | collective-permute-start | bytes 675848 | tf_op jit(solution)/shard_map/ppermute | solution.py:313
  14.7 0.0 copy-start.7
  14.7 13.2 %collective-permute-start.3 = (bf16[440,256]{1,0:T(8,128)(2,1)S(1)}, bf16[440,256]{1,0:T(8,128)(2,1)}, u32[]{:S(2)}, u32[]{:S(2)}) collective-permute-start(bf16[440,256]{1,0:T(8,128)(2,1)S(1)} %fusion.1), channel_id=1, source_target_pairs={{0,252},{4,0},{8,4},{12,8},{16,12},{20,16},{24,20},{28,24},{32,28}... | collective-permute-start | bytes 675848 | tf_op jit(solution)/shard_map/ppermute | solution.py:314
  27.9 0.0 copy-done.6
  27.9 0.2 copy.20
  28.1 0.8 %pad.45.w_in_ref = bf16[9,80,256]{2,1,0:T(8,128)(2,1)} pad(bf16[9,76,200]{2,1,0:T(8,128)(2,1)S(1)} %bitcast.20, bf16[]{:T(256)} %constant.49.clone.1), padding=0_0x0_4x0_56 | pad | bytes 642242 | tf_op jit(solution)/shard_map/jit(_pad)/pad | solution.py:285
  28.9 0.9 %pad.46.w_down_ref = bf16[4,256,256]{2,1,0:T(8,128)(2,1)} pad(bf16[4,200,200]{2,1,0:T(8,128)(2,1)S(1)} %bitcast.18, bf16[]{:T(256)} %constant.49.clone.1), padding=0_0x0_56x0_56 | pad | bytes 844290 | tf_op jit(solution)/shard_map/jit(_pad)/pad | solution.py:285
  29.8 0.0 copy-done.3
  29.8 0.2 copy.22
  30.0 0.9 %pad.48.w_up_ref = bf16[4,256,256]{2,1,0:T(8,128)(2,1)} pad(bf16[4,200,200]{2,1,0:T(8,128)(2,1)S(1)} %bitcast.19, bf16[]{:T(256)} %constant.49.clone.1), padding=0_0x0_56x0_56 | pad | bytes 844290 | tf_op jit(solution)/shard_map/jit(_pad)/pad | solution.py:285
  30.9 0.9 %copy.30 = bf16[3,200,3,76]{3,2,1,0:T(4,128)(2,1)S(1)} copy(bf16[3,200,3,76]{1,3,0,2:T(8,128)(2,1)S(1)} %bitcast.21) | data formatting | bytes 547200
  31.8 0.4 pad.49.clone
  32.2 0.0 copy-start.4
  32.2 0.3 reshape.69
  32.6 0.8 %pad.50.w_out_ref = bf16[768,256]{1,0:T(8,128)(2,1)} pad(bf16[768,240]{1,0:T(8,128)(2,1)S(1)} %reshape.69, bf16[]{:T(256)} %constant.49.clone.1), padding=0_0x0_16 | pad | bytes 761858 | tf_op jit(solution)/shard_map/jit(_pad)/pad | solution.py:289
  33.4 0.0 copy-done.4
  33.4 0.8 %copy.21 = bf16[3,3,200,200]{2,3,1,0:T(8,128)(2,1)S(1)} copy(bf16[3,3,200,200]{3,2,1,0:T(8,128)(2,1)S(1)} %copy-done.4) | data formatting | bytes 1440000 | tf_op args[5]
  34.2 1.2 %pad.47.w_mid_ref = bf16[9,256,256]{2,1,0:T(8,128)(2,1)} pad(bf16[9,200,200]{2,1,0:T(8,128)(2,1)S(1)} %bitcast.17, bf16[]{:T(256)} %constant.49.clone.1), padding=0_0x0_56x0_56 | pad | bytes 1899650 | tf_op jit(solution)/shard_map/jit(_pad)/pad | solution.py:285
  35.4 0.0 collective-permute-done.6.fold3_ref
  35.4 0.0 collective-permute-done.5.fold2_ref
  35.4 0.0 collective-permute-done.4.fold1_ref
  35.4 0.0 collective-permute-done.2.south_ref
  35.4 0.0 collective-permute-done.3.north_ref
  35.4 0.6 copy-done.10
  36.1 0.1 copy-done.11
  36.2 26.6 %shard_map.83 = bf16[76,12,270]{2,1,0:T(8,128)(2,1)} custom-call(s32[1080]{0:T(1024)} %seam_ref.1, bf16[12,80,384]{2,1,0:T(8,128)(2,1)} %copy-done.2, bf16[80,128]{1,0:T(8,128)(2,1)} %copy-done.12, bf16[80,128]{1,0:T(8,128)(2,1)} %copy-done.13, bf16[440,256]{1,0:T(8,128)(2,1)} %collective-permute-done.2.south_ref, ...), custom_call_target="tpu_custom_call" | custom-call | tf_op jit(solution)/shard_map/pallas_call | solution.py:262
  62.7 2.2 %copy.27 = bf16[76,12,270]{2,0,1:T(8,128)(2,1)} copy(bf16[76,12,270]{2,1,0:T(8,128)(2,1)} %shard_map.83) | data formatting | bytes 984960 | tf_op jit(solution)/shard_map/pallas_call | solution.py:262
  (16 shorter events, 0.0 us)
Async XLA Ops:
  0.0 1.2 %copy-start.5 = (bf16[76,12,270]{2,0,1:T(8,128)(2,1)S(1)}, bf16[76,12,270]{2,0,1:T(8,128)(2,1)}, u32[]{:S(2)}) copy-start(bf16[76,12,270]{2,0,1:T(8,128)(2,1)} %param.12) | copy-start | bytes 1477444
  1.2 1.1 %copy-start.1 = (s32[19,12,270]{2,1,0:T(8,128)}, s32[19,12,270]{2,1,0:T(8,128)S(1)}, u32[]{:S(2)}) copy-start(s32[19,12,270]{2,1,0:T(8,128)S(1)} %copy.19.mask_ref) | copy-start | bytes 738724
  1.4 26.7 %copy-start = (bf16[76,12,270]{2,1,0:T(8,128)(2,1)}, bf16[76,12,270]{2,1,0:T(8,128)(2,1)S(1)}, u32[]{:S(2)}) copy-start(bf16[76,12,270]{2,1,0:T(8,128)(2,1)S(1)} %copy.18.state_ref) | copy-start | bytes 1477444
  1.4 26.4 %copy-start.6 = (bf16[2,2,200,200]{3,2,1,0:T(8,128)(2,1)S(1)}, bf16[2,2,200,200]{3,2,1,0:T(8,128)(2,1)}, u32[]{:S(2)}) copy-start(bf16[2,2,200,200]{3,2,1,0:T(8,128)(2,1)} %param.16) | copy-start | bytes 960004
  1.4 26.6 %copy-start.8 = (bf16[3,3,200,76]{2,3,1,0:T(8,128)(2,1)S(1)}, bf16[3,3,200,76]{2,3,1,0:T(8,128)(2,1)}, u32[]{:S(2)}) copy-start(bf16[3,3,200,76]{2,3,1,0:T(8,128)(2,1)} %param.15) | copy-start | bytes 820804
  2.4 0.9 %copy-start.2 = (bf16[12,80,384]{2,1,0:T(8,128)(2,1)}, bf16[12,80,384]{2,1,0:T(8,128)(2,1)S(1)}, u32[]{:S(2)}) copy-start(bf16[12,80,384]{2,1,0:T(8,128)(2,1)S(1)} %get-tuple-element.33.rows_ref) | copy-start | bytes 2211844
  3.2 3.9 %collective-permute-start = (bf16[80,128]{1,0:T(8,128)(2,1)S(1)}, bf16[80,128]{1,0:T(8,128)(2,1)S(1)}, u32[]{:S(2)}, u32[]{:S(2)}) collective-permute-start(bf16[80,128]{1,0:T(8,128)(2,1)S(1)} %get-tuple-element.42), channel_id=1, source_target_pairs={{0,1},{1,2},{2,3},{3,0},{4,5},{5,6},{6,7},{7,4},{8,9},{9,10},{10,1... | collective-permute-start | bytes 61448 | tf_op jit(solution)/shard_map/ppermute | solution.py:297
  5.9 3.4 %collective-permute-start.1 = (bf16[80,128]{1,0:T(8,128)(2,1)S(1)}, bf16[80,128]{1,0:T(8,128)(2,1)S(1)}, u32[]{:S(2)}, u32[]{:S(2)}) collective-permute-start(bf16[80,128]{1,0:T(8,128)(2,1)S(1)} %get-tuple-element.41), channel_id=1, source_target_pairs={{0,3},{1,0},{2,1},{3,2},{4,7},{5,4},{6,5},{7,6},{8,11},{9,8},{10,9... | collective-permute-start | bytes 61448 | tf_op jit(solution)/shard_map/ppermute | solution.py:298
  7.1 22.6 %copy-start.12 = (bf16[80,128]{1,0:T(8,128)(2,1)}, bf16[80,128]{1,0:T(8,128)(2,1)S(1)}, u32[]{:S(2)}) copy-start(bf16[80,128]{1,0:T(8,128)(2,1)S(1)} %collective-permute-done.west_ref) | copy-start | bytes 61444
  9.4 20.4 %copy-start.13 = (bf16[80,128]{1,0:T(8,128)(2,1)}, bf16[80,128]{1,0:T(8,128)(2,1)S(1)}, u32[]{:S(2)}) copy-start(bf16[80,128]{1,0:T(8,128)(2,1)S(1)} %collective-permute-done.1.east_ref) | copy-start | bytes 61444
  9.6 20.2 %copy-start.3 = (bf16[440,256]{1,0:T(8,128)(2,1)}, bf16[440,256]{1,0:T(8,128)(2,1)S(1)}, u32[]{:S(2)}) copy-start(bf16[440,256]{1,0:T(8,128)(2,1)S(1)} %fusion.own_ref) | copy-start | bytes 675844
  9.6 25.8 %collective-permute-start.6 = (bf16[440,256]{1,0:T(8,128)(2,1)S(1)}, bf16[440,256]{1,0:T(8,128)(2,1)S(1)}, u32[]{:S(2)}, u32[]{:S(2)}) collective-permute-start(bf16[440,256]{1,0:T(8,128)(2,1)S(1)} %fusion.own_ref), channel_id=1, source_target_pairs={{0,0},{1,1},{2,2},{3,3},{4,4},{5,5},{6,6},{7,7},{8,8},{9,9},{10,10... | collective-permute-start | bytes 675848 | tf_op jit(solution)/shard_map/ppermute | solution.py:317
  10.2 25.1 %collective-permute-start.5 = (bf16[440,256]{1,0:T(8,128)(2,1)S(1)}, bf16[440,256]{1,0:T(8,128)(2,1)S(1)}, u32[]{:S(2)}, u32[]{:S(2)}) collective-permute-start(bf16[440,256]{1,0:T(8,128)(2,1)S(1)} %fusion.own_ref), channel_id=1, source_target_pairs={{0,0},{1,1},{2,2},{3,3},{4,4},{5,5},{6,6},{7,7},{8,8},{9,9},{10,10... | collective-permute-start | bytes 675848 | tf_op jit(solution)/shard_map/ppermute | solution.py:317
  10.9 24.5 %collective-permute-start.4 = (bf16[440,256]{1,0:T(8,128)(2,1)S(1)}, bf16[440,256]{1,0:T(8,128)(2,1)}, u32[]{:S(2)}, u32[]{:S(2)}) collective-permute-start(bf16[440,256]{1,0:T(8,128)(2,1)S(1)} %fusion.own_ref), channel_id=1, source_target_pairs={{0,0},{1,1},{2,2},{3,3},{4,4},{5,5},{6,6},{7,7},{8,8},{9,9},{10,10... | collective-permute-start | bytes 675848 | tf_op jit(solution)/shard_map/ppermute | solution.py:317
  12.3 23.1 %collective-permute-start.2 = (bf16[440,256]{1,0:T(8,128)(2,1)S(1)}, bf16[440,256]{1,0:T(8,128)(2,1)}, u32[]{:S(2)}, u32[]{:S(2)}) collective-permute-start(bf16[440,256]{1,0:T(8,128)(2,1)S(1)} %fusion.own_ref), channel_id=1, source_target_pairs={{0,4},{4,8},{8,12},{12,16},{16,20},{20,24},{24,28},{28,32},{32,36}... | collective-permute-start | bytes 675848 | tf_op jit(solution)/shard_map/ppermute | solution.py:313
  14.7 15.1 %copy-start.7 = (bf16[2,2,200,200]{3,2,1,0:T(8,128)(2,1)S(1)}, bf16[2,2,200,200]{3,2,1,0:T(8,128)(2,1)}, u32[]{:S(2)}) copy-start(bf16[2,2,200,200]{3,2,1,0:T(8,128)(2,1)} %param.18) | copy-start | bytes 960004
  14.7 20.7 %collective-permute-start.3 = (bf16[440,256]{1,0:T(8,128)(2,1)S(1)}, bf16[440,256]{1,0:T(8,128)(2,1)}, u32[]{:S(2)}, u32[]{:S(2)}) collective-permute-start(bf16[440,256]{1,0:T(8,128)(2,1)S(1)} %fusion.1), channel_id=1, source_target_pairs={{0,252},{4,0},{8,4},{12,8},{16,12},{20,16},{24,20},{28,24},{32,28}... | collective-permute-start | bytes 675848 | tf_op jit(solution)/shard_map/ppermute | solution.py:314
  28.9 2.0 %copy-start.9 = (bf16[3,3,76,200]{3,2,1,0:T(8,128)(2,1)S(1)}, bf16[3,3,76,200]{3,2,1,0:T(8,128)(2,1)}, u32[]{:S(2)}) copy-start(bf16[3,3,76,200]{3,2,1,0:T(8,128)(2,1)} %param.19) | copy-start | bytes 820804
  32.2 1.2 %copy-start.4 = (bf16[3,3,200,200]{3,2,1,0:T(8,128)(2,1)S(1)}, bf16[3,3,200,200]{3,2,1,0:T(8,128)(2,1)}, u32[]{:S(2)}) copy-start(bf16[3,3,200,200]{3,2,1,0:T(8,128)(2,1)} %param.17) | copy-start | bytes 2160004
  35.4 0.7 %copy-start.10 = (bf16[440,256]{1,0:T(8,128)(2,1)}, bf16[440,256]{1,0:T(8,128)(2,1)S(1)}, u32[]{:S(2)}) copy-start(bf16[440,256]{1,0:T(8,128)(2,1)S(1)} %collective-permute-done.6.fold3_ref) | copy-start | bytes 675844
  35.4 0.8 %copy-start.11 = (bf16[440,256]{1,0:T(8,128)(2,1)}, bf16[440,256]{1,0:T(8,128)(2,1)S(1)}, u32[]{:S(2)}) copy-start(bf16[440,256]{1,0:T(8,128)(2,1)S(1)} %collective-permute-done.5.fold2_ref) | copy-start | bytes 675844

commit v2 on v0

v2 whole, which is shorter than its diff:
```python
import jax
import jax.numpy as jnp
from jax import lax
from jax.experimental import pallas as pl
from jax.experimental.pallas import tpu as pltpu
from jax.sharding import PartitionSpec as P

VARS, LEVELS, CHANNELS, HIDDEN = 4, 19, 76, 200
ROWS, COLS = 12, 270
HALO = 5
CH = 80
LANES = 384
MAIN = 256
REST = COLS - MAIN
PAYLOAD = (HALO * CH + CH // 2, MAIN)
PIX = 144
HID = 256
TROWS = 408
CHUNK = 3
F32, BF16 = jnp.float32, jnp.bfloat16
VMEM = pl.BlockSpec(memory_space=pltpu.VMEM)
HBM = pl.BlockSpec(memory_space=pltpu.HBM)
SMEM = pl.BlockSpec(memory_space=pltpu.SMEM)


def dot_nt(a, b):
    return lax.dot_general(a, b, (((1,), (1,)), ((), ())), preferred_element_type=F32)


def gelu(x):
    inner = x * (0.7978845608028654 + 0.035677408136300125 * (x * x))
    half = 0.5 * x
    return half + half * jnp.tanh(inner)


def cost(us):
    return pl.CostEstimate(flops=int(us * 1e9), bytes_accessed=int(us * 3e6), transcendentals=0)


def call(kernel, ins, operands, outs, scratch, us, mib):
    return pl.pallas_call(
        kernel,
        out_shape=tuple(jax.ShapeDtypeStruct(shape, BF16) for shape in outs),
        in_specs=ins,
        out_specs=(VMEM,) * len(outs),
        scratch_shapes=scratch,
        cost_estimate=cost(us),
        compiler_params=pltpu.CompilerParams(vmem_limit_bytes=mib * 2**20),
    )(*operands)


def masked_row(state_ref, mask_ref, r):
    cover = mask_ref[r].astype(F32)
    row = state_ref[r].astype(F32) * jnp.concatenate([cover] * VARS, axis=0)
    row = jnp.concatenate([row, jnp.zeros((CHANNELS, LANES - COLS), F32)], axis=1)
    return jnp.concatenate([row, jnp.zeros((CH - CHANNELS, LANES), F32)], axis=0)


def tail_out(tail):
    return jnp.concatenate([tail[: CH // 2], tail[CH // 2 :]], axis=1).astype(BF16)


def tail_in(payload_ref):
    low = payload_ref[HALO * CH :, :]
    return jnp.concatenate([low[:, :128], low[:, 128:]], axis=0).astype(F32)


def edge_kernel(state_hbm, mask_hbm, rows_ref, east_ref, west_ref, fold_ref, state_ref, mask_ref, sems):
    copies = []
    for i in range(ROWS // CHUNK):
        rows = pl.ds(i * CHUNK, CHUNK)
        for j, (hbm, ref) in enumerate(((mask_hbm, mask_ref), (state_hbm, state_ref))):
            copies.append(pltpu.make_async_copy(hbm.at[rows], ref.at[rows], sems.at[j, i]))
            copies[-1].start()
    low, high, rest = [], [], []
    for r in range(ROWS):
        if r % CHUNK == 0:
            for copy in copies[2 * (r // CHUNK) : 2 * (r // CHUNK) + 2]:
                copy.wait()
        row = masked_row(state_ref, mask_ref, r)
        rows_ref[r] = row.astype(BF16)
        low.append(row[:, :HALO])
        high.append(row[:, COLS - HALO : COLS])
        k = r - (ROWS - HALO)
        if k >= 0:
            fold_ref[k * CH : (k + 1) * CH, :] = row[:, :MAIN].astype(BF16)
            rest.append(row[:, MAIN:COLS])
    zeros = lambda n: [jnp.zeros((CH, 128 - n), F32)]
    west_ref[...] = jnp.concatenate(low + zeros(ROWS * HALO), axis=1).astype(BF16)
    east_ref[...] = jnp.concatenate(high + zeros(ROWS * HALO), axis=1).astype(BF16)
    fold_ref[HALO * CH :, :] = tail_out(jnp.concatenate(rest + zeros(HALO * REST), axis=1))


def payload_kernel(rows_ref, west_ref, east_ref, pay0_ref, pay1_ref):
    odd = lax.rem(lax.axis_index("lat"), 2)
    lane = lax.broadcasted_iota(jnp.int32, (CH, 128), 1)
    beyond = []
    for first in (0, ROWS - HALO):
        sides = []
        for side, edge_ref in enumerate((west_ref, east_ref)):
            begin = HALO * (REST + side * HALO)
            rolled = pltpu.roll(edge_ref[...].astype(F32), (begin - first * HALO) % 128, 1)
            inside = jnp.logical_and(lane >= begin, lane < begin + HALO * HALO)
            sides.append(jnp.where(inside, rolled, 0.0))
        beyond.append(sides[0] + sides[1])
    for ref, north in ((pay0_ref, 1 - odd), (pay1_ref, odd)):
        rest = []
        for k in range(HALO):
            row = rows_ref[(ROWS - HALO) * north + k]
            ref[k * CH : (k + 1) * CH, :] = row[:, :MAIN]
            rest.append(row[:, MAIN:COLS].astype(F32))
        tail = jnp.concatenate(rest + [jnp.zeros((CH, 128 - HALO * REST), F32)], axis=1)
        ref[HALO * CH :, :] = tail_out(tail + jnp.where(north == 1, beyond[1], beyond[0]))


def weight_kernel(w_in, w_down, w_mid, w_up, w_out, in_ref, down_ref, mid_ref, up_ref, out_ref):
    for ref in (in_ref, down_ref, mid_ref, up_ref, out_ref):
        ref[...] = jnp.zeros(ref.shape, BF16)
    for raw, ref in ((w_in, in_ref), (w_down, down_ref), (w_mid, mid_ref), (w_up, up_ref)):
        for t in range(raw.shape[0]):
            ref[t, : raw.shape[1], :HIDDEN] = raw[t]
    for a in range(3):
        for b in range(3):
            for r in range(3):
                t = 3 * (a + r) + b
                out_ref[r * CH : r * CH + CHANNELS, t * HID : t * HID + HIDDEN] = w_out[3 * a + b]


def flip(block):
    n = block.shape[1]
    return jnp.concatenate([block, jnp.zeros((128 - CH, n), F32)], axis=0).T


def pack(t_ref, a_ref, ai):
    lane = lax.broadcasted_iota(jnp.int32, (PIX, 128), 1)
    odd_left, even, odd, even_right = (t_ref[pl.ds(3 + s, PIX, stride=2), :] for s in range(4))
    even80, odd80 = pltpu.roll(even, CH, 1), pltpu.roll(odd, CH, 1)
    for p, (left, mid, right) in enumerate(((odd_left, even80, odd), (even, odd80, even_right))):
        low = jnp.where(lane < CH, left, mid)
        high = jnp.where(lane < 2 * CH - 128, mid, pltpu.roll(right, 2 * CH - 128, 1))
        a_ref[ai, p * PIX : (p + 1) * PIX, :] = jnp.concatenate([low, high], axis=1).astype(BF16)


def straight(t, n):
    return t


def first_rows(a_ref, f_ref, w_ref, fr, n, tap):
    w = []
    for a in range(3):
        w += [w_ref[tap(3 * a + b, 9)] for b in range(3)] + [jnp.zeros((HID - 3 * CH, HID), BF16)]
    w = jnp.concatenate(w, axis=0)
    for q in range(n):
        taps = jnp.concatenate([a_ref[fr + q + a] for a in range(3)], axis=1)
        f_ref[fr + q] = gelu(jnp.dot(taps, w, preferred_element_type=F32)).astype(BF16)


def coarse_rows(f_ref, c_ref, w_ref, ci, n, tap, held):
    w = jnp.concatenate([w_ref[tap(t, 4)] for t in range(4)], axis=1)
    pieces = []
    for q in range(n):
        piece = [f_ref[2 * (ci + q) + a, b * PIX : (b + 1) * PIX, :] for a in range(2) for b in range(2)]
        pieces.append(jnp.concatenate(piece, axis=1))
    coarse = gelu(dot_nt(jnp.concatenate(pieces, axis=0), w))
    if held is not None:
        coarse = coarse * held
    for q in range(n):
        one = coarse[q * PIX : (q + 1) * PIX]
        planes = [pltpu.roll(one, 1, 0), one, pltpu.roll(one, PIX - 1, 0)]
        c_ref[ci + q] = jnp.concatenate(planes, axis=1).astype(BF16)


def mid_rows(c_ref, f_ref, j_ref, mid_ref, up_ref, mi, n, tap, held):
    taps = [c_ref[pl.ds(mi + a, n)].reshape(n * PIX, 3 * HID) for a in range(3)]
    w = jnp.concatenate([mid_ref[tap(t, 9)] for t in range(9)], axis=1)
    middle = gelu(dot_nt(jnp.concatenate(taps, axis=1), w)).astype(BF16)
    for a in range(2):
        grown = [dot_nt(middle, up_ref[tap(2 * a + b, 4)]) for b in range(2)]
        for q in range(n):
            row = 2 * (mi + q) + a
            halves = []
            for b in range(2):
                first = f_ref[row + 2, b * PIX : (b + 1) * PIX, :].astype(F32)
                half = gelu(grown[b][q * PIX : (q + 1) * PIX]) + first
                halves.append(half * held if held is not None and q == 0 else half)
            even, odd = halves
            planes = (pltpu.roll(odd, 1, 0), even, odd, pltpu.roll(even, PIX - 1, 0))
            for s, plane in enumerate(planes):
                j_ref[row, s * PIX : (s + 1) * PIX, :] = plane.astype(BF16)


A_KEPT = (5, 6, 15, 16)
F_KEPT = (5, 6, 7, 12, 13, 14)
C_KEPT = (3, 4, 5, 6)
J_KEPT = (6, 7, 8, 9)
KEPT = (A_KEPT, F_KEPT, C_KEPT, J_KEPT)
BLOCKS = ((2 * PIX, HID), (2 * PIX, HID), (PIX, 3 * HID), (4 * PIX, HID))
HELD = [pltpu.VMEM((n,) + block, BF16) for n, block in zip((22, 20, 10, 16), BLOCKS)]


def inner_kernel(rows_ref, west_ref, east_ref, in_ref, down_ref, mid_ref, up_ref, *refs):
    outs, (t_refs, edge_ref, a_ref, f_ref, c_ref, j_ref) = refs[:4], refs[4:]
    edge_ref[0] = flip(west_ref[...].astype(F32))
    edge_ref[1] = flip(east_ref[...].astype(F32))

    def own_rows(i, carry):
        for q in range(2):
            t_ref, r = t_refs.at[q], 2 * i + q
            t_ref[8 : 8 + LANES, :] = flip(rows_ref[r].astype(F32))
            t_ref[8 - HALO : 8, :] = edge_ref[0, pl.ds(r * HALO, HALO), :]
            t_ref[8 + COLS : 8 + COLS + HALO, :] = edge_ref[1, pl.ds(r * HALO, HALO), :]
            pack(t_ref, a_ref, r + HALO)
        return carry

    lax.fori_loop(0, ROWS // 2, own_rows, 0)

    def first_group(i, carry):
        first_rows(a_ref, f_ref, in_ref, 5 + 2 * i, 2, straight)
        return carry

    lax.fori_loop(0, 5, first_group, 0)
    coarse_rows(f_ref, c_ref, down_ref, 3, 4, straight, None)
    mid_rows(c_ref, f_ref, j_ref, mid_ref, up_ref, 3, 2, straight, None)
    for ref, out_ref, kept in zip((a_ref, f_ref, c_ref, j_ref), outs, KEPT):
        for i, row in enumerate(kept):
            out_ref[i] = ref[row]


def outer_kernel(
    seam_ref, got0_ref, got1_ref, fold2_ref, fold3_ref, own_ref, in_ref, down_ref, mid_ref, up_ref, w_out_ref,
    state_ref, mask_ref, a_in, f_in, c_in, j_in, out_ref, t_refs, edge_ref, a_ref, f_ref, c_ref, j_ref, u_ref,
):
    n_lat, n_lon = lax.axis_size("lat"), lax.axis_size("lon")
    lat, lon = lax.axis_index("lat"), lax.axis_index("lon")
    bottom, top = lat == 0, lat == n_lat - 1
    keep = jnp.where(bottom, 0.0, 1.0).astype(F32)
    for ref, in_ref_, kept in zip((a_ref, f_ref, c_ref, j_ref), (a_in, f_in, c_in, j_in), KEPT):
        for i, row in enumerate(kept):
            ref[row] = in_ref_[i]
    edge_ref[0] = flip(tail_in(got0_ref))
    edge_ref[1] = flip(tail_in(got1_ref))

    def halo_row(t_ref, ref, side, k, ai):
        t_ref[8 : 8 + MAIN, :] = flip(ref[pl.ds(pl.multiple_of(k * CH, CH), CH), :].astype(F32))
        t_ref[8 + MAIN : 8 + COLS, :] = edge_ref[side, pl.ds(k * REST, REST), :]
        t_ref[8 - HALO : 8, :] = edge_ref[side, pl.ds(HALO * REST + k * HALO, HALO), :]
        t_ref[8 + COLS : 8 + COLS + HALO, :] = edge_ref[side, pl.ds(HALO * (REST + HALO) + k * HALO, HALO), :]
        pack(t_ref, a_ref, ai)

    odd = lax.rem(lat, 2)
    at = (1 - odd) * (ROWS + HALO), odd * (ROWS + HALO)
    t_refs[...] = jnp.zeros(t_refs.shape, F32)

    def halo_rows(k, carry):
        halo_row(t_refs.at[0], got0_ref, 0, k, at[0] + k)
        halo_row(t_refs.at[1], got1_ref, 1, k, at[1] + k)
        return carry

    lax.fori_loop(0, HALO, halo_rows, 0)

    @pl.when(bottom)
    def _():
        a_ref[0:HALO] = jnp.zeros((HALO, 2 * PIX, HID), BF16)

    @pl.when(top)
    def _():
        circle = n_lon * COLS
        span = 288
        column = lax.broadcasted_iota(jnp.int32, (span, 128), 0) - 8 + COLS * lon
        source = lax.rem(seam_ref[0] - column + 3 * circle, circle)
        spot = lax.broadcasted_iota(jnp.int32, (span, 128), 1)

        def fold_row(k, carry):
            kk = HALO - 1 - k
            total = jnp.zeros((span, CH), F32)
            for d, ref in enumerate((own_ref, got1_ref, fold2_ref, fold3_ref)):
                place = source - lax.bitwise_xor(lon, d) * COLS
                hot = [(place == spot), (place == spot + 128)]
                inside = jnp.logical_and(place >= MAIN, place < COLS)
                hot.append(jnp.logical_and(inside, place - MAIN + kk * REST == spot))
                hot = jnp.concatenate([jnp.where(h, 1.0, 0.0).astype(BF16) for h in hot], axis=1)
                main = ref[pl.ds(pl.multiple_of(kk * CH, CH), CH), :]
                total += dot_nt(hot, jnp.concatenate([main, tail_in(ref).astype(BF16)], axis=1))
            t_refs[0, 0:span, :] = jnp.concatenate([total, jnp.zeros((span, 128 - CH), F32)], axis=1)
            pack(t_refs.at[0], a_ref, ROWS + HALO + k)
            return carry

        lax.fori_loop(0, HALO, fold_row, 0)

    def first_group(i, carry):
        turned = jnp.logical_and(top, i == 1)
        tap = lambda t, n: jnp.where(turned, n - 1 - t, t)
        first_rows(a_ref, f_ref, in_ref, 4 + 11 * i, 1, straight)
        first_rows(a_ref, f_ref, in_ref, 16 * i, 4, tap)
        coarse_rows(f_ref, c_ref, down_ref, 8 * i, 2, tap, jnp.where(i == 0, keep, 1.0))
        coarse_rows(f_ref, c_ref, down_ref, 2 + 5 * i, 1, straight, None)
        return carry

    lax.fori_loop(0, 2, first_group, 0)

    def mid_group(i, carry):
        held = jnp.where(i == 0, keep, 1.0)
        mid_rows(c_ref, f_ref, j_ref, mid_ref, up_ref, 5 * i, 3, straight, held)
        return carry

    lax.fori_loop(0, 2, mid_group, 0)

    @pl.when(top)
    def _():
        mid_rows(c_ref, f_ref, j_ref, mid_ref, up_ref, 7, 1, lambda t, n: n - 1 - t, None)

    def out_rows(g, carry):
        groups = []
        for q in range(2):
            jr = 6 * g + 3 * q + 1
            taps = [j_ref[jr + i, b * PIX : (b + 2) * PIX, :] for i in range(5) for b in range(3)]
            groups.append(jnp.concatenate(taps, axis=1))
        deltas = dot_nt(jnp.concatenate(groups, axis=0), w_out_ref[...])
        for q in range(2):
            flipped = []
            for t in range(2):
                for p in range(2):
                    begin = (2 * q + p) * PIX
                    half = deltas[begin : begin + PIX, t * 128 : (t + 1) * 128]
                    u_ref[pl.ds((2 * q + t) * TROWS + 4 + p, PIX, stride=2), :] = half
                begin = (2 * q + t) * TROWS + 8
                flipped.append(u_ref[begin : begin + LANES, :].T)
            flipped = jnp.concatenate(flipped, axis=0)
            for i in range(3):
                r = 6 * g + 3 * q + i
                delta = flipped[i * CH : i * CH + CHANNELS, :COLS]
                cover = jnp.concatenate([mask_ref[r].astype(F32)] * VARS, axis=0)
                out_ref[r] = ((state_ref[r].astype(F32) + delta) * cover).astype(BF16)
        return carry

    lax.fori_loop(0, 2, out_rows, 0)


def body(state, sea_mask, seam, w_in, w_down, w_mid, w_up, w_out):
    n_lat, n_lon = lax.axis_size("lat"), lax.axis_size("lon")
    ring = lambda n, d: [(i, (i + d) % n) for i in range(n)]
    state, sea_mask = jnp.swapaxes(state, 0, 1), jnp.swapaxes(sea_mask, 0, 1)
    flat = lambda w: w.reshape((-1,) + w.shape[2:])
    edge = (CH, 128)
    rows, east_going, west_going, fold = call(
        edge_kernel, [HBM] * 2, (state, sea_mask), [(ROWS, CH, LANES), edge, edge, PAYLOAD],
        [
            pltpu.VMEM((ROWS, CHANNELS, COLS), BF16),
            pltpu.VMEM((ROWS, LEVELS, COLS), jnp.int32),
            pltpu.SemaphoreType.DMA((2, ROWS // CHUNK)),
        ],
        1.5, 12,
    )
    west = lax.ppermute(east_going, "lon", ring(n_lon, 1))
    east = lax.ppermute(west_going, "lon", ring(n_lon, -1))

    def swap(begin, d):
        pairs = []
        for i in range(n_lat):
            for j in range(n_lon):
                mate = i + 1 if (i - begin) % 2 == 0 else i - 1
                if begin < n_lat and 0 <= mate < n_lat:
                    pairs.append((i * n_lon + j, mate * n_lon + j))
                else:
                    pairs.append((i * n_lon + j, i * n_lon + (j ^ (d if i == n_lat - 1 else 1))))
        return pairs

    axes = ("lat", "lon")
    folds = [lax.ppermute(fold, axes, swap(n_lat, d)) for d in (2, 3)]
    laid = call(
        weight_kernel, [VMEM] * 5, (flat(jnp.swapaxes(w_in, 2, 3)), flat(w_down), flat(w_mid), flat(w_up), flat(w_out)),
        [(9, CH, HID), (4, HID, HID), (9, HID, HID), (4, HID, HID), (HID, 15 * HID)], [], 1.5, 16,
    )
    pay0, pay1 = call(payload_kernel, [VMEM] * 3, (rows, west, east), [PAYLOAD] * 2, [], 0.5, 8)
    got0 = lax.ppermute(pay0, axes, swap(0, 1))
    got1 = lax.ppermute(pay1, axes, swap(1, 1))
    kept = [(len(k),) + block for k, block in zip(KEPT, BLOCKS)]
    inner = call(
        inner_kernel, [VMEM] * 7, (rows, west, east, *laid[:4]), kept,
        [pltpu.VMEM((2, TROWS, 128), F32), pltpu.VMEM((2, 128, 128), F32)] + HELD, 6, 30,
    )
    (out,) = call(
        outer_kernel, [SMEM] + [VMEM] * 16,
        (seam, got0, got1, *folds, fold, *laid, state, sea_mask, *inner), [(ROWS, CHANNELS, COLS)],
        [pltpu.VMEM((2, TROWS, 128), F32), pltpu.VMEM((2, 128, 128), F32)] + HELD + [pltpu.VMEM((4 * TROWS, 128), F32)],
        12, 36,
    )
    return jnp.swapaxes(out, 0, 1)


def solution(mesh):
    return jax.shard_map(
        body,
        mesh=mesh,
        in_specs=(P(None, "lat", "lon"), P(None, "lat", "lon"), P(), P(), P(), P(), P(), P()),
        out_specs=P(None, "lat", "lon"),
        check_vma=False,
    )
```

time: 139 us -> 43.3 us (0.31)
  the two profiles are of different devices: /device:TPU:7 before, /device:TPU:255 now
where the time goes in v2:
time: 43.3 us; the launch traced here: 43.1 us
  Pallas kernels  25.3 us (58%)
  waiting for transfers between devices  12.4 us (29%)
  starting transfers between devices  3.09 us (7%)
  local copies, waits for them, and re-layouts  2.17 us (5%)
    pallas_call x5, Pallas kernels, call(): pl.pallas_call(kernel, out_shape=tuple((jax.ShapeDtypeStruct(shape, BF16)...  25.3 us
    ppermute x1, waiting for transfers between devices, body(): west = lax.ppermute(east_going, 'lon', ring(n_lon, 1))  6.56 us
    ppermute x1, waiting for transfers between devices, body(): got0 = lax.ppermute(pay0, axes, swap(0, 1))  3.24 us
    ppermute x1, waiting for transfers between devices, body(): east = lax.ppermute(west_going, 'lon', ring(n_lon, -1))  2.59 us
    ppermute x2, starting transfers between devices, body(): folds = [lax.ppermute(fold, axes, swap(n_lat, d)) for d in (2, 3)]  2.39 us
    unnamed x20, local copies, waits for them, and re-layouts  2.17 us
  transfers between devices with their start and end apart: 6, of which 3 were waited for; matrix products, arithmetic and copies ran while one was open for 0% of the time, Pallas kernels for 17%

profile of v2, /device:TPU:255, one launch (start us, length us, event | category | flops | bytes accessed | tf_op | source)
XLA Modules:
  0.0 43.1 jit_solution(4736557539831313393)
XLA Ops:
  0.0 0.0 copy-start.1
  0.0 1.1 %copy-done.1 = bf16[76,12,270]{2,0,1:T(8,128)(2,1)S(1)} copy-done((bf16[76,12,270]{2,0,1:T(8,128)(2,1)S(1)}, bf16[76,12,270]{2,0,1:T(8,128)(2,1)}, u32[]{:S(2)}) %copy-start.1) | copy-done | bytes 492504
  1.1 0.0 copy-start.3
  1.1 1.0 %copy-done.3 = s32[19,12,270]{2,0,1:T(8,128)S(1)} copy-done((s32[19,12,270]{2,0,1:T(8,128)S(1)}, s32[19,12,270]{2,0,1:T(8,128)}, u32[]{:S(2)}) %copy-start.3) | copy-done | bytes 246264
  2.1 0.0 copy-start
  2.1 0.0 copy-start.5
  2.1 0.0 copy-start.6
  2.1 0.0 copy-start.7
  2.1 0.0 copy-start.8
  2.2 2.0 %shard_map.82 = (bf16[12,80,384]{2,1,0:T(8,128)(2,1)S(1)}, bf16[80,128]{1,0:T(8,128)(2,1)S(1)}, bf16[80,128]{1,0:T(8,128)(2,1)S(1)}, bf16[440,256]{1,0:T(8,128)(2,1)S(1)}) custom-call(bf16[12,76,270]{2,1,0:T(8,128)(2,1)S(1)} %bitcast.11, s32[12,19,270]{2,1,0:T(8,128)S(1)} %bitcast.13), custom_call_target="tpu_custom_call" | custom-call | flops 1500000000 | bytes 4500000 | tf_op jit(solution)/shard_map/pallas_call | solution.py:41
  4.2 0.5 %collective-permute-start.4 = (bf16[440,256]{1,0:T(8,128)(2,1)S(1)}, bf16[440,256]{1,0:T(8,128)(2,1)S(1)}, u32[]{:S(2)}, u32[]{:S(2)}) collective-permute-start(bf16[440,256]{1,0:T(8,128)(2,1)S(1)} %get-tuple-element.25.own_ref), channel_id=1, source_target_pairs={{0,1},{1,0},{2,3},{3,2},{4,5},{5,4},{6,7},{7,6},{8,9},{9,8},{10,11... | collective-permute-start | bytes 675848 | tf_op jit(solution)/shard_map/ppermute | solution.py:369
  4.7 1.8 %collective-permute-start.5 = (bf16[440,256]{1,0:T(8,128)(2,1)S(1)}, bf16[440,256]{1,0:T(8,128)(2,1)S(1)}, u32[]{:S(2)}, u32[]{:S(2)}) collective-permute-start(bf16[440,256]{1,0:T(8,128)(2,1)S(1)} %get-tuple-element.25.own_ref), channel_id=1, source_target_pairs={{0,1},{1,0},{2,3},{3,2},{4,5},{5,4},{6,7},{7,6},{8,9},{9,8},{10,11... | collective-permute-start | bytes 675848 | tf_op jit(solution)/shard_map/ppermute | solution.py:369
  6.6 0.0 collective-permute-start
  6.6 0.5 %collective-permute-start.1 = (bf16[80,128]{1,0:T(8,128)(2,1)S(1)}, bf16[80,128]{1,0:T(8,128)(2,1)S(1)}, u32[]{:S(2)}, u32[]{:S(2)}) collective-permute-start(bf16[80,128]{1,0:T(8,128)(2,1)S(1)} %get-tuple-element.22), channel_id=1, source_target_pairs={{0,3},{1,0},{2,1},{3,2},{4,7},{5,4},{6,5},{7,6},{8,11},{9,8},{10,9... | collective-permute-start | bytes 61448 | tf_op jit(solution)/shard_map/ppermute | solution.py:355
  7.1 0.0 copy-done
  7.1 0.0 copy-done.5
  7.1 0.0 copy-done.6
  7.1 0.0 copy-done.7
  7.1 0.0 copy-done.8
  7.1 0.5 %shard_map.84 = (bf16[9,80,256]{2,1,0:T(8,128)(2,1)S(1)}, bf16[4,256,256]{2,1,0:T(8,128)(2,1)S(1)}, bf16[9,256,256]{2,1,0:T(8,128)(2,1)S(1)}, bf16[4,256,256]{2,1,0:T(8,128)(2,1)S(1)}, bf16[256,3840]{1,0:T(8,128)(2,1)S(1)}) custom-call(bf16[9,76,200]{2,1,0:T(8,128)(2,1)S(1)} %bitcast.17, bf16[4,200,200]{2,1,0:T(8,128)(2,1)S(1)} %bitcast.15, ...), custom_call_target="tpu_custom_call" | custom-call | flops 1500000000 | bytes 4500000 | tf_op jit(solution)/shard_map/pallas_call | solution.py:41
  7.6 6.6 %collective-permute-done.west_ref = bf16[80,128]{1,0:T(8,128)(2,1)S(1)} collective-permute-done((bf16[80,128]{1,0:T(8,128)(2,1)S(1)}, bf16[80,128]{1,0:T(8,128)(2,1)S(1)}, u32[]{:S(2)}, u32[]{:S(2)}) %collective-permute-start) | collective-permute-done | bytes 20512 | tf_op jit(solution)/shard_map/ppermute | solution.py:354
  14.2 2.6 %collective-permute-done.1.east_ref = bf16[80,128]{1,0:T(8,128)(2,1)S(1)} collective-permute-done((bf16[80,128]{1,0:T(8,128)(2,1)S(1)}, bf16[80,128]{1,0:T(8,128)(2,1)S(1)}, u32[]{:S(2)}, u32[]{:S(2)}) %collective-permute-start.1) | collective-permute-done | bytes 20512 | tf_op jit(solution)/shard_map/ppermute | solution.py:355
  16.8 0.1 shard_map.83
  16.9 0.1 collective-permute-start.2
  17.0 0.1 collective-permute-start.3
  17.1 0.0 copy-start.2
  17.1 0.0 copy-start.4
  17.1 0.0 copy-start.9
  17.2 6.5 %shard_map.85 = (bf16[4,288,256]{2,1,0:T(8,128)(2,1)S(1)}, bf16[6,288,256]{2,1,0:T(8,128)(2,1)S(1)}, bf16[4,144,768]{2,1,0:T(8,128)(2,1)S(1)}, bf16[4,576,256]{2,1,0:T(8,128)(2,1)S(1)}) custom-call(bf16[12,80,384]{2,1,0:T(8,128)(2,1)S(1)} %get-tuple-element.20.rows_ref, bf16[80,128]{1,0:T(8,128)(2,1)S(1)} %collective-permute-done.west_ref, ...), custom_call_target="tpu_custom_call" | custom-call | flops 6000000000 | bytes 18000000 | tf_op jit(solution)/shard_map/pallas_call | solution.py:41
  23.6 0.0 collective-permute-done.4.fold2_ref
  23.6 0.0 collective-permute-done.5.fold3_ref
  23.7 3.2 %collective-permute-done.2.got0_ref = bf16[440,256]{1,0:T(8,128)(2,1)S(1)} collective-permute-done((bf16[440,256]{1,0:T(8,128)(2,1)S(1)}, bf16[440,256]{1,0:T(8,128)(2,1)S(1)}, u32[]{:S(2)}, u32[]{:S(2)}) %collective-permute-start.2) | collective-permute-done | bytes 225312 | tf_op jit(solution)/shard_map/ppermute | solution.py:375
  26.9 0.0 collective-permute-done.3.got1_ref
  26.9 0.0 copy-done.2
  26.9 0.0 copy-done.4
  26.9 0.0 copy-done.9
  26.9 16.2 %shard_map.86 = bf16[12,76,270]{2,1,0:T(8,128)(2,1)} custom-call(s32[1080]{0:T(1024)S(1)} %copy-done.9, bf16[440,256]{1,0:T(8,128)(2,1)S(1)} %collective-permute-done.2.got0_ref, bf16[440,256]{1,0:T(8,128)(2,1)S(1)} %collective-permute-done.3.got1_ref, bf16[440,256]{1,0:T(8,128)(2,1)S(1)} %collective-permute-done.4.fold2_ref, ...), custom_call_target="tpu_custom_call" | custom-call | flops 12000000000 | bytes 36000000 | tf_op jit(solution)/shard_map/pallas_call | solution.py:41
Async XLA Ops:
  0.0 1.1 %copy-start.1 = (bf16[76,12,270]{2,0,1:T(8,128)(2,1)S(1)}, bf16[76,12,270]{2,0,1:T(8,128)(2,1)}, u32[]{:S(2)}) copy-start(bf16[76,12,270]{2,0,1:T(8,128)(2,1)} %param.8) | copy-start | bytes 1477444
  1.1 1.0 %copy-start.3 = (s32[19,12,270]{2,0,1:T(8,128)S(1)}, s32[19,12,270]{2,0,1:T(8,128)}, u32[]{:S(2)}) copy-start(s32[19,12,270]{2,0,1:T(8,128)} %param.9) | copy-start | bytes 738724
  2.1 5.0 %copy-start = (bf16[3,3,200,200]{3,2,1,0:T(8,128)(2,1)S(1)}, bf16[3,3,200,200]{3,2,1,0:T(8,128)(2,1)}, u32[]{:S(2)}) copy-start(bf16[3,3,200,200]{3,2,1,0:T(8,128)(2,1)} %param.13) | copy-start | bytes 2160004
  2.1 5.0 %copy-start.5 = (bf16[2,2,200,200]{3,2,1,0:T(8,128)(2,1)S(1)}, bf16[2,2,200,200]{3,2,1,0:T(8,128)(2,1)}, u32[]{:S(2)}) copy-start(bf16[2,2,200,200]{3,2,1,0:T(8,128)(2,1)} %param.12) | copy-start | bytes 960004
  2.1 5.0 %copy-start.6 = (bf16[2,2,200,200]{3,2,1,0:T(8,128)(2,1)S(1)}, bf16[2,2,200,200]{3,2,1,0:T(8,128)(2,1)}, u32[]{:S(2)}) copy-start(bf16[2,2,200,200]{3,2,1,0:T(8,128)(2,1)} %param.14) | copy-start | bytes 960004
  2.1 5.0 %copy-start.7 = (bf16[3,3,200,76]{2,3,1,0:T(8,128)(2,1)S(1)}, bf16[3,3,200,76]{2,3,1,0:T(8,128)(2,1)}, u32[]{:S(2)}) copy-start(bf16[3,3,200,76]{2,3,1,0:T(8,128)(2,1)} %param.11) | copy-start | bytes 820804
  2.1 5.0 %copy-start.8 = (bf16[3,3,76,200]{3,2,1,0:T(8,128)(2,1)S(1)}, bf16[3,3,76,200]{3,2,1,0:T(8,128)(2,1)}, u32[]{:S(2)}) copy-start(bf16[3,3,76,200]{3,2,1,0:T(8,128)(2,1)} %param.15) | copy-start | bytes 820804
  4.2 19.5 %collective-permute-start.4 = (bf16[440,256]{1,0:T(8,128)(2,1)S(1)}, bf16[440,256]{1,0:T(8,128)(2,1)S(1)}, u32[]{:S(2)}, u32[]{:S(2)}) collective-permute-start(bf16[440,256]{1,0:T(8,128)(2,1)S(1)} %get-tuple-element.25.own_ref), channel_id=1, source_target_pairs={{0,1},{1,0},{2,3},{3,2},{4,5},{5,4},{6,7},{7,6},{8,9},{9,8},{10,11... | collective-permute-start | bytes 675848 | tf_op jit(solution)/shard_map/ppermute | solution.py:369
  4.7 18.9 %collective-permute-start.5 = (bf16[440,256]{1,0:T(8,128)(2,1)S(1)}, bf16[440,256]{1,0:T(8,128)(2,1)S(1)}, u32[]{:S(2)}, u32[]{:S(2)}) collective-permute-start(bf16[440,256]{1,0:T(8,128)(2,1)S(1)} %get-tuple-element.25.own_ref), channel_id=1, source_target_pairs={{0,1},{1,0},{2,3},{3,2},{4,5},{5,4},{6,7},{7,6},{8,9},{9,8},{10,11... | collective-permute-start | bytes 675848 | tf_op jit(solution)/shard_map/ppermute | solution.py:369
  6.6 7.6 %collective-permute-start = (bf16[80,128]{1,0:T(8,128)(2,1)S(1)}, bf16[80,128]{1,0:T(8,128)(2,1)S(1)}, u32[]{:S(2)}, u32[]{:S(2)}) collective-permute-start(bf16[80,128]{1,0:T(8,128)(2,1)S(1)} %get-tuple-element.21), channel_id=1, source_target_pairs={{0,1},{1,2},{2,3},{3,0},{4,5},{5,6},{6,7},{7,4},{8,9},{9,10},{10,1... | collective-permute-start | bytes 61448 | tf_op jit(solution)/shard_map/ppermute | solution.py:354
  6.6 10.2 %collective-permute-start.1 = (bf16[80,128]{1,0:T(8,128)(2,1)S(1)}, bf16[80,128]{1,0:T(8,128)(2,1)S(1)}, u32[]{:S(2)}, u32[]{:S(2)}) collective-permute-start(bf16[80,128]{1,0:T(8,128)(2,1)S(1)} %get-tuple-element.22), channel_id=1, source_target_pairs={{0,3},{1,0},{2,1},{3,2},{4,7},{5,4},{6,5},{7,6},{8,11},{9,8},{10,9... | collective-permute-start | bytes 61448 | tf_op jit(solution)/shard_map/ppermute | solution.py:355
  16.9 10.0 %collective-permute-start.2 = (bf16[440,256]{1,0:T(8,128)(2,1)S(1)}, bf16[440,256]{1,0:T(8,128)(2,1)S(1)}, u32[]{:S(2)}, u32[]{:S(2)}) collective-permute-start(bf16[440,256]{1,0:T(8,128)(2,1)S(1)} %get-tuple-element.23), channel_id=1, source_target_pairs={{0,4},{1,5},{2,6},{3,7},{4,0},{5,1},{6,2},{7,3},{8,12},{9,13},{10,... | collective-permute-start | bytes 675848 | tf_op jit(solution)/shard_map/ppermute | solution.py:375
  17.0 9.9 %collective-permute-start.3 = (bf16[440,256]{1,0:T(8,128)(2,1)S(1)}, bf16[440,256]{1,0:T(8,128)(2,1)S(1)}, u32[]{:S(2)}, u32[]{:S(2)}) collective-permute-start(bf16[440,256]{1,0:T(8,128)(2,1)S(1)} %get-tuple-element.24), channel_id=1, source_target_pairs={{0,1},{1,0},{2,3},{3,2},{4,8},{5,9},{6,10},{7,11},{8,4},{9,5},{10,... | collective-permute-start | bytes 675848 | tf_op jit(solution)/shard_map/ppermute | solution.py:376
  17.1 9.8 %copy-start.2 = (bf16[76,12,270]{2,0,1:T(8,128)(2,1)S(1)}, bf16[76,12,270]{2,0,1:T(8,128)(2,1)}, u32[]{:S(2)}) copy-start(bf16[76,12,270]{2,0,1:T(8,128)(2,1)} %param.8) | copy-start | bytes 1477444
  17.1 9.8 %copy-start.4 = (s32[19,12,270]{2,0,1:T(8,128)S(1)}, s32[19,12,270]{2,0,1:T(8,128)}, u32[]{:S(2)}) copy-start(s32[19,12,270]{2,0,1:T(8,128)} %param.9) | copy-start | bytes 738724
  17.1 9.8 %copy-start.9 = (s32[1080]{0:T(1024)S(1)}, s32[1080]{0:T(1024)}, u32[]{:S(2)}) copy-start(s32[1080]{0:T(1024)} %seam_ref.1) | copy-start | bytes 12964

commit v3 on v2

v3 whole, which is shorter than its diff:
```python
import functools

import jax
import jax.numpy as jnp
from jax import lax
from jax.experimental import pallas as pl
from jax.experimental.pallas import tpu as pltpu
from jax.sharding import PartitionSpec as P

VARS, LEVELS, CHANNELS, HIDDEN = 4, 19, 76, 200
ROWS, COLS = 12, 270
HALO = 5
CH = 80
LANES = 384
MAIN = 256
REST = COLS - MAIN
PAYLOAD = (HALO * CH + CH // 2, MAIN)
PIX = 144
HID = 256
TROWS = 408
FOLD_REST = COLS + 2 * HALO - MAIN
CHUNK = 3
F32, BF16 = jnp.float32, jnp.bfloat16
VMEM = pl.BlockSpec(memory_space=pltpu.VMEM)
HBM = pl.BlockSpec(memory_space=pltpu.HBM)
SMEM = pl.BlockSpec(memory_space=pltpu.SMEM)


def dot_nt(a, b):
    return lax.dot_general(a, b, (((1,), (1,)), ((), ())), preferred_element_type=F32)


def gelu(x):
    inner = x * (0.7978845608028654 + 0.035677408136300125 * (x * x))
    half = 0.5 * x
    return half + half * jnp.tanh(inner)


def cost(us):
    return pl.CostEstimate(flops=int(us * 1e9), bytes_accessed=int(us * 3e6), transcendentals=0)


def call(kernel, ins, operands, outs, scratch, us, mib):
    return pl.pallas_call(
        kernel,
        out_shape=tuple(jax.ShapeDtypeStruct(shape, BF16) for shape in outs),
        in_specs=ins,
        out_specs=(VMEM,) * len(outs),
        scratch_shapes=scratch,
        cost_estimate=cost(us),
        compiler_params=pltpu.CompilerParams(vmem_limit_bytes=mib * 2**20),
    )(*operands)


def masked_row(state_ref, mask_ref, r):
    cover = mask_ref[r].astype(F32)
    row = state_ref[r].astype(F32) * jnp.concatenate([cover] * VARS, axis=0)
    row = jnp.concatenate([row, jnp.zeros((CHANNELS, LANES - COLS), F32)], axis=1)
    return jnp.concatenate([row, jnp.zeros((CH - CHANNELS, LANES), F32)], axis=0)


def tail_out(tail):
    return jnp.concatenate([tail[: CH // 2], tail[CH // 2 :]], axis=1).astype(BF16)


def tail_in(payload_ref):
    low = payload_ref[HALO * CH :, :]
    return jnp.concatenate([low[:, :128], low[:, 128:]], axis=0).astype(F32)


def edge_kernel(state_hbm, mask_hbm, east_ref, west_ref, high_ref, state_ref, mask_ref, sems):
    copies = []
    for i in range(ROWS // CHUNK):
        rows = pl.ds(i * CHUNK, CHUNK)
        for j, (hbm, ref) in enumerate(((mask_hbm, mask_ref), (state_hbm, state_ref))):
            copies.append(pltpu.make_async_copy(hbm.at[rows], ref.at[rows], sems.at[j, i]))
            copies[-1].start()
    low, high = [], []
    for r in range(ROWS):
        if r % CHUNK == 0:
            for copy in copies[2 * (r // CHUNK) : 2 * (r // CHUNK) + 2]:
                copy.wait()
        for held, columns in ((low, slice(0, HALO)), (high, slice(COLS - HALO, COLS))):
            cover = mask_ref[r, :, columns].astype(F32)
            masked = state_ref[r, :, columns].astype(F32) * jnp.concatenate([cover] * VARS, axis=0)
            held.append(jnp.concatenate([masked, jnp.zeros((CH - CHANNELS, HALO), F32)], axis=0))
        k = r - (ROWS - HALO)
        if k >= 0:
            high_ref[k * CH : (k + 1) * CH, :] = masked_row(state_ref, mask_ref, r).astype(BF16)
    rest = [jnp.zeros((CH, 128 - ROWS * HALO), F32)]
    west_ref[...] = jnp.concatenate(low + rest, axis=1).astype(BF16)
    east_ref[...] = jnp.concatenate(high + rest, axis=1).astype(BF16)


def fill_payload(rows_ref, west_ref, east_ref, ref, north):
    lane = lax.broadcasted_iota(jnp.int32, (CH, 128), 1)
    sides = []
    for side, edge_ref in enumerate((west_ref, east_ref)):
        begin = HALO * (REST + side * HALO)
        edge = edge_ref[...].astype(F32)
        rolled = [pltpu.roll(edge, (begin - first * HALO) % 128, 1) for first in (0, ROWS - HALO)]
        inside = jnp.logical_and(lane >= begin, lane < begin + HALO * HALO)
        sides.append(jnp.where(inside, jnp.where(north == 1, rolled[1], rolled[0]), 0.0))
    rest = []
    for k in range(HALO):
        row = rows_ref[(ROWS - HALO) * north + k]
        ref[k * CH : (k + 1) * CH, :] = row[:, :MAIN]
        rest.append(row[:, MAIN:COLS].astype(F32))
    tail = jnp.concatenate(rest + [jnp.zeros((CH, 128 - HALO * REST), F32)], axis=1)
    ref[HALO * CH :, :] = tail_out(tail + sides[0] + sides[1])


def payload_kernel(seam_ref, rows_ref, west_ref, east_ref, high_ref, mate_ref, pay_ref, kept_ref):
    lat, lon = lax.axis_index("lat"), lax.axis_index("lon")
    top = lat == lax.axis_size("lat") - 1

    @pl.when(top)
    def _():
        fill_fold(seam_ref, high_ref, mate_ref, lax.bitwise_xor(lon, 2), pay_ref)
        fill_fold(seam_ref, high_ref, mate_ref, lon, kept_ref)

    @pl.when(jnp.logical_not(top))
    def _():
        fill_payload(rows_ref, west_ref, east_ref, pay_ref, lax.rem(lat, 2))


def pack_kernel(rows_ref, west_ref, east_ref, in_ref, packed_ref, pay_ref, f_ref, t_refs, edge_ref):
    fill_payload(rows_ref, west_ref, east_ref, pay_ref, 1 - lax.rem(lax.axis_index("lat"), 2))
    edge_ref[0] = flip(west_ref[...].astype(F32))
    edge_ref[1] = flip(east_ref[...].astype(F32))

    for r in range(ROWS):
        t_ref, edge = t_refs.at[r % 2], slice(r * HALO, (r + 1) * HALO)
        t_ref[8 : 8 + LANES, :] = flip(rows_ref[r].astype(F32))
        t_ref[8 - HALO : 8, :] = edge_ref[0, edge, :]
        t_ref[8 + COLS : 8 + COLS + HALO, :] = edge_ref[1, edge, :]
        pack(t_ref, packed_ref, r)
    first_rows(packed_ref, HALO, f_ref, F_FIRST, in_ref, F_FIRST, F_ROWS, straight)


def fill_fold(seam_ref, high_ref, mate_ref, target, ref):
    n_lon = lax.axis_size("lon")
    lon = lax.axis_index("lon")
    circle = n_lon * COLS
    held = jnp.concatenate([high_ref[...], mate_ref[...]], axis=1)
    spot = lax.broadcasted_iota(jnp.int32, (2 * LANES, LANES), 0)
    place = spot + jnp.where(spot < LANES, lon * COLS, lax.bitwise_xor(lon, 1) * COLS - LANES)
    column = lax.broadcasted_iota(jnp.int32, (2 * LANES, LANES), 1) - HALO + target * COLS
    source = lax.rem(seam_ref[0] - column + 3 * circle, circle)
    hot = jnp.where(place == source, 1.0, 0.0).astype(BF16)
    rows = jnp.dot(held, hot, preferred_element_type=F32)
    ref[: HALO * CH, :] = rows[:, :MAIN].astype(BF16)
    lane = lax.broadcasted_iota(jnp.int32, (CH, 128), 1)
    tail = jnp.zeros((CH, 128), F32)
    for k in range(HALO):
        shift = FOLD_REST * k
        rolled = pltpu.roll(rows[k * CH : (k + 1) * CH, MAIN:], shift, 1)
        tail += jnp.where(jnp.logical_and(lane >= shift, lane < shift + FOLD_REST), rolled, 0.0)
    ref[HALO * CH :, :] = tail_out(tail)


def ready_kernel(after_ref, state_ref, mask_ref, w_in, w_down, w_mid, w_up, w_out, rows_ref, *padded):
    for r in range(ROWS):
        rows_ref[r] = masked_row(state_ref, mask_ref, r).astype(BF16)
    weight_kernel(w_in, w_down, w_mid, w_up, w_out, *padded)


def weight_kernel(w_in, w_down, w_mid, w_up, w_out, in_ref, down_ref, mid_ref, up_ref, out_ref):
    for ref in (in_ref, down_ref, mid_ref, up_ref, out_ref):
        ref[...] = jnp.zeros(ref.shape, BF16)
    for raw, ref in ((w_in, in_ref), (w_down, down_ref), (w_mid, mid_ref), (w_up, up_ref)):
        for t in range(raw.shape[0]):
            ref[t, : raw.shape[1], :HIDDEN] = raw[t]
    for a in range(3):
        for b in range(3):
            for r in range(3):
                t = 3 * (a + r) + b
                out_ref[r * CH : r * CH + CHANNELS, t * HID : t * HID + HIDDEN] = w_out[3 * a + b]


def flip(block):
    n = block.shape[1]
    return jnp.concatenate([block, jnp.zeros((128 - CH, n), F32)], axis=0).T


def pack(t_ref, a_ref, ai):
    lane = lax.broadcasted_iota(jnp.int32, (PIX, 128), 1)
    odd_left, even, odd, even_right = (t_ref[pl.ds(3 + s, PIX, stride=2), :] for s in range(4))
    even80, odd80 = pltpu.roll(even, CH, 1), pltpu.roll(odd, CH, 1)
    for p, (left, mid, right) in enumerate(((odd_left, even80, odd), (even, odd80, even_right))):
        low = jnp.where(lane < CH, left, mid)
        high = jnp.where(lane < 2 * CH - 128, mid, pltpu.roll(right, 2 * CH - 128, 1))
        a_ref[ai, p * PIX : (p + 1) * PIX, :] = jnp.concatenate([low, high], axis=1).astype(BF16)


def straight(t, n):
    return t


def first_rows(a_ref, begin, f_ref, f_begin, w_ref, fr, n, tap):
    w = []
    for a in range(3):
        w += [w_ref[tap(3 * a + b, 9)] for b in range(3)] + [jnp.zeros((HID - 3 * CH, HID), BF16)]
    w = jnp.concatenate(w, axis=0)
    for q in range(n):
        taps = jnp.concatenate([a_ref[fr + q + a - begin] for a in range(3)], axis=1)
        f_ref[fr + q - f_begin] = gelu(jnp.dot(taps, w, preferred_element_type=F32)).astype(BF16)


def coarse_rows(f_ref, f_begin, c_ref, w_ref, ci, n, tap, held):
    w = jnp.concatenate([w_ref[tap(t, 4)] for t in range(4)], axis=1)
    pieces = []
    for q in range(n):
        piece = [f_ref[2 * (ci + q) + a - f_begin, b * PIX : (b + 1) * PIX, :] for a in range(2) for b in range(2)]
        pieces.append(jnp.concatenate(piece, axis=1))
    coarse = gelu(dot_nt(jnp.concatenate(pieces, axis=0), w))
    if held is not None:
        coarse = coarse * held
    for q in range(n):
        one = coarse[q * PIX : (q + 1) * PIX]
        planes = [pltpu.roll(one, 1, 0), one, pltpu.roll(one, PIX - 1, 0)]
        c_ref[ci + q] = jnp.concatenate(planes, axis=1).astype(BF16)


def mid_rows(c_ref, f_ref, f_begin, j_ref, mid_ref, up_ref, mi, n, tap, held):
    taps = [c_ref[pl.ds(mi + a, n)].reshape(n * PIX, 3 * HID) for a in range(3)]
    w = jnp.concatenate([mid_ref[tap(t, 9)] for t in range(9)], axis=1)
    middle = gelu(dot_nt(jnp.concatenate(taps, axis=1), w)).astype(BF16)
    for a in range(2):
        grown = [dot_nt(middle, up_ref[tap(2 * a + b, 4)]) for b in range(2)]
        for q in range(n):
            row = 2 * (mi + q) + a
            halves = []
            for b in range(2):
                first = f_ref[row + 2 - f_begin, b * PIX : (b + 1) * PIX, :].astype(F32)
                half = gelu(grown[b][q * PIX : (q + 1) * PIX]) + first
                halves.append(half * held if held is not None and q == 0 else half)
            even, odd = halves
            planes = (pltpu.roll(odd, 1, 0), even, odd, pltpu.roll(even, PIX - 1, 0))
            for s, plane in enumerate(planes):
                j_ref[row, s * PIX : (s + 1) * PIX, :] = plane.astype(BF16)


F_FIRST, F_ROWS = 5, 10
C_KEPT = (3, 4, 5, 6)
J_KEPT = (6, 7, 8, 9)
KEPT = (C_KEPT, J_KEPT)
PACKED = (2 * PIX, HID)
BLOCKS = ((PIX, 3 * HID), (4 * PIX, HID))
HELD = [pltpu.VMEM((n,) + block, BF16) for n, block in zip((10, 16), BLOCKS)]


def inner_kernel(f_ref, down_ref, mid_ref, up_ref, *refs):
    outs, (c_ref, j_ref) = refs[:2], refs[2:]
    coarse_rows(f_ref, F_FIRST, c_ref, down_ref, 3, 4, straight, None)
    mid_rows(c_ref, f_ref, F_FIRST, j_ref, mid_ref, up_ref, 3, 2, straight, None)
    for ref, out_ref, kept in zip((c_ref, j_ref), outs, KEPT):
        for i, row in enumerate(kept):
            out_ref[i] = ref[row]


def outer_kernel(second, *refs):
    got_ref, refs = refs[0], refs[1:]
    if second:
        half_ref, refs = refs[0], refs[1:]
    else:
        kept_ref, refs = refs[0], refs[1:]
    in_ref, down_ref, mid_ref, up_ref, w_out_ref, state_ref, mask_ref, packed_ref, f_in, c_in, j_in, out_ref = refs[:12]
    t_refs, edge_ref, a_ref, f_ref, c_ref, j_ref, u_ref = refs[12:]
    lat = lax.axis_index("lat")
    bottom, top = lat == 0, lat == lax.axis_size("lat") - 1

    def side(north):
        for q in range(2):
            a_ref[5 + 10 * north + q] = packed_ref[10 * north + q]
            c_ref[3 + 2 * north + q] = c_in[2 * north + q]
        for q in range(3):
            f_ref[5 + 7 * north + q] = f_in[7 * north + q]
            j_ref[6 + north + q] = j_in[north + q]
        edge_ref[0] = flip(tail_in(got_ref))
        t_refs[...] = jnp.zeros(t_refs.shape, F32)
        for k in range(HALO):
            t_ref = t_refs.at[k % 2]
            t_ref[8 : 8 + MAIN, :] = flip(got_ref[k * CH : (k + 1) * CH, :].astype(F32))
            for begin, at, n in ((0, MAIN, REST), (HALO * REST, -HALO, HALO), (HALO * (REST + HALO), COLS, HALO)):
                t_ref[8 + at : 8 + at + n, :] = edge_ref[0, begin + k * n : begin + (k + 1) * n, :]
            pack(t_ref, a_ref, (ROWS + HALO) * north + k)

        if not second and not north:

            @pl.when(bottom)
            def _():
                a_ref[0:HALO] = jnp.zeros((HALO,) + PACKED, BF16)

        if not second and north:
            @pl.when(top)
            def _():
                edge_ref[0] = flip(tail_in(got_ref) + tail_in(kept_ref))
                for k in range(HALO):
                    kk = HALO - 1 - k
                    rows = slice(kk * CH, (kk + 1) * CH)
                    t_ref = t_refs.at[k % 2]
                    t_ref[8 - HALO : 8 - HALO + MAIN, :] = flip(got_ref[rows, :].astype(F32) + kept_ref[rows, :].astype(F32))
                    rest = edge_ref[0, FOLD_REST * kk : FOLD_REST * (kk + 1), :]
                    t_ref[8 - HALO + MAIN : 8 + COLS + HALO, :] = rest
                    pack(t_ref, a_ref, ROWS + HALO + k)

        keep, turn = None, straight
        if not second and north:
            turn = lambda t, n: jnp.where(top, n - 1 - t, t)
        elif not second:
            keep = jnp.where(bottom, 0.0, 1.0).astype(F32)
        first_rows(a_ref, 0, f_ref, 0, in_ref, 4 + 11 * north, 1, straight)
        first_rows(a_ref, 0, f_ref, 0, in_ref, 16 * north, 4, turn)
        coarse_rows(f_ref, 0, c_ref, down_ref, 8 * north, 2, turn, keep)
        coarse_rows(f_ref, 0, c_ref, down_ref, 2 + 5 * north, 1, straight, None)
        mid_rows(c_ref, f_ref, 0, j_ref, mid_ref, up_ref, 5 * north, 3, straight, keep)

        if not second and north:

            @pl.when(top)
            def _():
                mid_rows(c_ref, f_ref, 0, j_ref, mid_ref, up_ref, 7, 1, lambda t, n: n - 1 - t, None)

        groups = []
        for q in range(2):
            taps = [j_ref[6 * north + 3 * q + 1 + i, b * PIX : (b + 2) * PIX, :] for i in range(5) for b in range(3)]
            groups.append(jnp.concatenate(taps, axis=1))
        deltas = dot_nt(jnp.concatenate(groups, axis=0), w_out_ref[...])
        for q in range(2):
            flipped = []
            for t in range(2):
                for p in range(2):
                    begin = (2 * q + p) * PIX
                    half = deltas[begin : begin + PIX, t * 128 : (t + 1) * 128]
                    u_ref[pl.ds((2 * q + t) * TROWS + 4 + p, PIX, stride=2), :] = half
                begin = (2 * q + t) * TROWS + 8
                flipped.append(u_ref[begin : begin + LANES, :].T)
            flipped = jnp.concatenate(flipped, axis=0)
            for i in range(3):
                r = 6 * north + 3 * q + i
                delta = flipped[i * CH : i * CH + CHANNELS, :COLS]
                cover = jnp.concatenate([mask_ref[r].astype(F32)] * VARS, axis=0)
                out = ((state_ref[r].astype(F32) + delta) * cover).astype(BF16)
                out_ref[r if second else 3 * q + i] = out
        if second:
            for q in range(6):
                out_ref[6 * (1 - north) + q] = half_ref[q]

    for north in range(2):
        pl.when(lax.rem(lat, 2) == (1 - north if second else north))(functools.partial(side, north))


def body(state, sea_mask, seam, w_in, w_down, w_mid, w_up, w_out):
    n_lat, n_lon = lax.axis_size("lat"), lax.axis_size("lon")
    ring = lambda n, d: [(i, (i + d) % n) for i in range(n)]
    state, sea_mask = jnp.swapaxes(state, 0, 1), jnp.swapaxes(sea_mask, 0, 1)
    flat = lambda w: w.reshape((-1,) + w.shape[2:])
    edge = (CH, 128)
    east_going, west_going, high = call(
        edge_kernel, [HBM] * 2, (state, sea_mask), [edge, edge, (HALO * CH, LANES)],
        [
            pltpu.VMEM((ROWS, CHANNELS, COLS), BF16),
            pltpu.VMEM((ROWS, LEVELS, COLS), jnp.int32),
            pltpu.SemaphoreType.DMA((2, ROWS // CHUNK)),
        ],
        1, 60,
    )
    west = lax.ppermute(east_going, "lon", ring(n_lon, 1))
    east = lax.ppermute(west_going, "lon", ring(n_lon, -1))

    axes = ("lat", "lon")
    within = [(i, i ^ 1) for i in range(n_lat * n_lon)]

    def swap(begin):
        pairs = []
        for i in range(n_lat):
            for j in range(n_lon):
                mate = i + 1 if (i - begin) % 2 == 0 else i - 1
                target = mate * n_lon + j if 0 <= mate < n_lat else i * n_lon + (j ^ 2)
                pairs.append((i * n_lon + j, target))
        return pairs

    mate = lax.ppermute(high, axes, within)
    rows, *laid = call(
        ready_kernel, [VMEM] * 8,
        (west_going, state, sea_mask, flat(jnp.swapaxes(w_in, 2, 3)), flat(w_down), flat(w_mid), flat(w_up), flat(w_out)),
        [
            (ROWS, CH, LANES),
            (9, CH, HID), (4, HID, HID), (9, HID, HID), (4, HID, HID), (HID, 15 * HID),
        ],
        [], 1.5, 16,
    )
    pay, kept = call(
        payload_kernel, [SMEM] + [VMEM] * 5, (seam, rows, west, east, high, mate), [PAYLOAD] * 2, [], 0.4, 8,
    )
    got = lax.ppermute(pay, axes, swap(1))
    turning = [pltpu.VMEM((2, TROWS, 128), F32), pltpu.VMEM((2, 128, 128), F32)]
    packed, pay, f_own = call(
        pack_kernel, [VMEM] * 4, (rows, west, east, laid[0]),
        [(ROWS,) + PACKED, PAYLOAD, (F_ROWS,) + PACKED], turning, 3.5, 18,
    )
    got_later = lax.ppermute(pay, axes, swap(0))
    handed = [(len(k),) + block for k, block in zip(KEPT, BLOCKS)]
    inner = call(inner_kernel, [VMEM] * 4, (f_own, *laid[1:4]), handed, HELD, 1.7, 24)
    scratch = turning + [pltpu.VMEM((n,) + PACKED, BF16) for n in (22, 20)] + HELD + [pltpu.VMEM((4 * TROWS, 128), F32)]
    shared = (*laid, state, sea_mask, packed, f_own, *inner)
    (half,) = call(
        functools.partial(outer_kernel, False), [VMEM] * 13, (got, kept, *shared), [(ROWS // 2, CHANNELS, COLS)],
        scratch, 5, 30,
    )
    (out,) = call(
        functools.partial(outer_kernel, True), [VMEM] * 13, (got_later, half, *shared), [(ROWS, CHANNELS, COLS)],
        scratch, 6, 30,
    )
    return jnp.swapaxes(out, 0, 1)


def solution(mesh):
    return jax.shard_map(
        body,
        mesh=mesh,
        in_specs=(P(None, "lat", "lon"), P(None, "lat", "lon"), P(), P(), P(), P(), P(), P()),
        out_specs=P(None, "lat", "lon"),
        check_vma=False,
    )
```

time: 43.3 us -> 34.7 us (0.80)
  the two profiles are of different devices: /device:TPU:255 before, /device:TPU:7 now
where the time goes in v3:
time: 34.7 us; the launch traced here: 34.5 us
  Pallas kernels  20.3 us (59%)
  starting transfers between devices  10.4 us (30%)
  waiting for transfers between devices  2.9 us (8%)
  local copies, waits for them, and re-layouts  0.76 us (2%)
    pallas_call x7, Pallas kernels, call(): pl.pallas_call(kernel, out_shape=tuple((jax.ShapeDtypeStruct(shape, BF16)...  20.3 us
    ppermute x1, starting transfers between devices, body(): got = lax.ppermute(pay, axes, swap(1))  8.26 us
    ppermute x1, waiting for transfers between devices, body(): east = lax.ppermute(west_going, 'lon', ring(n_lon, -1))  1.79 us
    ppermute x1, starting transfers between devices, body(): west = lax.ppermute(east_going, 'lon', ring(n_lon, 1))  1.27 us
    ppermute x1, waiting for transfers between devices, body(): got_later = lax.ppermute(pay, axes, swap(0))  1 us
    ppermute x1, starting transfers between devices, body(): mate = lax.ppermute(high, axes, within)  0.76 us
    unnamed x20, local copies, waits for them, and re-layouts  0.76 us
  transfers between devices with their start and end apart: 5, of which 3 were waited for; matrix products, arithmetic and copies ran while one was open for 0% of the time, Pallas kernels for 33%

profile of v3, /device:TPU:7, one launch (start us, length us, event | category | flops | bytes accessed | tf_op | source)
XLA Modules:
  0.0 34.5 jit_solution(17559894753461018275)
XLA Ops:
  0.0 0.0 copy-start
  0.0 0.0 copy-start.1
  0.0 0.0 copy-start.2
  0.0 0.0 copy-start.3
  0.0 0.0 copy-start.4
  0.0 0.0 copy-start.5
  0.0 0.0 copy-start.6
  0.0 2.4 %shard_map.82 = (bf16[80,128]{1,0:T(8,128)(2,1)}, bf16[80,128]{1,0:T(8,128)(2,1)}, bf16[400,384]{1,0:T(8,128)(2,1)}) custom-call(bf16[12,76,270]{2,1,0:T(8,128)(2,1)} %bitcast.11, s32[12,19,270]{2,1,0:T(8,128)} %bitcast.15), custom_call_target="tpu_custom_call" | custom-call | flops 1000000000 | bytes 3000000 | tf_op jit(solution)/shard_map/pallas_call | solution.py:44
  2.5 0.8 %collective-permute-start.3 = (bf16[400,384]{1,0:T(8,128)(2,1)}, bf16[400,384]{1,0:T(8,128)(2,1)S(1)}, u32[]{:S(2)}, u32[]{:S(2)}) collective-permute-start(bf16[400,384]{1,0:T(8,128)(2,1)} %get-tuple-element.26.high_ref), channel_id=1, source_target_pairs={{0,1},{1,0},{2,3},{3,2},{4,5},{5,4},{6,7},{7,6},{8,9},{9,8},{10,11... | collective-permute-start | bytes 921608 | tf_op jit(solution)/shard_map/ppermute | solution.py:384
  3.2 1.3 %collective-permute-start = (bf16[80,128]{1,0:T(8,128)(2,1)}, bf16[80,128]{1,0:T(8,128)(2,1)S(1)}, u32[]{:S(2)}, u32[]{:S(2)}) collective-permute-start(bf16[80,128]{1,0:T(8,128)(2,1)} %get-tuple-element.23), channel_id=1, source_target_pairs={{0,1},{1,2},{2,3},{3,0},{4,5},{5,6},{6,7},{7,4},{8,9},{9,10},{10,1... | collective-permute-start | bytes 61448 | tf_op jit(solution)/shard_map/ppermute | solution.py:369
  4.5 0.0 collective-permute-start.1
  4.5 0.0 copy-done
  4.5 0.0 copy-done.1
  4.5 0.0 copy-done.2
  4.5 0.0 copy-done.3
  4.5 0.0 copy-done.4
  4.5 0.0 copy-done.5
  4.5 0.0 copy-done.6
  4.6 0.0 copy-start.8
  4.6 0.7 %copy-done.8 = bf16[80,128]{1,0:T(8,128)(2,1)S(1)} copy-done((bf16[80,128]{1,0:T(8,128)(2,1)S(1)}, bf16[80,128]{1,0:T(8,128)(2,1)}, u32[]{:S(2)}) %copy-start.8) | copy-done | bytes 20504
  5.3 0.0 copy-start.7
  5.3 0.0 copy-start.9
  5.3 0.8 %shard_map.83 = (bf16[12,80,384]{2,1,0:T(8,128)(2,1)S(1)}, bf16[9,80,256]{2,1,0:T(8,128)(2,1)S(1)}, bf16[4,256,256]{2,1,0:T(8,128)(2,1)S(1)}, bf16[9,256,256]{2,...) custom-call(bf16[80,128]{1,0:T(8,128)(2,1)S(1)} %copy-done.8, ...), custom_call_target="tpu_custom_call" | custom-call | flops 1500000000 | bytes 4500000 | tf_op jit(solution)/shard_map/pallas_call | solution.py:44
  6.1 0.0 collective-permute-done.west_ref
  6.1 1.8 %collective-permute-done.1.east_ref = bf16[80,128]{1,0:T(8,128)(2,1)S(1)} collective-permute-done((bf16[80,128]{1,0:T(8,128)(2,1)}, bf16[80,128]{1,0:T(8,128)(2,1)S(1)}, u32[]{:S(2)}, u32[]{:S(2)}) %collective-permute-start.1) | collective-permute-done | bytes 20512 | tf_op jit(solution)/shard_map/ppermute | solution.py:370
  7.9 0.0 collective-permute-done.3.mate_ref
  7.9 0.0 copy-done.7
  7.9 0.0 copy-done.9
  7.9 0.7 %shard_map.85 = (bf16[440,256]{1,0:T(8,128)(2,1)S(1)}, bf16[440,256]{1,0:T(8,128)(2,1)S(1)}) custom-call(s32[1080]{0:T(1024)S(1)} %copy-done.9, bf16[12,80,384]{2,1,0:T(8,128)(2,1)S(1)} %get-tuple-element.22.rows_ref, bf16[80,128]{1,0:T(8,128)(2,1)S(1)} %collective-permute-done.west_ref, bf16[80,128]{1,0:T(8,128)(2,1)S(1)} %collective-permute-done.1.east_ref, ...), custom_call_target="tpu_custom_call" | custom-call | flops 400000000 | bytes 1200000 | tf_op jit(solution)/shard_map/pallas_call | solution.py:44
  8.7 8.3 %collective-permute-start.4 = (bf16[440,256]{1,0:T(8,128)(2,1)S(1)}, bf16[440,256]{1,0:T(8,128)(2,1)S(1)}, u32[]{:S(2)}, u32[]{:S(2)}) collective-permute-start(bf16[440,256]{1,0:T(8,128)(2,1)S(1)} %get-tuple-element.27), channel_id=1, source_target_pairs={{0,2},{1,3},{2,0},{3,1},{4,8},{5,9},{6,10},{7,11},{8,4},{9,5},{10,... | collective-permute-start | bytes 675848 | tf_op jit(solution)/shard_map/ppermute | solution.py:397
  16.9 2.8 %shard_map.84 = (bf16[12,288,256]{2,1,0:T(8,128)(2,1)S(1)}, bf16[440,256]{1,0:T(8,128)(2,1)S(1)}, bf16[10,288,256]{2,1,0:T(8,128)(2,1)S(1)}) custom-call(bf16[12,80,384]{2,1,0:T(8,128)(2,1)S(1)} %get-tuple-element.22.rows_ref, bf16[80,128]{1,0:T(8,128)(2,1)S(1)} %collective-permute-done.west_ref, bf16[80,128]{1,0:T(8,128)(2,1)S(1)} %collective-permute-done.1.east_ref, ...), custom_call_target="tpu_custom_call" | custom-call | flops 3500000000 | bytes 10500000 | tf_op jit(solution)/shard_map/pallas_call | solution.py:44
  19.7 0.1 collective-permute-start.2
  19.8 2.2 %shard_map.86 = (bf16[4,144,768]{2,1,0:T(8,128)(2,1)S(1)}, bf16[4,576,256]{2,1,0:T(8,128)(2,1)S(1)}) custom-call(bf16[10,288,256]{2,1,0:T(8,128)(2,1)S(1)} %get-tuple-element.34.f_ref.refs_10_, bf16[4,256,256]{2,1,0:T(8,128)(2,1)S(1)} %get-tuple-element.29.down_ref.refs_3_, bf16[9,256,256]{2,1,0:T(8,128)(2,1)S(1)} %get-tuple-element.30.mid_ref.refs_4_, ...), custom_call_target="tpu_custom_call" | custom-call | flops 1700000000 | bytes 5100000 | tf_op jit(solution)/shard_map/pallas_call | solution.py:44
  22.0 0.1 collective-permute-done.4.refs_0_
  22.1 5.6 %shard_map.87.refs_1_ = bf16[6,76,270]{2,1,0:T(8,128)(2,1)S(1)} custom-call(bf16[440,256]{1,0:T(8,128)(2,1)S(1)} %collective-permute-done.4.refs_0_, bf16[440,256]{1,0:T(8,128)(2,1)S(1)} %get-tuple-element.28.refs_1_, bf16[9,80,256]{2,1,0:T(8,128)(2,1)S(1)} %get-tuple-element.24.in_ref.refs_2_, bf16[4,256,256]{2,1,0:T(8,128)(2,1)S(1)} %get-tuple-element.29.down_ref.refs_3_, ...), custom_call_target="tpu_custom_call" | custom-call | flops 5000000000 | bytes 15000000 | tf_op jit(solution)/shard_map/pallas_call | solution.py:44
  27.7 1.0 %collective-permute-done.2.refs_0_ = bf16[440,256]{1,0:T(8,128)(2,1)S(1)} collective-permute-done((bf16[440,256]{1,0:T(8,128)(2,1)S(1)}, bf16[440,256]{1,0:T(8,128)(2,1)S(1)}, u32[]{:S(2)}, u32[]{:S(2)}) %collective-permute-start.2) | collective-permute-done | bytes 225312 | tf_op jit(solution)/shard_map/ppermute | solution.py:403
  28.7 5.8 %shard_map.88 = bf16[12,76,270]{2,1,0:T(8,128)(2,1)} custom-call(bf16[440,256]{1,0:T(8,128)(2,1)S(1)} %collective-permute-done.2.refs_0_, bf16[6,76,270]{2,1,0:T(8,128)(2,1)S(1)} %shard_map.87.refs_1_, bf16[9,80,256]{2,1,0:T(8,128)(2,1)S(1)} %get-tuple-element.24.in_ref.refs_2_, bf16[4,256,256]{2,1,0:T(8,128)(2,1)S(1)} %get-tuple-element.29.down_ref.refs_3_, ...), custom_call_target="tpu_custom_call" | custom-call | flops 6000000000 | bytes 18000000 | tf_op jit(solution)/shard_map/pallas_call | solution.py:44
Async XLA Ops:
  0.0 4.5 %copy-start = (bf16[3,3,200,200]{3,2,1,0:T(8,128)(2,1)S(1)}, bf16[3,3,200,200]{3,2,1,0:T(8,128)(2,1)}, u32[]{:S(2)}) copy-start(bf16[3,3,200,200]{3,2,1,0:T(8,128)(2,1)} %param.13) | copy-start | bytes 2160004
  0.0 4.5 %copy-start.1 = (bf16[76,12,270]{2,0,1:T(8,128)(2,1)S(1)}, bf16[76,12,270]{2,0,1:T(8,128)(2,1)}, u32[]{:S(2)}) copy-start(bf16[76,12,270]{2,0,1:T(8,128)(2,1)} %param.8) | copy-start | bytes 1477444
  0.0 4.5 %copy-start.2 = (s32[19,12,270]{2,0,1:T(8,128)S(1)}, s32[19,12,270]{2,0,1:T(8,128)}, u32[]{:S(2)}) copy-start(s32[19,12,270]{2,0,1:T(8,128)} %param.9) | copy-start | bytes 738724
  0.0 4.5 %copy-start.3 = (bf16[2,2,200,200]{3,2,1,0:T(8,128)(2,1)S(1)}, bf16[2,2,200,200]{3,2,1,0:T(8,128)(2,1)}, u32[]{:S(2)}) copy-start(bf16[2,2,200,200]{3,2,1,0:T(8,128)(2,1)} %param.12) | copy-start | bytes 960004
  0.0 4.5 %copy-start.4 = (bf16[2,2,200,200]{3,2,1,0:T(8,128)(2,1)S(1)}, bf16[2,2,200,200]{3,2,1,0:T(8,128)(2,1)}, u32[]{:S(2)}) copy-start(bf16[2,2,200,200]{3,2,1,0:T(8,128)(2,1)} %param.14) | copy-start | bytes 960004
  0.0 4.5 %copy-start.5 = (bf16[3,3,200,76]{2,3,1,0:T(8,128)(2,1)S(1)}, bf16[3,3,200,76]{2,3,1,0:T(8,128)(2,1)}, u32[]{:S(2)}) copy-start(bf16[3,3,200,76]{2,3,1,0:T(8,128)(2,1)} %param.11) | copy-start | bytes 820804
  0.0 4.5 %copy-start.6 = (bf16[3,3,76,200]{3,2,1,0:T(8,128)(2,1)S(1)}, bf16[3,3,76,200]{3,2,1,0:T(8,128)(2,1)}, u32[]{:S(2)}) copy-start(bf16[3,3,76,200]{3,2,1,0:T(8,128)(2,1)} %param.15) | copy-start | bytes 820804
  2.5 5.5 %collective-permute-start.3 = (bf16[400,384]{1,0:T(8,128)(2,1)}, bf16[400,384]{1,0:T(8,128)(2,1)S(1)}, u32[]{:S(2)}, u32[]{:S(2)}) collective-permute-start(bf16[400,384]{1,0:T(8,128)(2,1)} %get-tuple-element.26.high_ref), channel_id=1, source_target_pairs={{0,1},{1,0},{2,3},{3,2},{4,5},{5,4},{6,7},{7,6},{8,9},{9,8},{10,11... | collective-permute-start | bytes 921608 | tf_op jit(solution)/shard_map/ppermute | solution.py:384
  3.2 2.9 %collective-permute-start = (bf16[80,128]{1,0:T(8,128)(2,1)}, bf16[80,128]{1,0:T(8,128)(2,1)S(1)}, u32[]{:S(2)}, u32[]{:S(2)}) collective-permute-start(bf16[80,128]{1,0:T(8,128)(2,1)} %get-tuple-element.23), channel_id=1, source_target_pairs={{0,1},{1,2},{2,3},{3,0},{4,5},{5,6},{6,7},{7,4},{8,9},{9,10},{10,1... | collective-permute-start | bytes 61448 | tf_op jit(solution)/shard_map/ppermute | solution.py:369
  4.5 3.4 %collective-permute-start.1 = (bf16[80,128]{1,0:T(8,128)(2,1)}, bf16[80,128]{1,0:T(8,128)(2,1)S(1)}, u32[]{:S(2)}, u32[]{:S(2)}) collective-permute-start(bf16[80,128]{1,0:T(8,128)(2,1)} %get-tuple-element.21.after_ref), channel_id=1, source_target_pairs={{0,3},{1,0},{2,1},{3,2},{4,7},{5,4},{6,5},{7,6},{8,11},{9,8},{10,9... | collective-permute-start | bytes 61448 | tf_op jit(solution)/shard_map/ppermute | solution.py:370
  4.6 0.7 %copy-start.8 = (bf16[80,128]{1,0:T(8,128)(2,1)S(1)}, bf16[80,128]{1,0:T(8,128)(2,1)}, u32[]{:S(2)}) copy-start(bf16[80,128]{1,0:T(8,128)(2,1)} %get-tuple-element.21.after_ref) | copy-start | bytes 61444
  5.3 2.6 %copy-start.7 = (bf16[400,384]{1,0:T(8,128)(2,1)S(1)}, bf16[400,384]{1,0:T(8,128)(2,1)}, u32[]{:S(2)}) copy-start(bf16[400,384]{1,0:T(8,128)(2,1)} %get-tuple-element.26.high_ref) | copy-start | bytes 921604
  5.3 2.6 %copy-start.9 = (s32[1080]{0:T(1024)S(1)}, s32[1080]{0:T(1024)}, u32[]{:S(2)}) copy-start(s32[1080]{0:T(1024)} %seam_ref.1) | copy-start | bytes 12964
  8.7 13.4 %collective-permute-start.4 = (bf16[440,256]{1,0:T(8,128)(2,1)S(1)}, bf16[440,256]{1,0:T(8,128)(2,1)S(1)}, u32[]{:S(2)}, u32[]{:S(2)}) collective-permute-start(bf16[440,256]{1,0:T(8,128)(2,1)S(1)} %get-tuple-element.27), channel_id=1, source_target_pairs={{0,2},{1,3},{2,0},{3,1},{4,8},{5,9},{6,10},{7,11},{8,4},{9,5},{10,... | collective-permute-start | bytes 675848 | tf_op jit(solution)/shard_map/ppermute | solution.py:397
  19.7 9.0 %collective-permute-start.2 = (bf16[440,256]{1,0:T(8,128)(2,1)S(1)}, bf16[440,256]{1,0:T(8,128)(2,1)S(1)}, u32[]{:S(2)}, u32[]{:S(2)}) collective-permute-start(bf16[440,256]{1,0:T(8,128)(2,1)S(1)} %get-tuple-element.25), channel_id=1, source_target_pairs={{0,4},{1,5},{2,6},{3,7},{4,0},{5,1},{6,2},{7,3},{8,12},{9,13},{10,... | collective-permute-start | bytes 675848 | tf_op jit(solution)/shard_map/ppermute | solution.py:403

commit v4 on v3

--- a/solution.py
+++ b/solution.py
@@ -19,6 +19,7 @@
 HID = 256
 TROWS = 408
 FOLD_REST = COLS + 2 * HALO - MAIN
+EARLY = 16
 CHUNK = 3
 F32, BF16 = jnp.float32, jnp.bfloat16
 VMEM = pl.BlockSpec(memory_space=pltpu.VMEM)
@@ -40,12 +41,13 @@
     return pl.CostEstimate(flops=int(us * 1e9), bytes_accessed=int(us * 3e6), transcendentals=0)
 
 
-def call(kernel, ins, operands, outs, scratch, us, mib):
+def call(kernel, ins, operands, outs, scratch, us, mib, out_spec=VMEM, aliases={}):
     return pl.pallas_call(
         kernel,
-        out_shape=tuple(jax.ShapeDtypeStruct(shape, BF16) for shape in outs),
+        out_shape=tuple(jax.ShapeDtypeStruct(shape, F32 if shape == PARTS else BF16) for shape in outs),
         in_specs=ins,
-        out_specs=(VMEM,) * len(outs),
+        out_specs=(out_spec,) * len(outs),
+        input_output_aliases=aliases,
         scratch_shapes=scratch,
         cost_estimate=cost(us),
         compiler_params=pltpu.CompilerParams(vmem_limit_bytes=mib * 2**20),
@@ -110,25 +112,9 @@
     ref[HALO * CH :, :] = tail_out(tail + sides[0] + sides[1])
 
 
-def payload_kernel(seam_ref, rows_ref, west_ref, east_ref, high_ref, mate_ref, pay_ref, kept_ref):
-    lat, lon = lax.axis_index("lat"), lax.axis_index("lon")
-    top = lat == lax.axis_size("lat") - 1
-
-    @pl.when(top)
-    def _():
-        fill_fold(seam_ref, high_ref, mate_ref, lax.bitwise_xor(lon, 2), pay_ref)
-        fill_fold(seam_ref, high_ref, mate_ref, lon, kept_ref)
-
-    @pl.when(jnp.logical_not(top))
-    def _():
-        fill_payload(rows_ref, west_ref, east_ref, pay_ref, lax.rem(lat, 2))
-
-
-def pack_kernel(rows_ref, west_ref, east_ref, in_ref, packed_ref, pay_ref, f_ref, t_refs, edge_ref):
-    fill_payload(rows_ref, west_ref, east_ref, pay_ref, 1 - lax.rem(lax.axis_index("lat"), 2))
+def own_rows(rows_ref, west_ref, east_ref, in_ref, packed_ref, f_ref, t_refs, edge_ref):
     edge_ref[0] = flip(west_ref[...].astype(F32))
     edge_ref[1] = flip(east_ref[...].astype(F32))
-
     for r in range(ROWS):
         t_ref, edge = t_refs.at[r % 2], slice(r * HALO, (r + 1) * HALO)
         t_ref[8 : 8 + LANES, :] = flip(rows_ref[r].astype(F32))
@@ -136,6 +122,42 @@
         t_ref[8 + COLS : 8 + COLS + HALO, :] = edge_ref[1, edge, :]
         pack(t_ref, packed_ref, r)
     first_rows(packed_ref, HALO, f_ref, F_FIRST, in_ref, F_FIRST, F_ROWS, straight)
+
+
+def starts_early():
+    lat = lax.axis_index("lat")
+    return jnp.logical_and(lax.rem(lat, EARLY) == 0, lat > 0)
+
+
+def payload_kernel(
+    seam_ref, rows_ref, west_ref, east_ref, high_ref, mate_ref, in_ref, pay_ref, kept_ref, packed_ref, f_ref,
+    t_refs, edge_ref,
+):
+    lat, lon = lax.axis_index("lat"), lax.axis_index("lon")
+    top = lat == lax.axis_size("lat") - 1
+
+    @pl.when(top)
+    def _():
+        fill_fold(seam_ref, high_ref, mate_ref, lax.bitwise_xor(lon, 2), pay_ref)
+        fill_fold(seam_ref, high_ref, mate_ref, lon, kept_ref)
+
+    @pl.when(jnp.logical_not(top))
+    def _():
+        fill_payload(rows_ref, west_ref, east_ref, pay_ref, lax.rem(lat, 2))
+
+    @pl.when(starts_early())
+    def _():
+        own_rows(rows_ref, west_ref, east_ref, in_ref, packed_ref, f_ref, t_refs, edge_ref)
+
+
+def pack_kernel(
+    rows_ref, west_ref, east_ref, in_ref, packed_in, f_in, packed_ref, f_ref, pay_ref, t_refs, edge_ref
+):
+    fill_payload(rows_ref, west_ref, east_ref, pay_ref, 1 - lax.rem(lax.axis_index("lat"), 2))
+
+    @pl.when(jnp.logical_not(starts_early()))
+    def _():
+        own_rows(rows_ref, west_ref, east_ref, in_ref, packed_ref, f_ref, t_refs, edge_ref)
 
 
 def fill_fold(seam_ref, high_ref, mate_ref, target, ref):
@@ -242,21 +264,23 @@
 
 
 F_FIRST, F_ROWS = 5, 10
-C_KEPT = (3, 4, 5, 6)
-J_KEPT = (6, 7, 8, 9)
-KEPT = (C_KEPT, J_KEPT)
+C_FIRST, C_ROWS = 3, 4
 PACKED = (2 * PIX, HID)
-BLOCKS = ((PIX, 3 * HID), (4 * PIX, HID))
-HELD = [pltpu.VMEM((n,) + block, BF16) for n, block in zip((10, 16), BLOCKS)]
-
-
-def inner_kernel(f_ref, down_ref, mid_ref, up_ref, *refs):
-    outs, (c_ref, j_ref) = refs[:2], refs[2:]
-    coarse_rows(f_ref, F_FIRST, c_ref, down_ref, 3, 4, straight, None)
+PARTS = (2,) + PACKED
+HELD = [pltpu.VMEM((n,) + block, BF16) for n, block in zip((10, 16), ((PIX, 3 * HID), (4 * PIX, HID)))]
+
+
+def out_taps(j_ref, rows):
+    return jnp.concatenate([j_ref[r, b * PIX : (b + 2) * PIX, :] for r in rows for b in range(3)], axis=1)
+
+
+def inner_kernel(f_ref, down_ref, mid_ref, up_ref, w_out_ref, c_out, part_ref, c_ref, j_ref):
+    coarse_rows(f_ref, F_FIRST, c_ref, down_ref, C_FIRST, C_ROWS, straight, None)
     mid_rows(c_ref, f_ref, F_FIRST, j_ref, mid_ref, up_ref, 3, 2, straight, None)
-    for ref, out_ref, kept in zip((c_ref, j_ref), outs, KEPT):
-        for i, row in enumerate(kept):
-            out_ref[i] = ref[row]
+    for i in range(C_ROWS):
+        c_out[i] = c_ref[C_FIRST + i]
+    part_ref[0] = dot_nt(out_taps(j_ref, (6, 7, 8)), w_out_ref[:, 6 * HID :])
+    part_ref[1] = dot_nt(out_taps(j_ref, (7, 8, 9)), w_out_ref[:, : 9 * HID])
 
 
 def outer_kernel(second, *refs):
@@ -265,8 +289,10 @@
         half_ref, refs = refs[0], refs[1:]
     else:
         kept_ref, refs = refs[0], refs[1:]
-    in_ref, down_ref, mid_ref, up_ref, w_out_ref, state_ref, mask_ref, packed_ref, f_in, c_in, j_in, out_ref = refs[:12]
-    t_refs, edge_ref, a_ref, f_ref, c_ref, j_ref, u_ref = refs[12:]
+    in_ref, down_ref, mid_ref, up_ref, w_out_ref, state_ref, mask_ref, packed_ref, f_in, c_in, part_ref, next_ref = refs[:12]
+    t_refs, edge_ref, a_ref, f_ref, c_ref, j_ref, u_ref = refs[12:19]
+    if second:
+        out_ref, sems = refs[19:]
     lat = lax.axis_index("lat")
     bottom, top = lat == 0, lat == lax.axis_size("lat") - 1
 
@@ -276,7 +302,6 @@
             c_ref[3 + 2 * north + q] = c_in[2 * north + q]
         for q in range(3):
             f_ref[5 + 7 * north + q] = f_in[7 * north + q]
-            j_ref[6 + north + q] = j_in[north + q]
         edge_ref[0] = flip(tail_in(got_ref))
         t_refs[...] = jnp.zeros(t_refs.shape, F32)
         for k in range(HALO):
@@ -322,17 +347,21 @@
             def _():
                 mid_rows(c_ref, f_ref, 0, j_ref, mid_ref, up_ref, 7, 1, lambda t, n: n - 1 - t, None)
 
-        groups = []
-        for q in range(2):
-            taps = [j_ref[6 * north + 3 * q + 1 + i, b * PIX : (b + 2) * PIX, :] for i in range(5) for b in range(3)]
-            groups.append(jnp.concatenate(taps, axis=1))
-        deltas = dot_nt(jnp.concatenate(groups, axis=0), w_out_ref[...])
+        if north:
+            near = dot_nt(out_taps(j_ref, (10, 11)), w_out_ref[:, 9 * HID :]) + part_ref[1]
+            deltas = [near, dot_nt(out_taps(j_ref, range(10, 15)), w_out_ref[...])]
+        else:
+            near = dot_nt(out_taps(j_ref, (4, 5)), w_out_ref[:, : 6 * HID]) + part_ref[0]
+            deltas = [dot_nt(out_taps(j_ref, range(1, 6)), w_out_ref[...]), near]
+        copies = []
+        if second:
+            copies.append(pltpu.make_async_copy(half_ref, next_ref.at[pl.ds(6 * (1 - north), 6)], sems.at[6]))
+            copies[0].start()
         for q in range(2):
             flipped = []
             for t in range(2):
                 for p in range(2):
-                    begin = (2 * q + p) * PIX
-                    half = deltas[begin : begin + PIX, t * 128 : (t + 1) * 128]
+                    half = deltas[q][p * PIX : (p + 1) * PIX, t * 128 : (t + 1) * 128]
                     u_ref[pl.ds((2 * q + t) * TROWS + 4 + p, PIX, stride=2), :] = half
                 begin = (2 * q + t) * TROWS + 8
                 flipped.append(u_ref[begin : begin + LANES, :].T)
@@ -342,10 +371,14 @@
                 delta = flipped[i * CH : i * CH + CHANNELS, :COLS]
                 cover = jnp.concatenate([mask_ref[r].astype(F32)] * VARS, axis=0)
                 out = ((state_ref[r].astype(F32) + delta) * cover).astype(BF16)
-                out_ref[r if second else 3 * q + i] = out
-        if second:
-            for q in range(6):
-                out_ref[6 * (1 - north) + q] = half_ref[q]
+                if second:
+                    out_ref[3 * q + i] = out
+                    copies.append(pltpu.make_async_copy(out_ref.at[3 * q + i], next_ref.at[r], sems.at[3 * q + i]))
+                    copies[-1].start()
+                else:
+                    next_ref[3 * q + i] = out
+        for copy in copies:
+            copy.wait()
 
     for north in range(2):
         pl.when(lax.rem(lat, 2) == (1 - north if second else north))(functools.partial(side, north))
@@ -377,7 +410,8 @@
         for i in range(n_lat):
             for j in range(n_lon):
                 mate = i + 1 if (i - begin) % 2 == 0 else i - 1
-                target = mate * n_lon + j if 0 <= mate < n_lat else i * n_lon + (j ^ 2)
+                side = i * n_lon + (j ^ (2 if i == n_lat - 1 else 1))
+                target = mate * n_lon + j if 0 <= mate < n_lat else side
                 pairs.append((i * n_lon + j, target))
         return pairs
 
@@ -391,18 +425,21 @@
         ],
         [], 1.5, 16,
     )
-    pay, kept = call(
-        payload_kernel, [SMEM] + [VMEM] * 5, (seam, rows, west, east, high, mate), [PAYLOAD] * 2, [], 0.4, 8,
+    turning = [pltpu.VMEM((2, TROWS, 128), F32), pltpu.VMEM((2, 128, 128), F32)]
+    owned = [(ROWS,) + PACKED, (F_ROWS,) + PACKED]
+    pay, kept, packed, f_own = call(
+        payload_kernel, [SMEM] + [VMEM] * 6, (seam, rows, west, east, high, mate, laid[0]), [PAYLOAD] * 2 + owned,
+        turning, 0.4, 18,
     )
     got = lax.ppermute(pay, axes, swap(1))
-    turning = [pltpu.VMEM((2, TROWS, 128), F32), pltpu.VMEM((2, 128, 128), F32)]
-    packed, pay, f_own = call(
-        pack_kernel, [VMEM] * 4, (rows, west, east, laid[0]),
-        [(ROWS,) + PACKED, PAYLOAD, (F_ROWS,) + PACKED], turning, 3.5, 18,
+    packed, f_own, pay = call(
+        pack_kernel, [VMEM] * 6, (rows, west, east, laid[0], packed, f_own), owned + [PAYLOAD], turning, 3.5, 18,
+        VMEM, {4: 0, 5: 1},
     )
     got_later = lax.ppermute(pay, axes, swap(0))
-    handed = [(len(k),) + block for k, block in zip(KEPT, BLOCKS)]
-    inner = call(inner_kernel, [VMEM] * 4, (f_own, *laid[1:4]), handed, HELD, 1.7, 24)
+    inner = call(
+        inner_kernel, [VMEM] * 5, (f_own, *laid[1:]), [(C_ROWS, PIX, 3 * HID), PARTS], HELD, 2.2, 28,
+    )
     scratch = turning + [pltpu.VMEM((n,) + PACKED, BF16) for n in (22, 20)] + HELD + [pltpu.VMEM((4 * TROWS, 128), F32)]
     shared = (*laid, state, sea_mask, packed, f_own, *inner)
     (half,) = call(
@@ -411,7 +448,7 @@
     )
     (out,) = call(
         functools.partial(outer_kernel, True), [VMEM] * 13, (got_later, half, *shared), [(ROWS, CHANNELS, COLS)],
-        scratch, 6, 30,
+        scratch + [pltpu.VMEM((ROWS // 2, CHANNELS, COLS), BF16), pltpu.SemaphoreType.DMA((ROWS // 2 + 1,))], 6, 30, HBM,
     )
     return jnp.swapaxes(out, 0, 1)
 

time: 34.7 us -> 33 us (0.951)
  starting transfers between devices: 10.4 us -> 7.78 us
  waiting for transfers between devices: 2.9 us -> 4.51 us
  Pallas kernels: 20.3 us -> 19.2 us
    ppermute x1, starting transfers between devices: 8.26 us -> 5.65 us  [body(): got = lax.ppermute(pay, axes, swap(1))]
    ppermute x1, waiting for transfers between devices: 0.11 us -> 2.57 us  [body(): got = lax.ppermute(pay, axes, swap(1))]
    pallas_call x7, Pallas kernels: 20.3 us -> 19.2 us  [call(): pl.pallas_call(kernel, out_shape=tuple((jax.ShapeDtypeStruct(shape, F32 i...]
    ppermute x1, waiting for transfers between devices: 1 us -> 0.14 us  [body(): got_later = lax.ppermute(pay, axes, swap(0))]
  transfers between devices with their start and end apart: 5 -> 5, of which waited for: 3 -> 3; matrix products, arithmetic and copies ran while one was open for 0% -> 0% of each run, Pallas kernels for 33% -> 27%
where the time goes in v4:
time: 33 us; the launch traced here: 32.5 us
  Pallas kernels  19.2 us (58%)
  starting transfers between devices  7.78 us (24%)
  waiting for transfers between devices  4.51 us (14%)
  local copies, waits for them, and re-layouts  0.76 us (2%)
  between operations  0.33 us (1%)
    pallas_call x7, Pallas kernels, call(): pl.pallas_call(kernel, out_shape=tuple((jax.ShapeDtypeStruct(shape, F32 i...  19.2 us
    ppermute x1, starting transfers between devices, body(): got = lax.ppermute(pay, axes, swap(1))  5.65 us
    ppermute x1, waiting for transfers between devices, body(): got = lax.ppermute(pay, axes, swap(1))  2.57 us
    ppermute x1, waiting for transfers between devices, body(): east = lax.ppermute(west_going, 'lon', ring(n_lon, -1))  1.79 us
    ppermute x1, starting transfers between devices, body(): west = lax.ppermute(east_going, 'lon', ring(n_lon, 1))  1.27 us
    ppermute x1, starting transfers between devices, body(): mate = lax.ppermute(high, axes, within)  0.76 us
    unnamed x20, local copies, waits for them, and re-layouts  0.76 us
  transfers between devices with their start and end apart: 5, of which 3 were waited for; matrix products, arithmetic and copies ran while one was open for 0% of the time, Pallas kernels for 27%

profile of v4, /device:TPU:7, one launch (start us, length us, event | category | flops | bytes accessed | tf_op | source)
XLA Modules:
  0.0 32.5 jit_solution(9232919916424659031)
XLA Ops:
  0.0 0.0 copy-start.2
  0.0 0.0 copy-start.3
  0.0 0.0 copy-start.4
  0.0 0.0 copy-start.5
  0.0 0.0 copy-start.6
  0.0 0.0 copy-start.7
  0.0 0.0 copy-start.8
  0.0 2.4 %shard_map.82 = (bf16[80,128]{1,0:T(8,128)(2,1)}, bf16[80,128]{1,0:T(8,128)(2,1)}, bf16[400,384]{1,0:T(8,128)(2,1)}) custom-call(bf16[12,76,270]{2,1,0:T(8,128)(2,1)} %bitcast.11, s32[12,19,270]{2,1,0:T(8,128)} %bitcast.15), custom_call_target="tpu_custom_call" | custom-call | flops 1000000000 | bytes 3000000 | tf_op jit(solution)/shard_map/pallas_call | solution.py:45
  2.5 0.8 %collective-permute-start.2 = (bf16[400,384]{1,0:T(8,128)(2,1)}, bf16[400,384]{1,0:T(8,128)(2,1)S(1)}, u32[]{:S(2)}, u32[]{:S(2)}) collective-permute-start(bf16[400,384]{1,0:T(8,128)(2,1)} %get-tuple-element.27.high_ref), channel_id=1, source_target_pairs={{0,1},{1,0},{2,3},{3,2},{4,5},{5,4},{6,7},{7,6},{8,9},{9,8},{10,11... | collective-permute-start | bytes 921608 | tf_op jit(solution)/shard_map/ppermute | solution.py:418
  3.2 1.3 %collective-permute-start = (bf16[80,128]{1,0:T(8,128)(2,1)}, bf16[80,128]{1,0:T(8,128)(2,1)S(1)}, u32[]{:S(2)}, u32[]{:S(2)}) collective-permute-start(bf16[80,128]{1,0:T(8,128)(2,1)} %get-tuple-element.25), channel_id=1, source_target_pairs={{0,1},{1,2},{2,3},{3,0},{4,5},{5,6},{6,7},{7,4},{8,9},{9,10},{10,1... | collective-permute-start | bytes 61448 | tf_op jit(solution)/shard_map/ppermute | solution.py:402
  4.5 0.0 collective-permute-start.1
  4.5 0.0 copy-done.2
  4.5 0.0 copy-done.3
  4.5 0.0 copy-done.4
  4.5 0.0 copy-done.5
  4.5 0.0 copy-done.6
  4.5 0.0 copy-done.7
  4.5 0.0 copy-done.8
  4.6 0.0 copy-start.9
  4.6 0.7 %copy-done.9 = bf16[80,128]{1,0:T(8,128)(2,1)S(1)} copy-done((bf16[80,128]{1,0:T(8,128)(2,1)S(1)}, bf16[80,128]{1,0:T(8,128)(2,1)}, u32[]{:S(2)}) %copy-start.9) | copy-done | bytes 20504
  5.3 0.0 copy-start
  5.3 0.0 copy-start.1
  5.3 0.8 %shard_map.83 = (bf16[12,80,384]{2,1,0:T(8,128)(2,1)S(1)}, bf16[9,80,256]{2,1,0:T(8,128)(2,1)S(1)}, bf16[4,256,256]{2,1,0:T(8,128)(2,1)S(1)}, bf16[9,256,256]{2,...) custom-call(bf16[80,128]{1,0:T(8,128)(2,1)S(1)} %copy-done.9, ...), custom_call_target="tpu_custom_call" | custom-call | flops 1500000000 | bytes 4500000 | tf_op jit(solution)/shard_map/pallas_call | solution.py:45
  6.1 0.0 collective-permute-done.west_ref
  6.1 1.8 %collective-permute-done.1.east_ref = bf16[80,128]{1,0:T(8,128)(2,1)S(1)} collective-permute-done((bf16[80,128]{1,0:T(8,128)(2,1)}, bf16[80,128]{1,0:T(8,128)(2,1)S(1)}, u32[]{:S(2)}, u32[]{:S(2)}) %collective-permute-start.1) | collective-permute-done | bytes 20512 | tf_op jit(solution)/shard_map/ppermute | solution.py:403
  7.9 0.0 collective-permute-done.2.mate_ref
  7.9 0.0 copy-done
  7.9 0.0 copy-done.1
  7.9 3.4 %shard_map.84 = (bf16[440,256]{1,0:T(8,128)(2,1)S(1)}, bf16[440,256]{1,0:T(8,128)(2,1)S(1)}, bf16[12,288,256]{2,1,0:T(8,128)(2,1)S(1)}, bf16[10,288,256]{2,1,0:T(8,128)(2,1)S(1)}) custom-call(s32[1080]{0:T(1024)S(1)} %copy-done.1, bf16[12,80,384]{2,1,0:T(8,128)(2,1)S(1)} %get-tuple-element.24.rows_ref, bf16[80,128]{1,0:T(8,128)(2,1)S(1)} %collective-permute-done.west_ref, ...), custom_call_target="tpu_custom_call" | custom-call | flops 400000000 | bytes 1200000 | tf_op jit(solution)/shard_map/pallas_call | solution.py:45
  11.3 5.6 %collective-permute-start.4 = (bf16[440,256]{1,0:T(8,128)(2,1)S(1)}, bf16[440,256]{1,0:T(8,128)(2,1)S(1)}, u32[]{:S(2)}, u32[]{:S(2)}) collective-permute-start(bf16[440,256]{1,0:T(8,128)(2,1)S(1)} %get-tuple-element.31), channel_id=1, source_target_pairs={{0,1},{1,0},{2,3},{3,2},{4,8},{5,9},{6,10},{7,11},{8,4},{9,5},{10,... | collective-permute-start | bytes 675848 | tf_op jit(solution)/shard_map/ppermute | solution.py:434
  16.9 0.1 shard_map.85
  17.1 0.1 collective-permute-start.3
  17.2 2.9 %shard_map.86 = (bf16[4,144,768]{2,1,0:T(8,128)(2,1)S(1)}, f32[2,288,256]{2,1,0:T(8,128)S(1)}) custom-call(bf16[10,288,256]{2,1,0:T(8,128)(2,1)S(1)} %get-tuple-element.38.f_ref.refs_10_, bf16[4,256,256]{2,1,0:T(8,128)(2,1)S(1)} %get-tuple-element.33.down_ref.refs_3_, bf16[9,256,256]{2,1,0:T(8,128)(2,1)S(1)} %get-tuple-element.34.mid_ref.refs_4_, ...), custom_call_target="tpu_custom_call" | custom-call | flops 2200000000 | bytes 6600000 | tf_op jit(solution)/shard_map/pallas_call | solution.py:45
  20.0 2.6 %collective-permute-done.4.refs_0_ = bf16[440,256]{1,0:T(8,128)(2,1)S(1)} collective-permute-done((bf16[440,256]{1,0:T(8,128)(2,1)S(1)}, bf16[440,256]{1,0:T(8,128)(2,1)S(1)}, u32[]{:S(2)}, u32[]{:S(2)}) %collective-permute-start.4) | collective-permute-done | bytes 225312 | tf_op jit(solution)/shard_map/ppermute | solution.py:434
  22.6 4.9 %shard_map.87.refs_1_ = bf16[6,76,270]{2,1,0:T(8,128)(2,1)S(1)} custom-call(bf16[440,256]{1,0:T(8,128)(2,1)S(1)} %collective-permute-done.4.refs_0_, bf16[440,256]{1,0:T(8,128)(2,1)S(1)} %get-tuple-element.32.refs_1_, bf16[9,80,256]{2,1,0:T(8,128)(2,1)S(1)} %get-tuple-element.26.in_ref.refs_2_, bf16[4,256,256]{2,1,0:T(8,128)(2,1)S(1)} %get-tuple-element.33.down_ref.refs_3_, ...), custom_call_target="tpu_custom_call" | custom-call | flops 5000000000 | bytes 15000000 | tf_op jit(solution)/shard_map/pallas_call | solution.py:45
  27.5 0.1 collective-permute-done.3.refs_0_
  27.6 4.7 %shard_map.88 = bf16[12,76,270]{2,1,0:T(8,128)(2,1)} custom-call(bf16[440,256]{1,0:T(8,128)(2,1)S(1)} %collective-permute-done.3.refs_0_, bf16[6,76,270]{2,1,0:T(8,128)(2,1)S(1)} %shard_map.87.refs_1_, bf16[9,80,256]{2,1,0:T(8,128)(2,1)S(1)} %get-tuple-element.26.in_ref.refs_2_, bf16[4,256,256]{2,1,0:T(8,128)(2,1)S(1)} %get-tuple-element.33.down_ref.refs_3_, ...), custom_call_target="tpu_custom_call" | custom-call | flops 6000000000 | bytes 18000000 | tf_op jit(solution)/shard_map/pallas_call | solution.py:45
Async XLA Ops:
  0.0 4.5 %copy-start.2 = (bf16[3,3,200,200]{3,2,1,0:T(8,128)(2,1)S(1)}, bf16[3,3,200,200]{3,2,1,0:T(8,128)(2,1)}, u32[]{:S(2)}) copy-start(bf16[3,3,200,200]{3,2,1,0:T(8,128)(2,1)} %param.13) | copy-start | bytes 2160004
  0.0 4.5 %copy-start.3 = (bf16[76,12,270]{2,0,1:T(8,128)(2,1)S(1)}, bf16[76,12,270]{2,0,1:T(8,128)(2,1)}, u32[]{:S(2)}) copy-start(bf16[76,12,270]{2,0,1:T(8,128)(2,1)} %param.8) | copy-start | bytes 1477444
  0.0 4.5 %copy-start.4 = (s32[19,12,270]{2,0,1:T(8,128)S(1)}, s32[19,12,270]{2,0,1:T(8,128)}, u32[]{:S(2)}) copy-start(s32[19,12,270]{2,0,1:T(8,128)} %param.9) | copy-start | bytes 738724
  0.0 4.5 %copy-start.5 = (bf16[2,2,200,200]{3,2,1,0:T(8,128)(2,1)S(1)}, bf16[2,2,200,200]{3,2,1,0:T(8,128)(2,1)}, u32[]{:S(2)}) copy-start(bf16[2,2,200,200]{3,2,1,0:T(8,128)(2,1)} %param.12) | copy-start | bytes 960004
  0.0 4.5 %copy-start.6 = (bf16[2,2,200,200]{3,2,1,0:T(8,128)(2,1)S(1)}, bf16[2,2,200,200]{3,2,1,0:T(8,128)(2,1)}, u32[]{:S(2)}) copy-start(bf16[2,2,200,200]{3,2,1,0:T(8,128)(2,1)} %param.14) | copy-start | bytes 960004
  0.0 4.5 %copy-start.7 = (bf16[3,3,200,76]{2,3,1,0:T(8,128)(2,1)S(1)}, bf16[3,3,200,76]{2,3,1,0:T(8,128)(2,1)}, u32[]{:S(2)}) copy-start(bf16[3,3,200,76]{2,3,1,0:T(8,128)(2,1)} %param.11) | copy-start | bytes 820804
  0.0 4.5 %copy-start.8 = (bf16[3,3,76,200]{3,2,1,0:T(8,128)(2,1)S(1)}, bf16[3,3,76,200]{3,2,1,0:T(8,128)(2,1)}, u32[]{:S(2)}) copy-start(bf16[3,3,76,200]{3,2,1,0:T(8,128)(2,1)} %param.15) | copy-start | bytes 820804
  2.5 5.5 %collective-permute-start.2 = (bf16[400,384]{1,0:T(8,128)(2,1)}, bf16[400,384]{1,0:T(8,128)(2,1)S(1)}, u32[]{:S(2)}, u32[]{:S(2)}) collective-permute-start(bf16[400,384]{1,0:T(8,128)(2,1)} %get-tuple-element.27.high_ref), channel_id=1, source_target_pairs={{0,1},{1,0},{2,3},{3,2},{4,5},{5,4},{6,7},{7,6},{8,9},{9,8},{10,11... | collective-permute-start | bytes 921608 | tf_op jit(solution)/shard_map/ppermute | solution.py:418
  3.2 2.9 %collective-permute-start = (bf16[80,128]{1,0:T(8,128)(2,1)}, bf16[80,128]{1,0:T(8,128)(2,1)S(1)}, u32[]{:S(2)}, u32[]{:S(2)}) collective-permute-start(bf16[80,128]{1,0:T(8,128)(2,1)} %get-tuple-element.25), channel_id=1, source_target_pairs={{0,1},{1,2},{2,3},{3,0},{4,5},{5,6},{6,7},{7,4},{8,9},{9,10},{10,1... | collective-permute-start | bytes 61448 | tf_op jit(solution)/shard_map/ppermute | solution.py:402
  4.5 3.4 %collective-permute-start.1 = (bf16[80,128]{1,0:T(8,128)(2,1)}, bf16[80,128]{1,0:T(8,128)(2,1)S(1)}, u32[]{:S(2)}, u32[]{:S(2)}) collective-permute-start(bf16[80,128]{1,0:T(8,128)(2,1)} %get-tuple-element.23.after_ref), channel_id=1, source_target_pairs={{0,3},{1,0},{2,1},{3,2},{4,7},{5,4},{6,5},{7,6},{8,11},{9,8},{10,9... | collective-permute-start | bytes 61448 | tf_op jit(solution)/shard_map/ppermute | solution.py:403
  4.6 0.7 %copy-start.9 = (bf16[80,128]{1,0:T(8,128)(2,1)S(1)}, bf16[80,128]{1,0:T(8,128)(2,1)}, u32[]{:S(2)}) copy-start(bf16[80,128]{1,0:T(8,128)(2,1)} %get-tuple-element.23.after_ref) | copy-start | bytes 61444
  5.3 2.6 %copy-start = (bf16[400,384]{1,0:T(8,128)(2,1)S(1)}, bf16[400,384]{1,0:T(8,128)(2,1)}, u32[]{:S(2)}) copy-start(bf16[400,384]{1,0:T(8,128)(2,1)} %get-tuple-element.27.high_ref) | copy-start | bytes 921604
  5.3 2.6 %copy-start.1 = (s32[1080]{0:T(1024)S(1)}, s32[1080]{0:T(1024)}, u32[]{:S(2)}) copy-start(s32[1080]{0:T(1024)} %seam_ref.1) | copy-start | bytes 12964
  11.3 11.3 %collective-permute-start.4 = (bf16[440,256]{1,0:T(8,128)(2,1)S(1)}, bf16[440,256]{1,0:T(8,128)(2,1)S(1)}, u32[]{:S(2)}, u32[]{:S(2)}) collective-permute-start(bf16[440,256]{1,0:T(8,128)(2,1)S(1)} %get-tuple-element.31), channel_id=1, source_target_pairs={{0,1},{1,0},{2,3},{3,2},{4,8},{5,9},{6,10},{7,11},{8,4},{9,5},{10,... | collective-permute-start | bytes 675848 | tf_op jit(solution)/shard_map/ppermute | solution.py:434
  17.1 10.5 %collective-permute-start.3 = (bf16[440,256]{1,0:T(8,128)(2,1)S(1)}, bf16[440,256]{1,0:T(8,128)(2,1)S(1)}, u32[]{:S(2)}, u32[]{:S(2)}) collective-permute-start(bf16[440,256]{1,0:T(8,128)(2,1)S(1)} %get-tuple-element.30), channel_id=1, source_target_pairs={{0,4},{1,5},{2,6},{3,7},{4,0},{5,1},{6,2},{7,3},{8,12},{9,13},{10,... | collective-permute-start | bytes 675848 | tf_op jit(solution)/shard_map/ppermute | solution.py:439

commit v5 on v4

--- a/solution.py
+++ b/solution.py
@@ -20,7 +20,7 @@
 TROWS = 408
 FOLD_REST = COLS + 2 * HALO - MAIN
 EARLY = 16
-CHUNK = 3
+CHUNK = 6
 F32, BF16 = jnp.float32, jnp.bfloat16
 VMEM = pl.BlockSpec(memory_space=pltpu.VMEM)
 HBM = pl.BlockSpec(memory_space=pltpu.HBM)
@@ -121,7 +121,7 @@
         t_ref[8 - HALO : 8, :] = edge_ref[0, edge, :]
         t_ref[8 + COLS : 8 + COLS + HALO, :] = edge_ref[1, edge, :]
         pack(t_ref, packed_ref, r)
-    first_rows(packed_ref, HALO, f_ref, F_FIRST, in_ref, F_FIRST, F_ROWS, straight)
+    first_rows(Rows(packed_ref, HALO), f_ref, F_FIRST, in_ref, F_FIRST, F_ROWS, straight)
 
 
 def starts_early():
@@ -219,21 +219,33 @@
     return t
 
 
-def first_rows(a_ref, begin, f_ref, f_begin, w_ref, fr, n, tap):
+class Rows:
+    def __init__(self, own, first, rest=None):
+        self.own, self.first, self.rest = own, first, rest
+        self.last = first + own.shape[0] - 1
+
+    def __getitem__(self, at):
+        row, rest = (at[0], at[1:]) if isinstance(at, tuple) else (at, ())
+        if self.first <= row <= self.last:
+            return self.own[(row - self.first,) + rest]
+        return self.rest[(row,) + rest]
+
+
+def first_rows(packed, f_ref, f_begin, w_ref, fr, n, tap):
     w = []
     for a in range(3):
         w += [w_ref[tap(3 * a + b, 9)] for b in range(3)] + [jnp.zeros((HID - 3 * CH, HID), BF16)]
     w = jnp.concatenate(w, axis=0)
     for q in range(n):
-        taps = jnp.concatenate([a_ref[fr + q + a - begin] for a in range(3)], axis=1)
+        taps = jnp.concatenate([packed[fr + q + a] for a in range(3)], axis=1)
         f_ref[fr + q - f_begin] = gelu(jnp.dot(taps, w, preferred_element_type=F32)).astype(BF16)
 
 
-def coarse_rows(f_ref, f_begin, c_ref, w_ref, ci, n, tap, held):
+def coarse_rows(first, c_ref, c_begin, w_ref, ci, n, tap, held):
     w = jnp.concatenate([w_ref[tap(t, 4)] for t in range(4)], axis=1)
     pieces = []
     for q in range(n):
-        piece = [f_ref[2 * (ci + q) + a - f_begin, b * PIX : (b + 1) * PIX, :] for a in range(2) for b in range(2)]
+        piece = [first[2 * (ci + q) + a, b * PIX : (b + 1) * PIX, :] for a in range(2) for b in range(2)]
         pieces.append(jnp.concatenate(piece, axis=1))
     coarse = gelu(dot_nt(jnp.concatenate(pieces, axis=0), w))
     if held is not None:
@@ -241,21 +253,25 @@
     for q in range(n):
         one = coarse[q * PIX : (q + 1) * PIX]
         planes = [pltpu.roll(one, 1, 0), one, pltpu.roll(one, PIX - 1, 0)]
-        c_ref[ci + q] = jnp.concatenate(planes, axis=1).astype(BF16)
-
-
-def mid_rows(c_ref, f_ref, f_begin, j_ref, mid_ref, up_ref, mi, n, tap, held):
-    taps = [c_ref[pl.ds(mi + a, n)].reshape(n * PIX, 3 * HID) for a in range(3)]
+        c_ref[ci + q - c_begin] = jnp.concatenate(planes, axis=1).astype(BF16)
+
+
+def mid_rows(coarse, first, j_ref, mid_ref, up_ref, mi, n, tap, held, needed):
+    taps = [jnp.concatenate([coarse[mi + a + q] for q in range(n)], axis=0) for a in range(3)]
     w = jnp.concatenate([mid_ref[tap(t, 9)] for t in range(9)], axis=1)
     middle = gelu(dot_nt(jnp.concatenate(taps, axis=1), w)).astype(BF16)
     for a in range(2):
-        grown = [dot_nt(middle, up_ref[tap(2 * a + b, 4)]) for b in range(2)]
-        for q in range(n):
+        rows = [q for q in range(n) if 2 * (mi + q) + a in needed]
+        if not rows:
+            continue
+        begin, end = rows[0], rows[-1] + 1
+        grown = [dot_nt(middle[begin * PIX : end * PIX], up_ref[tap(2 * a + b, 4)]) for b in range(2)]
+        for q in rows:
             row = 2 * (mi + q) + a
             halves = []
             for b in range(2):
-                first = f_ref[row + 2 - f_begin, b * PIX : (b + 1) * PIX, :].astype(F32)
-                half = gelu(grown[b][q * PIX : (q + 1) * PIX]) + first
+                skip = first[row + 2, b * PIX : (b + 1) * PIX, :].astype(F32)
+                half = gelu(grown[b][(q - begin) * PIX : (q - begin + 1) * PIX]) + skip
                 halves.append(half * held if held is not None and q == 0 else half)
             even, odd = halves
             planes = (pltpu.roll(odd, 1, 0), even, odd, pltpu.roll(even, PIX - 1, 0))
@@ -274,11 +290,10 @@
     return jnp.concatenate([j_ref[r, b * PIX : (b + 2) * PIX, :] for r in rows for b in range(3)], axis=1)
 
 
-def inner_kernel(f_ref, down_ref, mid_ref, up_ref, w_out_ref, c_out, part_ref, c_ref, j_ref):
-    coarse_rows(f_ref, F_FIRST, c_ref, down_ref, C_FIRST, C_ROWS, straight, None)
-    mid_rows(c_ref, f_ref, F_FIRST, j_ref, mid_ref, up_ref, 3, 2, straight, None)
-    for i in range(C_ROWS):
-        c_out[i] = c_ref[C_FIRST + i]
+def inner_kernel(f_ref, down_ref, mid_ref, up_ref, w_out_ref, c_out, part_ref, j_ref):
+    first = Rows(f_ref, F_FIRST)
+    coarse_rows(first, c_out, C_FIRST, down_ref, C_FIRST, C_ROWS, straight, None)
+    mid_rows(Rows(c_out, C_FIRST), first, j_ref, mid_ref, up_ref, 3, 2, straight, None, range(6, 10))
     part_ref[0] = dot_nt(out_taps(j_ref, (6, 7, 8)), w_out_ref[:, 6 * HID :])
     part_ref[1] = dot_nt(out_taps(j_ref, (7, 8, 9)), w_out_ref[:, : 9 * HID])
 
@@ -297,11 +312,7 @@
     bottom, top = lat == 0, lat == lax.axis_size("lat") - 1
 
     def side(north):
-        for q in range(2):
-            a_ref[5 + 10 * north + q] = packed_ref[10 * north + q]
-            c_ref[3 + 2 * north + q] = c_in[2 * north + q]
-        for q in range(3):
-            f_ref[5 + 7 * north + q] = f_in[7 * north + q]
+        packed, first, coarse = Rows(packed_ref, HALO, a_ref), Rows(f_in, F_FIRST, f_ref), Rows(c_in, C_FIRST, c_ref)
         edge_ref[0] = flip(tail_in(got_ref))
         t_refs[...] = jnp.zeros(t_refs.shape, F32)
         for k in range(HALO):
@@ -335,17 +346,17 @@
             turn = lambda t, n: jnp.where(top, n - 1 - t, t)
         elif not second:
             keep = jnp.where(bottom, 0.0, 1.0).astype(F32)
-        first_rows(a_ref, 0, f_ref, 0, in_ref, 4 + 11 * north, 1, straight)
-        first_rows(a_ref, 0, f_ref, 0, in_ref, 16 * north, 4, turn)
-        coarse_rows(f_ref, 0, c_ref, down_ref, 8 * north, 2, turn, keep)
-        coarse_rows(f_ref, 0, c_ref, down_ref, 2 + 5 * north, 1, straight, None)
-        mid_rows(c_ref, f_ref, 0, j_ref, mid_ref, up_ref, 5 * north, 3, straight, keep)
+        first_rows(packed, f_ref, 0, in_ref, 4 + 11 * north, 1, straight)
+        first_rows(packed, f_ref, 0, in_ref, 16 * north, 4, turn)
+        coarse_rows(first, c_ref, 0, down_ref, 8 * north, 2, turn, keep)
+        coarse_rows(first, c_ref, 0, down_ref, 2 + 5 * north, 1, straight, None)
+        mid_rows(coarse, first, j_ref, mid_ref, up_ref, 5 * north, 3, straight, keep, range(1, 15))
 
         if not second and north:
 
             @pl.when(top)
             def _():
-                mid_rows(c_ref, f_ref, 0, j_ref, mid_ref, up_ref, 7, 1, lambda t, n: n - 1 - t, None)
+                mid_rows(coarse, first, j_ref, mid_ref, up_ref, 7, 1, lambda t, n: n - 1 - t, None, (14,))
 
         if north:
             near = dot_nt(out_taps(j_ref, (10, 11)), w_out_ref[:, 9 * HID :]) + part_ref[1]
@@ -438,7 +449,7 @@
     )
     got_later = lax.ppermute(pay, axes, swap(0))
     inner = call(
-        inner_kernel, [VMEM] * 5, (f_own, *laid[1:]), [(C_ROWS, PIX, 3 * HID), PARTS], HELD, 2.2, 28,
+        inner_kernel, [VMEM] * 5, (f_own, *laid[1:]), [(C_ROWS, PIX, 3 * HID), PARTS], HELD[1:], 2.2, 28,
     )
     scratch = turning + [pltpu.VMEM((n,) + PACKED, BF16) for n in (22, 20)] + HELD + [pltpu.VMEM((4 * TROWS, 128), F32)]
     shared = (*laid, state, sea_mask, packed, f_own, *inner)

time: 33 us -> 32.7 us (level)
  transfers between devices with their start and end apart: 5 -> 5, of which waited for: 3 -> 3; matrix products, arithmetic and copies ran while one was open for 0% -> 0% of each run, Pallas kernels for 27% -> 26%
where the time goes in v5:
time: 32.7 us; the launch traced here: 32.4 us
  Pallas kernels  19 us (58%)
  starting transfers between devices  7.78 us (24%)
  waiting for transfers between devices  4.61 us (14%)
  local copies, waits for them, and re-layouts  0.76 us (2%)
  between operations  0.33 us (1%)
    pallas_call x7, Pallas kernels, call(): pl.pallas_call(kernel, out_shape=tuple((jax.ShapeDtypeStruct(shape, F32 i...  19 us
    ppermute x1, starting transfers between devices, body(): got = lax.ppermute(pay, axes, swap(1))  5.65 us
    ppermute x1, waiting for transfers between devices, body(): got = lax.ppermute(pay, axes, swap(1))  2.53 us
    ppermute x1, waiting for transfers between devices, body(): east = lax.ppermute(west_going, 'lon', ring(n_lon, -1))  1.79 us
    ppermute x1, starting transfers between devices, body(): west = lax.ppermute(east_going, 'lon', ring(n_lon, 1))  1.27 us
    ppermute x1, starting transfers between devices, body(): mate = lax.ppermute(high, axes, within)  0.76 us
    unnamed x20, local copies, waits for them, and re-layouts  0.76 us
  transfers between devices with their start and end apart: 5, of which 3 were waited for; matrix products, arithmetic and copies ran while one was open for 0% of the time, Pallas kernels for 26%

profile of v5, /device:TPU:7, one launch (start us, length us, event | category | flops | bytes accessed | tf_op | source)
XLA Modules:
  0.0 32.4 jit_solution(12884835669871366007)
XLA Ops:
  0.0 0.0 copy-start.2
  0.0 0.0 copy-start.3
  0.0 0.0 copy-start.4
  0.0 0.0 copy-start.5
  0.0 0.0 copy-start.6
  0.0 0.0 copy-start.7
  0.0 0.0 copy-start.8
  0.0 2.4 %shard_map.82 = (bf16[80,128]{1,0:T(8,128)(2,1)}, bf16[80,128]{1,0:T(8,128)(2,1)}, bf16[400,384]{1,0:T(8,128)(2,1)}) custom-call(bf16[12,76,270]{2,1,0:T(8,128)(2,1)} %bitcast.11, s32[12,19,270]{2,1,0:T(8,128)} %bitcast.15), custom_call_target="tpu_custom_call" | custom-call | flops 1000000000 | bytes 3000000 | tf_op jit(solution)/shard_map/pallas_call | solution.py:45
  2.4 0.8 %collective-permute-start.2 = (bf16[400,384]{1,0:T(8,128)(2,1)}, bf16[400,384]{1,0:T(8,128)(2,1)S(1)}, u32[]{:S(2)}, u32[]{:S(2)}) collective-permute-start(bf16[400,384]{1,0:T(8,128)(2,1)} %get-tuple-element.27.high_ref), channel_id=1, source_target_pairs={{0,1},{1,0},{2,3},{3,2},{4,5},{5,4},{6,7},{7,6},{8,9},{9,8},{10,11... | collective-permute-start | bytes 921608 | tf_op jit(solution)/shard_map/ppermute | solution.py:429
  3.2 1.3 %collective-permute-start = (bf16[80,128]{1,0:T(8,128)(2,1)}, bf16[80,128]{1,0:T(8,128)(2,1)S(1)}, u32[]{:S(2)}, u32[]{:S(2)}) collective-permute-start(bf16[80,128]{1,0:T(8,128)(2,1)} %get-tuple-element.25), channel_id=1, source_target_pairs={{0,1},{1,2},{2,3},{3,0},{4,5},{5,6},{6,7},{7,4},{8,9},{9,10},{10,1... | collective-permute-start | bytes 61448 | tf_op jit(solution)/shard_map/ppermute | solution.py:413
  4.5 0.0 collective-permute-start.1
  4.5 0.0 copy-done.2
  4.5 0.0 copy-done.3
  4.5 0.0 copy-done.4
  4.5 0.0 copy-done.5
  4.5 0.0 copy-done.6
  4.5 0.0 copy-done.7
  4.5 0.0 copy-done.8
  4.5 0.0 copy-start.9
  4.5 0.7 %copy-done.9 = bf16[80,128]{1,0:T(8,128)(2,1)S(1)} copy-done((bf16[80,128]{1,0:T(8,128)(2,1)S(1)}, bf16[80,128]{1,0:T(8,128)(2,1)}, u32[]{:S(2)}) %copy-start.9) | copy-done | bytes 20504
  5.2 0.0 copy-start
  5.2 0.0 copy-start.1
  5.2 0.8 %shard_map.83 = (bf16[12,80,384]{2,1,0:T(8,128)(2,1)S(1)}, bf16[9,80,256]{2,1,0:T(8,128)(2,1)S(1)}, bf16[4,256,256]{2,1,0:T(8,128)(2,1)S(1)}, bf16[9,256,256]{2,...) custom-call(bf16[80,128]{1,0:T(8,128)(2,1)S(1)} %copy-done.9, ...), custom_call_target="tpu_custom_call" | custom-call | flops 1500000000 | bytes 4500000 | tf_op jit(solution)/shard_map/pallas_call | solution.py:45
  6.1 0.0 collective-permute-done.west_ref
  6.1 1.8 %collective-permute-done.1.east_ref = bf16[80,128]{1,0:T(8,128)(2,1)S(1)} collective-permute-done((bf16[80,128]{1,0:T(8,128)(2,1)}, bf16[80,128]{1,0:T(8,128)(2,1)S(1)}, u32[]{:S(2)}, u32[]{:S(2)}) %collective-permute-start.1) | collective-permute-done | bytes 20512 | tf_op jit(solution)/shard_map/ppermute | solution.py:414
  7.9 0.0 collective-permute-done.2.mate_ref
  7.9 0.0 copy-done
  7.9 0.0 copy-done.1
  7.9 3.4 %shard_map.84 = (bf16[440,256]{1,0:T(8,128)(2,1)S(1)}, bf16[440,256]{1,0:T(8,128)(2,1)S(1)}, bf16[12,288,256]{2,1,0:T(8,128)(2,1)S(1)}, bf16[10,288,256]{2,1,0:T(8,128)(2,1)S(1)}) custom-call(s32[1080]{0:T(1024)S(1)} %copy-done.1, bf16[12,80,384]{2,1,0:T(8,128)(2,1)S(1)} %get-tuple-element.24.rows_ref, bf16[80,128]{1,0:T(8,128)(2,1)S(1)} %collective-permute-done.west_ref, ...), custom_call_target="tpu_custom_call" | custom-call | flops 400000000 | bytes 1200000 | tf_op jit(solution)/shard_map/pallas_call | solution.py:45
  11.3 5.6 %collective-permute-start.4 = (bf16[440,256]{1,0:T(8,128)(2,1)S(1)}, bf16[440,256]{1,0:T(8,128)(2,1)S(1)}, u32[]{:S(2)}, u32[]{:S(2)}) collective-permute-start(bf16[440,256]{1,0:T(8,128)(2,1)S(1)} %get-tuple-element.31), channel_id=1, source_target_pairs={{0,1},{1,0},{2,3},{3,2},{4,8},{5,9},{6,10},{7,11},{8,4},{9,5},{10,... | collective-permute-start | bytes 675848 | tf_op jit(solution)/shard_map/ppermute | solution.py:445
  16.9 0.1 shard_map.85
  17.0 0.1 collective-permute-start.3
  17.1 2.9 %shard_map.86 = (bf16[4,144,768]{2,1,0:T(8,128)(2,1)S(1)}, f32[2,288,256]{2,1,0:T(8,128)S(1)}) custom-call(bf16[10,288,256]{2,1,0:T(8,128)(2,1)S(1)} %get-tuple-element.38.f_ref.refs_10_, bf16[4,256,256]{2,1,0:T(8,128)(2,1)S(1)} %get-tuple-element.33.down_ref.refs_3_, bf16[9,256,256]{2,1,0:T(8,128)(2,1)S(1)} %get-tuple-element.34.mid_ref.refs_4_, ...), custom_call_target="tpu_custom_call" | custom-call | flops 2200000000 | bytes 6600000 | tf_op jit(solution)/shard_map/pallas_call | solution.py:45
  20.0 2.5 %collective-permute-done.4.refs_0_ = bf16[440,256]{1,0:T(8,128)(2,1)S(1)} collective-permute-done((bf16[440,256]{1,0:T(8,128)(2,1)S(1)}, bf16[440,256]{1,0:T(8,128)(2,1)S(1)}, u32[]{:S(2)}, u32[]{:S(2)}) %collective-permute-start.4) | collective-permute-done | bytes 225312 | tf_op jit(solution)/shard_map/ppermute | solution.py:445
  22.6 4.7 %shard_map.87.refs_1_ = bf16[6,76,270]{2,1,0:T(8,128)(2,1)S(1)} custom-call(bf16[440,256]{1,0:T(8,128)(2,1)S(1)} %collective-permute-done.4.refs_0_, bf16[440,256]{1,0:T(8,128)(2,1)S(1)} %get-tuple-element.32.refs_1_, bf16[9,80,256]{2,1,0:T(8,128)(2,1)S(1)} %get-tuple-element.26.in_ref.refs_2_, bf16[4,256,256]{2,1,0:T(8,128)(2,1)S(1)} %get-tuple-element.33.down_ref.refs_3_, ...), custom_call_target="tpu_custom_call" | custom-call | flops 5000000000 | bytes 15000000 | tf_op jit(solution)/shard_map/pallas_call | solution.py:45
  27.3 0.3 collective-permute-done.3.refs_0_
  27.6 4.7 %shard_map.88 = bf16[12,76,270]{2,1,0:T(8,128)(2,1)} custom-call(bf16[440,256]{1,0:T(8,128)(2,1)S(1)} %collective-permute-done.3.refs_0_, bf16[6,76,270]{2,1,0:T(8,128)(2,1)S(1)} %shard_map.87.refs_1_, bf16[9,80,256]{2,1,0:T(8,128)(2,1)S(1)} %get-tuple-element.26.in_ref.refs_2_, bf16[4,256,256]{2,1,0:T(8,128)(2,1)S(1)} %get-tuple-element.33.down_ref.refs_3_, ...), custom_call_target="tpu_custom_call" | custom-call | flops 6000000000 | bytes 18000000 | tf_op jit(solution)/shard_map/pallas_call | solution.py:45
Async XLA Ops:
  0.0 4.5 %copy-start.2 = (bf16[3,3,200,200]{3,2,1,0:T(8,128)(2,1)S(1)}, bf16[3,3,200,200]{3,2,1,0:T(8,128)(2,1)}, u32[]{:S(2)}) copy-start(bf16[3,3,200,200]{3,2,1,0:T(8,128)(2,1)} %param.13) | copy-start | bytes 2160004
  0.0 4.5 %copy-start.3 = (bf16[76,12,270]{2,0,1:T(8,128)(2,1)S(1)}, bf16[76,12,270]{2,0,1:T(8,128)(2,1)}, u32[]{:S(2)}) copy-start(bf16[76,12,270]{2,0,1:T(8,128)(2,1)} %param.8) | copy-start | bytes 1477444
  0.0 4.5 %copy-start.4 = (s32[19,12,270]{2,0,1:T(8,128)S(1)}, s32[19,12,270]{2,0,1:T(8,128)}, u32[]{:S(2)}) copy-start(s32[19,12,270]{2,0,1:T(8,128)} %param.9) | copy-start | bytes 738724
  0.0 4.5 %copy-start.5 = (bf16[2,2,200,200]{3,2,1,0:T(8,128)(2,1)S(1)}, bf16[2,2,200,200]{3,2,1,0:T(8,128)(2,1)}, u32[]{:S(2)}) copy-start(bf16[2,2,200,200]{3,2,1,0:T(8,128)(2,1)} %param.12) | copy-start | bytes 960004
  0.0 4.5 %copy-start.6 = (bf16[2,2,200,200]{3,2,1,0:T(8,128)(2,1)S(1)}, bf16[2,2,200,200]{3,2,1,0:T(8,128)(2,1)}, u32[]{:S(2)}) copy-start(bf16[2,2,200,200]{3,2,1,0:T(8,128)(2,1)} %param.14) | copy-start | bytes 960004
  0.0 4.5 %copy-start.7 = (bf16[3,3,200,76]{2,3,1,0:T(8,128)(2,1)S(1)}, bf16[3,3,200,76]{2,3,1,0:T(8,128)(2,1)}, u32[]{:S(2)}) copy-start(bf16[3,3,200,76]{2,3,1,0:T(8,128)(2,1)} %param.11) | copy-start | bytes 820804
  0.0 4.5 %copy-start.8 = (bf16[3,3,76,200]{3,2,1,0:T(8,128)(2,1)S(1)}, bf16[3,3,76,200]{3,2,1,0:T(8,128)(2,1)}, u32[]{:S(2)}) copy-start(bf16[3,3,76,200]{3,2,1,0:T(8,128)(2,1)} %param.15) | copy-start | bytes 820804
  2.4 5.5 %collective-permute-start.2 = (bf16[400,384]{1,0:T(8,128)(2,1)}, bf16[400,384]{1,0:T(8,128)(2,1)S(1)}, u32[]{:S(2)}, u32[]{:S(2)}) collective-permute-start(bf16[400,384]{1,0:T(8,128)(2,1)} %get-tuple-element.27.high_ref), channel_id=1, source_target_pairs={{0,1},{1,0},{2,3},{3,2},{4,5},{5,4},{6,7},{7,6},{8,9},{9,8},{10,11... | collective-permute-start | bytes 921608 | tf_op jit(solution)/shard_map/ppermute | solution.py:429
  3.2 2.9 %collective-permute-start = (bf16[80,128]{1,0:T(8,128)(2,1)}, bf16[80,128]{1,0:T(8,128)(2,1)S(1)}, u32[]{:S(2)}, u32[]{:S(2)}) collective-permute-start(bf16[80,128]{1,0:T(8,128)(2,1)} %get-tuple-element.25), channel_id=1, source_target_pairs={{0,1},{1,2},{2,3},{3,0},{4,5},{5,6},{6,7},{7,4},{8,9},{9,10},{10,1... | collective-permute-start | bytes 61448 | tf_op jit(solution)/shard_map/ppermute | solution.py:413
  4.5 3.4 %collective-permute-start.1 = (bf16[80,128]{1,0:T(8,128)(2,1)}, bf16[80,128]{1,0:T(8,128)(2,1)S(1)}, u32[]{:S(2)}, u32[]{:S(2)}) collective-permute-start(bf16[80,128]{1,0:T(8,128)(2,1)} %get-tuple-element.23.after_ref), channel_id=1, source_target_pairs={{0,3},{1,0},{2,1},{3,2},{4,7},{5,4},{6,5},{7,6},{8,11},{9,8},{10,9... | collective-permute-start | bytes 61448 | tf_op jit(solution)/shard_map/ppermute | solution.py:414
  4.5 0.7 %copy-start.9 = (bf16[80,128]{1,0:T(8,128)(2,1)S(1)}, bf16[80,128]{1,0:T(8,128)(2,1)}, u32[]{:S(2)}) copy-start(bf16[80,128]{1,0:T(8,128)(2,1)} %get-tuple-element.23.after_ref) | copy-start | bytes 61444
  5.2 2.6 %copy-start = (bf16[400,384]{1,0:T(8,128)(2,1)S(1)}, bf16[400,384]{1,0:T(8,128)(2,1)}, u32[]{:S(2)}) copy-start(bf16[400,384]{1,0:T(8,128)(2,1)} %get-tuple-element.27.high_ref) | copy-start | bytes 921604
  5.2 2.6 %copy-start.1 = (s32[1080]{0:T(1024)S(1)}, s32[1080]{0:T(1024)}, u32[]{:S(2)}) copy-start(s32[1080]{0:T(1024)} %seam_ref.1) | copy-start | bytes 12964
  11.3 11.3 %collective-permute-start.4 = (bf16[440,256]{1,0:T(8,128)(2,1)S(1)}, bf16[440,256]{1,0:T(8,128)(2,1)S(1)}, u32[]{:S(2)}, u32[]{:S(2)}) collective-permute-start(bf16[440,256]{1,0:T(8,128)(2,1)S(1)} %get-tuple-element.31), channel_id=1, source_target_pairs={{0,1},{1,0},{2,3},{3,2},{4,8},{5,9},{6,10},{7,11},{8,4},{9,5},{10,... | collective-permute-start | bytes 675848 | tf_op jit(solution)/shard_map/ppermute | solution.py:445
  17.0 10.5 %collective-permute-start.3 = (bf16[440,256]{1,0:T(8,128)(2,1)S(1)}, bf16[440,256]{1,0:T(8,128)(2,1)S(1)}, u32[]{:S(2)}, u32[]{:S(2)}) collective-permute-start(bf16[440,256]{1,0:T(8,128)(2,1)S(1)} %get-tuple-element.30), channel_id=1, source_target_pairs={{0,4},{1,5},{2,6},{3,7},{4,0},{5,1},{6,2},{7,3},{8,12},{9,13},{10,... | collective-permute-start | bytes 675848 | tf_op jit(solution)/shard_map/ppermute | solution.py:450

commit v6 on v5

--- a/solution.py
+++ b/solution.py
@@ -237,8 +237,9 @@
         w += [w_ref[tap(3 * a + b, 9)] for b in range(3)] + [jnp.zeros((HID - 3 * CH, HID), BF16)]
     w = jnp.concatenate(w, axis=0)
     for q in range(n):
-        taps = jnp.concatenate([packed[fr + q + a] for a in range(3)], axis=1)
-        f_ref[fr + q - f_begin] = gelu(jnp.dot(taps, w, preferred_element_type=F32)).astype(BF16)
+        for p in (slice(0, PIX), slice(PIX, 2 * PIX)):
+            taps = jnp.concatenate([packed[fr + q + a, p, :] for a in range(3)], axis=1)
+            f_ref[fr + q - f_begin, p, :] = gelu(jnp.dot(taps, w, preferred_element_type=F32)).astype(BF16)
 
 
 def coarse_rows(first, c_ref, c_begin, w_ref, ci, n, tap, held):
@@ -259,7 +260,10 @@
 def mid_rows(coarse, first, j_ref, mid_ref, up_ref, mi, n, tap, held, needed):
     taps = [jnp.concatenate([coarse[mi + a + q] for q in range(n)], axis=0) for a in range(3)]
     w = jnp.concatenate([mid_ref[tap(t, 9)] for t in range(9)], axis=1)
-    middle = gelu(dot_nt(jnp.concatenate(taps, axis=1), w)).astype(BF16)
+    taps = jnp.concatenate(taps, axis=1)
+    size = PIX if n == 2 else n * PIX
+    middle = [dot_nt(taps[i : i + size], w) for i in range(0, n * PIX, size)]
+    middle = gelu(jnp.concatenate(middle, axis=0)).astype(BF16)
     for a in range(2):
         rows = [q for q in range(n) if 2 * (mi + q) + a in needed]
         if not rows:

time: 32.7 us -> 34.6 us (1.058)
  Pallas kernels: 19 us -> 21.2 us
    pallas_call x7, Pallas kernels: 19 us -> 21.2 us  [call(): pl.pallas_call(kernel, out_shape=tuple((jax.ShapeDtypeStruct(shape, F32 i...]
  transfers between devices with their start and end apart: 5 -> 5, of which waited for: 3 -> 2; matrix products, arithmetic and copies ran while one was open for 0% -> 0% of each run, Pallas kernels for 26% -> 28%
where the time goes in v6:
time: 34.6 us; the launch traced here: 34.5 us
  Pallas kernels  21.2 us (61%)
  starting transfers between devices  7.88 us (23%)
  waiting for transfers between devices  4.29 us (12%)
  local copies, waits for them, and re-layouts  0.76 us (2%)
    pallas_call x7, Pallas kernels, call(): pl.pallas_call(kernel, out_shape=tuple((jax.ShapeDtypeStruct(shape, F32 i...  21.2 us
    ppermute x1, starting transfers between devices, body(): got = lax.ppermute(pay, axes, swap(1))  5.75 us
    ppermute x1, waiting for transfers between devices, body(): got = lax.ppermute(pay, axes, swap(1))  2.49 us
    ppermute x1, waiting for transfers between devices, body(): east = lax.ppermute(west_going, 'lon', ring(n_lon, -1))  1.79 us
    ppermute x1, starting transfers between devices, body(): west = lax.ppermute(east_going, 'lon', ring(n_lon, 1))  1.27 us
    ppermute x1, starting transfers between devices, body(): mate = lax.ppermute(high, axes, within)  0.76 us
    unnamed x20, local copies, waits for them, and re-layouts  0.76 us
  transfers between devices with their start and end apart: 5, of which 2 were waited for; matrix products, arithmetic and copies ran while one was open for 0% of the time, Pallas kernels for 28%

profile of v6, /device:TPU:7, one launch (start us, length us, event | category | flops | bytes accessed | tf_op | source)
XLA Modules:
  0.0 34.5 jit_solution(2201294450726673980)
XLA Ops:
  0.0 0.0 copy-start.2
  0.0 0.0 copy-start.3
  0.0 0.0 copy-start.4
  0.0 0.0 copy-start.5
  0.0 0.0 copy-start.6
  0.0 0.0 copy-start.7
  0.0 0.0 copy-start.8
  0.0 2.4 %shard_map.82 = (bf16[80,128]{1,0:T(8,128)(2,1)}, bf16[80,128]{1,0:T(8,128)(2,1)}, bf16[400,384]{1,0:T(8,128)(2,1)}) custom-call(bf16[12,76,270]{2,1,0:T(8,128)(2,1)} %bitcast.11, s32[12,19,270]{2,1,0:T(8,128)} %bitcast.15), custom_call_target="tpu_custom_call" | custom-call | flops 1000000000 | bytes 3000000 | tf_op jit(solution)/shard_map/pallas_call | solution.py:45
  2.4 0.8 %collective-permute-start.2 = (bf16[400,384]{1,0:T(8,128)(2,1)}, bf16[400,384]{1,0:T(8,128)(2,1)S(1)}, u32[]{:S(2)}, u32[]{:S(2)}) collective-permute-start(bf16[400,384]{1,0:T(8,128)(2,1)} %get-tuple-element.27.high_ref), channel_id=1, source_target_pairs={{0,1},{1,0},{2,3},{3,2},{4,5},{5,4},{6,7},{7,6},{8,9},{9,8},{10,11... | collective-permute-start | bytes 921608 | tf_op jit(solution)/shard_map/ppermute | solution.py:433
  3.2 1.3 %collective-permute-start = (bf16[80,128]{1,0:T(8,128)(2,1)}, bf16[80,128]{1,0:T(8,128)(2,1)S(1)}, u32[]{:S(2)}, u32[]{:S(2)}) collective-permute-start(bf16[80,128]{1,0:T(8,128)(2,1)} %get-tuple-element.25), channel_id=1, source_target_pairs={{0,1},{1,2},{2,3},{3,0},{4,5},{5,6},{6,7},{7,4},{8,9},{9,10},{10,1... | collective-permute-start | bytes 61448 | tf_op jit(solution)/shard_map/ppermute | solution.py:417
  4.5 0.0 collective-permute-start.1
  4.5 0.0 copy-done.2
  4.5 0.0 copy-done.3
  4.5 0.0 copy-done.4
  4.5 0.0 copy-done.5
  4.5 0.0 copy-done.6
  4.5 0.0 copy-done.7
  4.5 0.0 copy-done.8
  4.5 0.0 copy-start.9
  4.5 0.7 %copy-done.9 = bf16[80,128]{1,0:T(8,128)(2,1)S(1)} copy-done((bf16[80,128]{1,0:T(8,128)(2,1)S(1)}, bf16[80,128]{1,0:T(8,128)(2,1)}, u32[]{:S(2)}) %copy-start.9) | copy-done | bytes 20504
  5.2 0.0 copy-start
  5.2 0.0 copy-start.1
  5.2 0.8 %shard_map.83 = (bf16[12,80,384]{2,1,0:T(8,128)(2,1)S(1)}, bf16[9,80,256]{2,1,0:T(8,128)(2,1)S(1)}, bf16[4,256,256]{2,1,0:T(8,128)(2,1)S(1)}, bf16[9,256,256]{2,...) custom-call(bf16[80,128]{1,0:T(8,128)(2,1)S(1)} %copy-done.9, ...), custom_call_target="tpu_custom_call" | custom-call | flops 1500000000 | bytes 4500000 | tf_op jit(solution)/shard_map/pallas_call | solution.py:45
  6.1 0.0 collective-permute-done.west_ref
  6.1 1.8 %collective-permute-done.1.east_ref = bf16[80,128]{1,0:T(8,128)(2,1)S(1)} collective-permute-done((bf16[80,128]{1,0:T(8,128)(2,1)}, bf16[80,128]{1,0:T(8,128)(2,1)S(1)}, u32[]{:S(2)}, u32[]{:S(2)}) %collective-permute-start.1) | collective-permute-done | bytes 20512 | tf_op jit(solution)/shard_map/ppermute | solution.py:418
  7.9 0.0 collective-permute-done.2.mate_ref
  7.9 0.0 copy-done
  7.9 0.0 copy-done.1
  7.9 3.3 %shard_map.84 = (bf16[440,256]{1,0:T(8,128)(2,1)S(1)}, bf16[440,256]{1,0:T(8,128)(2,1)S(1)}, bf16[12,288,256]{2,1,0:T(8,128)(2,1)S(1)}, bf16[10,288,256]{2,1,0:T(8,128)(2,1)S(1)}) custom-call(s32[1080]{0:T(1024)S(1)} %copy-done.1, bf16[12,80,384]{2,1,0:T(8,128)(2,1)S(1)} %get-tuple-element.24.rows_ref, bf16[80,128]{1,0:T(8,128)(2,1)S(1)} %collective-permute-done.west_ref, ...), custom_call_target="tpu_custom_call" | custom-call | flops 400000000 | bytes 1200000 | tf_op jit(solution)/shard_map/pallas_call | solution.py:45
  11.1 5.8 %collective-permute-start.4 = (bf16[440,256]{1,0:T(8,128)(2,1)S(1)}, bf16[440,256]{1,0:T(8,128)(2,1)S(1)}, u32[]{:S(2)}, u32[]{:S(2)}) collective-permute-start(bf16[440,256]{1,0:T(8,128)(2,1)S(1)} %get-tuple-element.31), channel_id=1, source_target_pairs={{0,1},{1,0},{2,3},{3,2},{4,8},{5,9},{6,10},{7,11},{8,4},{9,5},{10,... | collective-permute-start | bytes 675848 | tf_op jit(solution)/shard_map/ppermute | solution.py:449
  16.9 0.1 shard_map.85
  17.0 0.1 collective-permute-start.3
  17.1 2.8 %shard_map.86 = (bf16[4,144,768]{2,1,0:T(8,128)(2,1)S(1)}, f32[2,288,256]{2,1,0:T(8,128)S(1)}) custom-call(bf16[10,288,256]{2,1,0:T(8,128)(2,1)S(1)} %get-tuple-element.38.f_ref.refs_10_, bf16[4,256,256]{2,1,0:T(8,128)(2,1)S(1)} %get-tuple-element.33.down_ref.refs_3_, bf16[9,256,256]{2,1,0:T(8,128)(2,1)S(1)} %get-tuple-element.34.mid_ref.refs_4_, ...), custom_call_target="tpu_custom_call" | custom-call | flops 2200000000 | bytes 6600000 | tf_op jit(solution)/shard_map/pallas_call | solution.py:45
  20.0 2.5 %collective-permute-done.4.refs_0_ = bf16[440,256]{1,0:T(8,128)(2,1)S(1)} collective-permute-done((bf16[440,256]{1,0:T(8,128)(2,1)S(1)}, bf16[440,256]{1,0:T(8,128)(2,1)S(1)}, u32[]{:S(2)}, u32[]{:S(2)}) %collective-permute-start.4) | collective-permute-done | bytes 225312 | tf_op jit(solution)/shard_map/ppermute | solution.py:449
  22.5 5.9 %shard_map.87.refs_1_ = bf16[6,76,270]{2,1,0:T(8,128)(2,1)S(1)} custom-call(bf16[440,256]{1,0:T(8,128)(2,1)S(1)} %collective-permute-done.4.refs_0_, bf16[440,256]{1,0:T(8,128)(2,1)S(1)} %get-tuple-element.32.refs_1_, bf16[9,80,256]{2,1,0:T(8,128)(2,1)S(1)} %get-tuple-element.26.in_ref.refs_2_, bf16[4,256,256]{2,1,0:T(8,128)(2,1)S(1)} %get-tuple-element.33.down_ref.refs_3_, ...), custom_call_target="tpu_custom_call" | custom-call | flops 5000000000 | bytes 15000000 | tf_op jit(solution)/shard_map/pallas_call | solution.py:45
  28.4 0.0 collective-permute-done.3.refs_0_
  28.4 5.9 %shard_map.88 = bf16[12,76,270]{2,1,0:T(8,128)(2,1)} custom-call(bf16[440,256]{1,0:T(8,128)(2,1)S(1)} %collective-permute-done.3.refs_0_, bf16[6,76,270]{2,1,0:T(8,128)(2,1)S(1)} %shard_map.87.refs_1_, bf16[9,80,256]{2,1,0:T(8,128)(2,1)S(1)} %get-tuple-element.26.in_ref.refs_2_, bf16[4,256,256]{2,1,0:T(8,128)(2,1)S(1)} %get-tuple-element.33.down_ref.refs_3_, ...), custom_call_target="tpu_custom_call" | custom-call | flops 6000000000 | bytes 18000000 | tf_op jit(solution)/shard_map/pallas_call | solution.py:45
Async XLA Ops:
  0.0 4.5 %copy-start.2 = (bf16[3,3,200,200]{3,2,1,0:T(8,128)(2,1)S(1)}, bf16[3,3,200,200]{3,2,1,0:T(8,128)(2,1)}, u32[]{:S(2)}) copy-start(bf16[3,3,200,200]{3,2,1,0:T(8,128)(2,1)} %param.13) | copy-start | bytes 2160004
  0.0 4.5 %copy-start.3 = (bf16[76,12,270]{2,0,1:T(8,128)(2,1)S(1)}, bf16[76,12,270]{2,0,1:T(8,128)(2,1)}, u32[]{:S(2)}) copy-start(bf16[76,12,270]{2,0,1:T(8,128)(2,1)} %param.8) | copy-start | bytes 1477444
  0.0 4.5 %copy-start.4 = (s32[19,12,270]{2,0,1:T(8,128)S(1)}, s32[19,12,270]{2,0,1:T(8,128)}, u32[]{:S(2)}) copy-start(s32[19,12,270]{2,0,1:T(8,128)} %param.9) | copy-start | bytes 738724
  0.0 4.5 %copy-start.5 = (bf16[2,2,200,200]{3,2,1,0:T(8,128)(2,1)S(1)}, bf16[2,2,200,200]{3,2,1,0:T(8,128)(2,1)}, u32[]{:S(2)}) copy-start(bf16[2,2,200,200]{3,2,1,0:T(8,128)(2,1)} %param.12) | copy-start | bytes 960004
  0.0 4.5 %copy-start.6 = (bf16[2,2,200,200]{3,2,1,0:T(8,128)(2,1)S(1)}, bf16[2,2,200,200]{3,2,1,0:T(8,128)(2,1)}, u32[]{:S(2)}) copy-start(bf16[2,2,200,200]{3,2,1,0:T(8,128)(2,1)} %param.14) | copy-start | bytes 960004
  0.0 4.5 %copy-start.7 = (bf16[3,3,200,76]{2,3,1,0:T(8,128)(2,1)S(1)}, bf16[3,3,200,76]{2,3,1,0:T(8,128)(2,1)}, u32[]{:S(2)}) copy-start(bf16[3,3,200,76]{2,3,1,0:T(8,128)(2,1)} %param.11) | copy-start | bytes 820804
  0.0 4.5 %copy-start.8 = (bf16[3,3,76,200]{3,2,1,0:T(8,128)(2,1)S(1)}, bf16[3,3,76,200]{3,2,1,0:T(8,128)(2,1)}, u32[]{:S(2)}) copy-start(bf16[3,3,76,200]{3,2,1,0:T(8,128)(2,1)} %param.15) | copy-start | bytes 820804
  2.4 5.5 %collective-permute-start.2 = (bf16[400,384]{1,0:T(8,128)(2,1)}, bf16[400,384]{1,0:T(8,128)(2,1)S(1)}, u32[]{:S(2)}, u32[]{:S(2)}) collective-permute-start(bf16[400,384]{1,0:T(8,128)(2,1)} %get-tuple-element.27.high_ref), channel_id=1, source_target_pairs={{0,1},{1,0},{2,3},{3,2},{4,5},{5,4},{6,7},{7,6},{8,9},{9,8},{10,11... | collective-permute-start | bytes 921608 | tf_op jit(solution)/shard_map/ppermute | solution.py:433
  3.2 2.9 %collective-permute-start = (bf16[80,128]{1,0:T(8,128)(2,1)}, bf16[80,128]{1,0:T(8,128)(2,1)S(1)}, u32[]{:S(2)}, u32[]{:S(2)}) collective-permute-start(bf16[80,128]{1,0:T(8,128)(2,1)} %get-tuple-element.25), channel_id=1, source_target_pairs={{0,1},{1,2},{2,3},{3,0},{4,5},{5,6},{6,7},{7,4},{8,9},{9,10},{10,1... | collective-permute-start | bytes 61448 | tf_op jit(solution)/shard_map/ppermute | solution.py:417
  4.5 3.4 %collective-permute-start.1 = (bf16[80,128]{1,0:T(8,128)(2,1)}, bf16[80,128]{1,0:T(8,128)(2,1)S(1)}, u32[]{:S(2)}, u32[]{:S(2)}) collective-permute-start(bf16[80,128]{1,0:T(8,128)(2,1)} %get-tuple-element.23.after_ref), channel_id=1, source_target_pairs={{0,3},{1,0},{2,1},{3,2},{4,7},{5,4},{6,5},{7,6},{8,11},{9,8},{10,9... | collective-permute-start | bytes 61448 | tf_op jit(solution)/shard_map/ppermute | solution.py:418
  4.5 0.7 %copy-start.9 = (bf16[80,128]{1,0:T(8,128)(2,1)S(1)}, bf16[80,128]{1,0:T(8,128)(2,1)}, u32[]{:S(2)}) copy-start(bf16[80,128]{1,0:T(8,128)(2,1)} %get-tuple-element.23.after_ref) | copy-start | bytes 61444
  5.2 2.6 %copy-start = (bf16[400,384]{1,0:T(8,128)(2,1)S(1)}, bf16[400,384]{1,0:T(8,128)(2,1)}, u32[]{:S(2)}) copy-start(bf16[400,384]{1,0:T(8,128)(2,1)} %get-tuple-element.27.high_ref) | copy-start | bytes 921604
  5.2 2.6 %copy-start.1 = (s32[1080]{0:T(1024)S(1)}, s32[1080]{0:T(1024)}, u32[]{:S(2)}) copy-start(s32[1080]{0:T(1024)} %seam_ref.1) | copy-start | bytes 12964
  11.1 11.3 %collective-permute-start.4 = (bf16[440,256]{1,0:T(8,128)(2,1)S(1)}, bf16[440,256]{1,0:T(8,128)(2,1)S(1)}, u32[]{:S(2)}, u32[]{:S(2)}) collective-permute-start(bf16[440,256]{1,0:T(8,128)(2,1)S(1)} %get-tuple-element.31), channel_id=1, source_target_pairs={{0,1},{1,0},{2,3},{3,2},{4,8},{5,9},{6,10},{7,11},{8,4},{9,5},{10,... | collective-permute-start | bytes 675848 | tf_op jit(solution)/shard_map/ppermute | solution.py:449
  17.0 11.3 %collective-permute-start.3 = (bf16[440,256]{1,0:T(8,128)(2,1)S(1)}, bf16[440,256]{1,0:T(8,128)(2,1)S(1)}, u32[]{:S(2)}, u32[]{:S(2)}) collective-permute-start(bf16[440,256]{1,0:T(8,128)(2,1)S(1)} %get-tuple-element.30), channel_id=1, source_target_pairs={{0,4},{1,5},{2,6},{3,7},{4,0},{5,1},{6,2},{7,3},{8,12},{9,13},{10,... | collective-permute-start | bytes 675848 | tf_op jit(solution)/shard_map/ppermute | solution.py:454
